TPU v7x, 256 devices: a whole 4x4x8 slice. The times are simulated.
256 devices in a mesh: wide: 32 (over y_lo, z, core), blk: 8 (over y_hi, x).
Axes of the slice: x: 4, y: 4 (y_hi: 2, y_lo: 2; y = y_hi * 2 + y_lo), z: 8, core: 2. Of those that a mesh axis runs over, the one named last changes fastest.
Arguments:
- records: bfloat16 [8, 2304, 4, 8192], P('blk', 'wide'), may hold values from -6 to 6
- lengths: int32 [8, 2304], P('blk', 'wide'), may hold values from 8192 to 32768
- owners: int32 [8, 2304], P('blk', 'wide'), may hold values from -1 to 767, as said below
- own_pick: int32 [8, 32, 8, 2, 4], P('blk', 'wide'), may hold values from 0 to 23
- visit_pick: int32 [8, 32, 8, 2, 4], P('blk', 'wide'), may hold values from 0 to 23
- pair_mask: int32 [8, 32, 8, 2, 4, 4], P('blk', 'wide'), may hold values 0 or 1
Outputs:
- correlations: float32 [8, 32, 8, 2, 4, 4, 1024], P('blk', 'wide')
Inputs may be any that keep to these rules, and one draw needn't show every extreme that they name: `owners`: in each group every station number 0 to 767 is named by exactly one slot. A device's valid slots come first and its other slots hold -1. The busiest device of each group fills all 72 slots and two devices hold none. At most 3 slots of one device name stations of one owner (stations w * 24 to w * 24 + 23 belong to owner w), and this most is reached in every group.
All inputs are finite; a program needn't handle non-finite values. No bound on the sum of `pair_mask` on one device may be relied on, other than what follows from the above.
Results may differ from a plain program's by a relative error of at most 0.0049.
Values may be sent and summed in bfloat16 or wider, within the bound.
No kernel may reach another device: no remote copies, remote signals or barrier semaphores. Data moves between devices by JAX's collectives and lax.ppermute only.
A program may use at most 192 MiB of HBM per device.

v0:
```python
import math

import jax
import jax.numpy as jnp
import numpy as np
from jax import lax
from jax.sharding import PartitionSpec as P

ST_DEV = 24
SEG = 4
P_SIZE = 64
Q = 128
NT = 8192
NF = 4096
LAGS = 1024


def from_behind(shard, axis, by):
    size = lax.axis_size(axis)
    return lax.ppermute(shard, axis, [(i, (i + by) % size) for i in range(size)])


def lag_table():
    bins = np.arange(NF, dtype=np.int64)
    delay = np.arange(LAGS, dtype=np.int64) - LAGS // 2
    phase = bins[:, None] * (delay % NT)[None, :] % NT
    angle = phase.astype(np.float32) * np.float32(2.0 * math.pi / NT)
    weight = np.where(bins == 0, 0.5, 1.0).astype(np.float32) / np.float32(math.sqrt(NF * SEG))
    upper = weight[:, None] * np.cos(angle)
    lower = -weight[:, None] * np.sin(angle)
    joined = np.concatenate([upper, lower], 0).astype(np.float32)
    return jnp.asarray(joined, dtype=jnp.float32).astype(jnp.bfloat16)


def cos_sin(phase, period):
    angle = phase.astype(jnp.float32) * (2.0 * math.pi / period)
    return (jnp.cos(angle), jnp.sin(angle))


def whiten(signal):
    count, segments, length = signal.shape
    values = signal.astype(jnp.float32).reshape(count * segments, P_SIZE, Q)
    highest = lax.Precision.HIGHEST
    first = jnp.arange(P_SIZE, dtype=jnp.int32)
    second = jnp.arange(Q, dtype=jnp.int32)
    halfway = jnp.arange(Q // 2, dtype=jnp.int32)
    small_cos, small_sin = cos_sin(first[:, None] * first[None, :] % P_SIZE, P_SIZE)
    part_re = jnp.einsum("kn,rnm->rkm", small_cos, values, precision=highest)
    part_im = -jnp.einsum("kn,rnm->rkm", small_sin, values, precision=highest)
    twist_cos, twist_sin = cos_sin(first[:, None] * second[None, :] % (P_SIZE * Q), P_SIZE * Q)
    mixed_re = part_re * twist_cos + part_im * twist_sin
    mixed_im = part_im * twist_cos - part_re * twist_sin
    wave_cos, wave_sin = cos_sin(second[:, None] * halfway[None, :] % Q, Q)
    spec_re = jnp.einsum("rkn,nm->rmk", mixed_re, wave_cos, precision=highest) + jnp.einsum(
        "rkn,nm->rmk", mixed_im, wave_sin, precision=highest
    )
    spec_im = jnp.einsum("rkn,nm->rmk", mixed_im, wave_cos, precision=highest) - jnp.einsum(
        "rkn,nm->rmk", mixed_re, wave_sin, precision=highest
    )
    power = jnp.mean(spec_re * spec_re + spec_im * spec_im, axis=-1, keepdims=True)
    norm_scale = jnp.sqrt(power + 1e-06)
    white = jnp.stack([spec_re / norm_scale, spec_im / norm_scale], 1)
    return white.reshape(count, segments, 2, Q // 2 * P_SIZE).astype(jnp.bfloat16)


def place_rows(rows, slots, count):
    holder = jnp.zeros((count + 1,) + rows.shape[1:], rows.dtype)
    return holder.at[slots].set(rows)[:count]


def on_device(records, lengths, owners, own_pick, visit_pick, pair_mask):
    wide_count = lax.axis_size("wide")
    cycle_count = lax.axis_size("blk")
    local_records = records[0]
    in_slots, segments, length = local_records.shape
    capacity = (in_slots + wide_count - 1) // wide_count
    position = jnp.arange(segments * length, dtype=jnp.int32).reshape(segments, length)
    kept = jnp.where(
        position[None] < lengths[0][:, None, None],
        local_records,
        jnp.zeros((), local_records.dtype),
    )
    target = owners[0]
    valid = target >= 0
    owner_dev = jnp.where(valid, target // ST_DEV, -1)
    onehot = (owner_dev[:, None] == jnp.arange(wide_count, dtype=jnp.int32)[None, :]).astype(
        jnp.int32
    )
    before = jnp.cumsum(onehot, axis=0) - onehot
    rank = jnp.sum(before * onehot, axis=1)
    slot_index = jnp.where(valid, owner_dev * capacity + rank, wide_count * capacity)
    source = (
        jnp.full((wide_count * capacity + 1,), -1, jnp.int32)
        .at[slot_index]
        .set(jnp.arange(in_slots, dtype=jnp.int32))[:-1]
    )
    present = source >= 0
    picked = jnp.maximum(source, 0)
    send_slot = jnp.where(present, target[picked] % ST_DEV, ST_DEV).reshape(wide_count, capacity)
    payload = jnp.where(present[:, None, None], kept[picked], jnp.zeros((), kept.dtype))
    payload = payload.reshape(wide_count, capacity, segments, length)
    got, got_slot = (
        lax.all_to_all(payload, "wide", split_axis=0, concat_axis=0, tiled=True),
        lax.all_to_all(send_slot, "wide", split_axis=0, concat_axis=0, tiled=True),
    )
    owned = place_rows(
        got.reshape(wide_count * capacity, segments, length), got_slot.reshape(-1), ST_DEV
    )
    spectra = whiten(owned)
    table = lag_table()
    own_rows = own_pick[0, 0]
    visit_rows = visit_pick[0, 0]
    masks = pair_mask[0, 0].astype(jnp.float32)

    def cross_rows(far_rows, stop):
        near = spectra[own_rows[stop]].astype(jnp.float32)
        far = far_rows.astype(jnp.float32)
        near_re = near[:, :, None, :, 0]
        near_im = near[:, :, None, :, 1]
        far_re = far[:, None, :, :, 0]
        far_im = far[:, None, :, :, 1]
        cross_re = jnp.sum(near_re * far_re + near_im * far_im, axis=3)
        cross_im = jnp.sum(near_im * far_re - near_re * far_im, axis=3)
        cross = jnp.stack([cross_re, cross_im], 3).astype(jnp.bfloat16)
        blocks, sides = (cross.shape[0], cross.shape[1])
        return cross.reshape(blocks * sides * sides, -1)

    results = [None] * cycle_count
    results[0] = cross_rows(spectra[visit_rows[0]], 0)
    current = spectra
    for stop in range(1, cycle_count):
        current = from_behind(current, "blk", 1)
        results[stop] = cross_rows(current[visit_rows[stop]], stop)
    stacked = jnp.concatenate(results, 0)
    lagged = jnp.dot(stacked, table, preferred_element_type=jnp.float32)
    lagged = lagged.reshape(masks.shape + (table.shape[1],))
    return (lagged * masks[..., None])[None, None]


def solution(mesh):
    return jax.shard_map(
        on_device,
        mesh=mesh,
        in_specs=(
            P("blk", "wide", None, None),
            P("blk", "wide"),
            P("blk", "wide"),
            P("blk", "wide", None, None, None),
            P("blk", "wide", None, None, None),
            P("blk", "wide", None, None, None, None),
        ),
        out_specs=P("blk", "wide", None, None, None, None, None),
        check_vma=False,
    )
```

profile of v0, /device:TPU:72, one launch (start us, length us, event | category | flops | bytes accessed | tf_op | source)
XLA Modules:
  0.0 566.3 jit_solution(676061323815181522)
XLA Ops:
  6.5 9.2 %all-to-all-start = ((s32[32,1,3]{2,1,0:T(1,128)}), s32[32,1,3]{2,1,0:T(1,128)S(1)}, u32[]{:S(2)}, u32[]{:S(2)}) async-start(s32[32,1,3]{2,1,0:T(1,128)} %bitcast.7), calls=%async_computation | async-start | bytes 32768 | tf_op jit(solution)/shard_map/all_to_all | solution.py:104
  15.9 8.3 %compare_select_fusion = bf16[72,4,8192]{2,1,0:T(4,128)(2,1)} fusion(bf16[1,72,4,8192]{3,2,1,0:T(4,128)(2,1)} %param.7, s32[4,8192]{1,0:T(4,128)S(1)} %multiply_add_fusion, s32[72]{0:T(128)} %bitcast.377), kind=kLoop, calls=%fused_computation.20 | loop fusion | flops 4718592 | bytes 9568544 | tf_op jit(solution)/shard_map/jit(_where)/select_n | solution.py:78
  24.2 10.6 %gather_fusion.1 = bf16[96,4,8192]{2,1,0:T(4,128)(2,1)} fusion(bf16[72,4,8192]{2,1,0:T(4,128)(2,1)} %compare_select_fusion, s32[1024]{0:T(1024)S(1)} %get-tuple-element.84), kind=kCustom, calls=%fused_computation.1 | custom fusion | bytes 12583296 | tf_op jit(solution)/shard_map/gather | solution.py:100
  34.8 8.1 %broadcast_select_fusion = bf16[32,3,4,8192]{3,2,1,0:T(4,128)(2,1)} fusion(bf16[32,3,4,8192]{3,2,1,0:T(4,128)(2,1)} %bitcast.328, pred[32,3]{1,0:T(8,128)(4,1)S(1)} %ge.41), kind=kLoop, calls=%fused_computation.21 | loop fusion | flops 3145728 | bytes 12583008 | tf_op jit(solution)/shard_map/jit(_where)/select_n | solution.py:100
  42.9 19.1 %all-to-all-start.1 = ((bf16[32,3,4,8192]{3,2,1,0:T(4,128)(2,1)}), bf16[32,3,4,8192]{3,2,1,0:T(4,128)(2,1)}, u32[]{:S(2)}, u32[]{:S(2)}) async-start(bf16[32,3,4,8192]{3,2,1,0:T(4,128)(2,1)} %broadcast_select_fusion), calls=%async_computation.1 | async-start | bytes 12582912 | tf_op jit(solution)/shard_map/all_to_all | solution.py:103
  65.5 132.8 %all-to-all-done.1 = bf16[32,3,4,8192]{3,2,1,0:T(4,128)(2,1)} async-done(((bf16[32,3,4,8192]{3,2,1,0:T(4,128)(2,1)}), bf16[32,3,4,8192]{3,2,1,0:T(4,128)(2,1)}, u32[]{:S(2)}, u32[]{:S(2)}) %all-to-all-start.1) | async-done | bytes 6291488 | tf_op jit(solution)/shard_map/all_to_all | solution.py:103
  199.1 16.8 %scatter_fusion = bf16[25,4,8192]{2,1,0:T(4,128)(2,1)S(1)} fusion(bf16[25,4,8192]{2,1,0:T(4,128)(2,1)S(1)} %broadcast_in_dim.29, s32[96]{0:T(128)S(1)} %fusion.63, bf16[96,4,8192]{2,1,0:T(4,128)(2,1)} %bitcast.12), kind=kCustom, calls=%fused_computation.19 | custom fusion | bytes 18874752 | tf_op jit(solution)/shard_map/scatter | solution.py:68
  222.2 8.0 %fusion.4 = f32[64,96,64]{1,0,2:T(8,128)S(1)} fusion(f32[96,64,128]{2,1,0:T(8,128)S(1)} %get-tuple-element.38), kind=kOutput, calls=%fused_computation.30 | convolution fusion | flops 604094464 | bytes 4718592 | tf_op jit(solution)/shard_map/rkn,nm->rmk/dot_general | solution.py:54
  230.3 8.2 %fusion.2 = f32[64,96,64]{1,0,2:T(8,128)S(1)} fusion(f32[96,64,128]{2,1,0:T(8,128)S(1)} %get-tuple-element.38), kind=kOutput, calls=%fused_computation.28 | convolution fusion | flops 604094464 | bytes 4718592 | tf_op jit(solution)/shard_map/rkn,nm->rmk/dot_general | solution.py:57
  238.5 8.1 %fusion.14 = f32[64,96,64]{1,0,2:T(8,128)S(1)} fusion(f32[64,96,64]{1,0,2:T(8,128)S(1)} %fusion.4, f32[96,64,128]{2,1,0:T(8,128)S(1)} %get-tuple-element.37), kind=kOutput, calls=%fused_computation.60 | convolution fusion | flops 604487680 | bytes 6291456 | tf_op jit(solution)/shard_map/rkn,nm->rmk/dot_general | solution.py:54
  246.6 8.5 %fusion.11 = (f32[96,64]{0,1:T(8,128)S(1)}, f32[64,96,64]{1,0,2:T(8,128)S(1)}) fusion(f32[64,96,64]{1,0,2:T(8,128)S(1)} %fusion.14, f32[64,96,64]{1,0,2:T(8,128)S(1)} %fusion.2, f32[96,64,128]{2,1,0:T(8,128)S(1)} %get-tuple-element.37), kind=kOutput, calls=%fused_computation.39 | convolution fusion | flops 606054400 | bytes 7888896 | tf_op jit(solution)/shard_map/rkn,nm->rmk/dot_general | solution.py:57
  256.7 2.8 copy.63
  261.0 4.0 copy.64
  288.7 3.3 add_reduce_fusion.7
  294.9 14.4 %collective-permute-done = bf16[24,4,2,4096]{3,1,0,2:T(4,128)(2,1)} collective-permute-done((bf16[24,4,2,4096]{3,1,0,2:T(4,128)(2,1)S(1)}, bf16[24,4,2,4096]{3,1,0,2:T(4,128)(2,1)}, u32[]{:S(2)}, u32[]{:S(2)}) %collective-permute-start) | collective-permute-done | bytes 1572896 | tf_op jit(solution)/shard_map/ppermute | solution.py:20
  309.3 2.4 gather_fusion.5
  312.8 3.3 add_reduce_fusion.6
  318.1 34.3 %collective-permute-done.1 = bf16[24,4,2,4096]{3,1,0,2:T(4,128)(2,1)} collective-permute-done((bf16[24,4,2,4096]{3,1,0,2:T(4,128)(2,1)}, bf16[24,4,2,4096]{3,1,0,2:T(4,128)(2,1)}, u32[]{:S(2)}, u32[]{:S(2)}) %collective-permute-start.1) | collective-permute-done | bytes 1572896 | tf_op jit(solution)/shard_map/ppermute | solution.py:20
  352.5 2.4 gather_fusion.7
  356.1 3.3 add_reduce_fusion.5
  361.4 32.8 %collective-permute-done.2 = bf16[24,4,2,4096]{3,1,0,2:T(4,128)(2,1)S(1)} collective-permute-done((bf16[24,4,2,4096]{3,1,0,2:T(4,128)(2,1)}, bf16[24,4,2,4096]{3,1,0,2:T(4,128)(2,1)S(1)}, u32[]{:S(2)}, u32[]{:S(2)}) %collective-permute-start.2) | collective-permute-done | bytes 1572896 | tf_op jit(solution)/shard_map/ppermute | solution.py:20
  396.4 3.3 add_reduce_fusion.4
  401.8 31.9 %collective-permute-done.3 = bf16[24,4,2,4096]{3,1,0,2:T(4,128)(2,1)} collective-permute-done((bf16[24,4,2,4096]{3,1,0,2:T(4,128)(2,1)S(1)}, bf16[24,4,2,4096]{3,1,0,2:T(4,128)(2,1)}, u32[]{:S(2)}, u32[]{:S(2)}) %collective-permute-start.3) | collective-permute-done | bytes 1572896 | tf_op jit(solution)/shard_map/ppermute | solution.py:20
  433.7 2.4 gather_fusion.11
  437.3 3.3 add_reduce_fusion.3
  442.6 31.0 %collective-permute-done.4 = bf16[24,4,2,4096]{3,1,0,2:T(4,128)(2,1)S(1)} collective-permute-done((bf16[24,4,2,4096]{3,1,0,2:T(4,128)(2,1)}, bf16[24,4,2,4096]{3,1,0,2:T(4,128)(2,1)S(1)}, u32[]{:S(2)}, u32[]{:S(2)}) %collective-permute-start.4) | collective-permute-done | bytes 1572896 | tf_op jit(solution)/shard_map/ppermute | solution.py:20
  475.8 3.3 add_reduce_fusion.2
  481.1 29.9 %collective-permute-done.5 = bf16[24,4,2,4096]{3,1,0,2:T(4,128)(2,1)} collective-permute-done((bf16[24,4,2,4096]{3,1,0,2:T(4,128)(2,1)S(1)}, bf16[24,4,2,4096]{3,1,0,2:T(4,128)(2,1)}, u32[]{:S(2)}, u32[]{:S(2)}) %collective-permute-start.5) | collective-permute-done | bytes 1572896 | tf_op jit(solution)/shard_map/ppermute | solution.py:20
  514.6 3.3 add_reduce_fusion.1
  520.0 29.3 %collective-permute-done.6 = bf16[24,4,2,4096]{3,1,0,2:T(4,128)(2,1)S(1)} collective-permute-done((bf16[24,4,2,4096]{3,1,0,2:T(4,128)(2,1)}, bf16[24,4,2,4096]{3,1,0,2:T(4,128)(2,1)S(1)}, u32[]{:S(2)}, u32[]{:S(2)}) %collective-permute-start.6) | collective-permute-done | bytes 1572896 | tf_op jit(solution)/shard_map/ppermute | solution.py:20
  551.5 3.3 add_reduce_fusion
  556.1 8.4 %fusion.90 = f32[256,1024]{1,0:T(8,128)S(1)} fusion(bf16[256,8192]{1,0:T(8,128)(2,1)S(1)} %constant_dynamic-update-slice_fusion.2, bf16[8192,1024]{1,0:T(8,128)(2,1)} %constant.109), kind=kOutput, calls=%fused_computation.267 | convolution fusion | flops 4294967296 | bytes 22020096 | tf_op jit(solution)/shard_map/dot_general | solution.py:135
  (200 shorter events, 75.0 us)
Async XLA Ops:
  6.5 36.4 %all-to-all-start = ((s32[32,1,3]{2,1,0:T(1,128)}), s32[32,1,3]{2,1,0:T(1,128)S(1)}, u32[]{:S(2)}, u32[]{:S(2)}) async-start(s32[32,1,3]{2,1,0:T(1,128)} %bitcast.7), calls=%async_computation | async-start | bytes 32768 | tf_op jit(solution)/shard_map/all_to_all | solution.py:104
  42.9 19.1 %copy-start.15 = (s32[1,1,8,2,4]{2,4,3,1,0:T(4,128)S(1)}, s32[1,1,8,2,4]{2,4,3,1,0:T(4,128)}, u32[]{:S(2)}) copy-start(s32[1,1,8,2,4]{2,4,3,1,0:T(4,128)} %param.11) | copy-start | bytes 772
  42.9 20.9 %copy-start.17 = (s32[1,1,8,2,4,4]{2,5,4,3,1,0:T(4,128)S(1)}, s32[1,1,8,2,4,4]{2,5,4,3,1,0:T(4,128)}, u32[]{:S(2)}) copy-start(s32[1,1,8,2,4,4]{2,5,4,3,1,0:T(4,128)} %param.12) | copy-start | bytes 3076
  42.9 155.4 %all-to-all-start.1 = ((bf16[32,3,4,8192]{3,2,1,0:T(4,128)(2,1)}), bf16[32,3,4,8192]{3,2,1,0:T(4,128)(2,1)}, u32[]{:S(2)}, u32[]{:S(2)}) async-start(bf16[32,3,4,8192]{3,2,1,0:T(4,128)(2,1)} %broadcast_select_fusion), calls=%async_computation.1 | async-start | bytes 12582912 | tf_op jit(solution)/shard_map/all_to_all | solution.py:103
  268.5 40.8 %collective-permute-start = (bf16[24,4,2,4096]{3,1,0,2:T(4,128)(2,1)S(1)}, bf16[24,4,2,4096]{3,1,0,2:T(4,128)(2,1)}, u32[]{:S(2)}, u32[]{:S(2)}) collective-permute-start(bf16[24,4,2,4096]{3,1,0,2:T(4,128)(2,1)S(1)} %constant_dynamic-update-slice_fusion), channel_id=1, source_target_pairs={{0,1},{1,2},{2,3},{3,4},{4,5},{5,6},{6,7},{7,0},{8,9},{9,10},{10,1... | collective-permute-start | bytes 4718600 | tf_op jit(solution)/shard_map/ppermute | solution.py:20
  287.5 1.0 copy-start.13
  287.5 1.2 copy-start.14
  311.7 1.0 copy-start.12
  312.0 40.5 %collective-permute-start.1 = (bf16[24,4,2,4096]{3,1,0,2:T(4,128)(2,1)}, bf16[24,4,2,4096]{3,1,0,2:T(4,128)(2,1)}, u32[]{:S(2)}, u32[]{:S(2)}) collective-permute-start(bf16[24,4,2,4096]{3,1,0,2:T(4,128)(2,1)} %collective-permute-done), channel_id=1, source_target_pairs={{0,1},{1,2},{2,3},{3,4},{4,5},{5,6},{6,7},{7,0},{8,9},{9,10},{10,1... | collective-permute-start | bytes 4718600 | tf_op jit(solution)/shard_map/ppermute | solution.py:20
  354.9 1.0 copy-start.10
  354.9 1.2 copy-start.11
  355.1 39.1 %collective-permute-start.2 = (bf16[24,4,2,4096]{3,1,0,2:T(4,128)(2,1)}, bf16[24,4,2,4096]{3,1,0,2:T(4,128)(2,1)S(1)}, u32[]{:S(2)}, u32[]{:S(2)}) collective-permute-start(bf16[24,4,2,4096]{3,1,0,2:T(4,128)(2,1)} %collective-permute-done.1), channel_id=1, source_target_pairs={{0,1},{1,2},{2,3},{3,4},{4,5},{5,6},{6,7},{7,0},{8,9},{9,10},{10,1... | collective-permute-start | bytes 4718600 | tf_op jit(solution)/shard_map/ppermute | solution.py:20
  395.2 1.0 copy-start.8
  395.2 1.2 copy-start.9
  395.4 38.3 %collective-permute-start.3 = (bf16[24,4,2,4096]{3,1,0,2:T(4,128)(2,1)S(1)}, bf16[24,4,2,4096]{3,1,0,2:T(4,128)(2,1)}, u32[]{:S(2)}, u32[]{:S(2)}) collective-permute-start(bf16[24,4,2,4096]{3,1,0,2:T(4,128)(2,1)S(1)} %collective-permute-done.2), channel_id=1, source_target_pairs={{0,1},{1,2},{2,3},{3,4},{4,5},{5,6},{6,7},{7,0},{8,9},{9,10},{10,1... | collective-permute-start | bytes 4718600 | tf_op jit(solution)/shard_map/ppermute | solution.py:20
  436.1 1.0 copy-start.6
  436.1 1.2 copy-start.7
  436.3 37.3 %collective-permute-start.4 = (bf16[24,4,2,4096]{3,1,0,2:T(4,128)(2,1)}, bf16[24,4,2,4096]{3,1,0,2:T(4,128)(2,1)S(1)}, u32[]{:S(2)}, u32[]{:S(2)}) collective-permute-start(bf16[24,4,2,4096]{3,1,0,2:T(4,128)(2,1)} %collective-permute-done.3), channel_id=1, source_target_pairs={{0,1},{1,2},{2,3},{3,4},{4,5},{5,6},{6,7},{7,0},{8,9},{9,10},{10,1... | collective-permute-start | bytes 4718600 | tf_op jit(solution)/shard_map/ppermute | solution.py:20
  474.6 1.0 copy-start.4
  474.6 1.2 copy-start.5
  474.8 36.3 %collective-permute-start.5 = (bf16[24,4,2,4096]{3,1,0,2:T(4,128)(2,1)S(1)}, bf16[24,4,2,4096]{3,1,0,2:T(4,128)(2,1)}, u32[]{:S(2)}, u32[]{:S(2)}) collective-permute-start(bf16[24,4,2,4096]{3,1,0,2:T(4,128)(2,1)S(1)} %collective-permute-done.4), channel_id=1, source_target_pairs={{0,1},{1,2},{2,3},{3,4},{4,5},{5,6},{6,7},{7,0},{8,9},{9,10},{10,1... | collective-permute-start | bytes 4718600 | tf_op jit(solution)/shard_map/ppermute | solution.py:20
  513.4 1.0 copy-start.2
  513.5 1.2 copy-start.3
  513.7 35.7 %collective-permute-start.6 = (bf16[24,4,2,4096]{3,1,0,2:T(4,128)(2,1)}, bf16[24,4,2,4096]{3,1,0,2:T(4,128)(2,1)S(1)}, u32[]{:S(2)}, u32[]{:S(2)}) collective-permute-start(bf16[24,4,2,4096]{3,1,0,2:T(4,128)(2,1)} %collective-permute-done.5), channel_id=1, source_target_pairs={{0,1},{1,2},{2,3},{3,4},{4,5},{5,6},{6,7},{7,0},{8,9},{9,10},{10,1... | collective-permute-start | bytes 4718600 | tf_op jit(solution)/shard_map/ppermute | solution.py:20
  550.3 1.0 copy-start
  550.3 1.2 copy-start.1
  551.5 4.5 copy-start.16
where the time goes:
time: 576 us; the launch traced here: 566 us
  waiting for transfers between devices  336 us (58%)
  local copies, waits for them, and re-layouts  98.9 us (17%)
  other arithmetic  53.2 us (9%)
  matrix products  45.1 us (8%)
  starting transfers between devices  31.2 us (5%)
    ppermute x7, waiting for transfers between devices, from_behind(): lax.ppermute(shard, axis, [(i, (i + by) % size) for i in range(size)])  204 us
    all_to_all x1, waiting for transfers between devices, on_device(): lax.all_to_all(payload, 'wide', split_axis=0, concat_axis=0, tiled=True)  133 us
    reduce_sum x8, other arithmetic, cross_rows(): cross_re = jnp.sum(near_re * far_re + near_im * far_im, axis=3)  26.1 us
    all_to_all x1, starting transfers between devices, on_device(): lax.all_to_all(payload, 'wide', split_axis=0, concat_axis=0, tiled=True)  19.1 us
    scatter x1, local copies, waits for them, and re-layouts, place_rows(): return holder.at[slots].set(rows)[:count]  16.8 us
    unnamed x52, local copies, waits for them, and re-layouts  15.1 us
    gather x7, local copies, waits for them, and re-layouts, on_device(): results[stop] = cross_rows(current[visit_rows[stop]], stop)  12.6 us
  transfers between devices with their start and end apart: 9, of which 8 were waited for; matrix products, arithmetic and copies ran while one was open for 15% of the time, Pallas kernels for 0%

commit v1 on v0

v1 whole, which is shorter than its diff:
```python
import functools
import math

import jax
import jax.numpy as jnp
import numpy as np
from jax import lax
from jax.experimental import pallas as pl
from jax.experimental.pallas import tpu as pltpu
from jax.sharding import PartitionSpec as P

ST_DEV = 24
SEG = 4
NT = 8192
NF = 4096
LAGS = 1024
ROWS = 64
LANES = 128
BASE = 4
EXTRA = 2
LEN_BITS = 16
SMEM = pl.BlockSpec(memory_space=pltpu.SMEM)
VMEM = pl.BlockSpec(memory_space=pltpu.VMEM)
ANY = pl.BlockSpec(memory_space=pl.ANY)


def split_bf16(values):
    high = values.astype(jnp.bfloat16)
    low = (values - high.astype(np.float64)).astype(jnp.bfloat16)
    return high, low


def transform_tables():
    first = np.arange(ROWS)
    second = np.arange(LANES)
    half = np.arange(LANES // 2)
    angle = 2.0 * math.pi / ROWS * (first[:, None] * first[None, :] % ROWS)
    wave = np.concatenate([np.cos(angle), -np.sin(angle)], 0)
    first_table = np.concatenate(split_bf16(wave), 1)
    twist = 2.0 * math.pi / NT * (first[:, None] * second[None, :] % NT)
    twist_table = np.stack([np.cos(twist), np.sin(twist)]).astype(np.float32)
    angle = 2.0 * math.pi / LANES * (second[:, None] * half[None, :] % LANES)
    cos, sin = np.cos(angle), np.sin(angle)
    wave = np.concatenate([np.concatenate([cos, -sin], 1), np.concatenate([sin, cos], 1)], 0)
    second_table = np.concatenate(split_bf16(wave), 1)
    return first_table, twist_table, second_table


def lag_table():
    bins = np.arange(NF, dtype=np.int64)
    delay = np.arange(LAGS, dtype=np.int64) - LAGS // 2
    phase = bins[:, None] * (delay % NT)[None, :] % NT
    angle = phase.astype(np.float32) * np.float32(2.0 * math.pi / NT)
    weight = np.where(bins == 0, 0.5, 1.0).astype(np.float32) / np.float32(math.sqrt(NF * SEG))
    upper = (weight[:, None] * np.cos(angle)).reshape(ROWS, ROWS, LAGS).transpose(1, 0, 2)
    lower = (-weight[:, None] * np.sin(angle)).reshape(ROWS, ROWS, LAGS).transpose(1, 0, 2)
    joined = np.concatenate([upper, lower], 1).astype(np.float32)
    return joined.reshape(ROWS * LANES, LAGS).astype(jnp.bfloat16)


def pack_kernel(part, low, count, packed, core_ref, own, mate, out, fill, sem):
    core = core_ref[0]
    slots = packed.shape[0] // 2

    @pl.loop(0, out.shape[0])
    def _(dev):
        fill[dev] = 0

    def place(at, started, half):
        value = packed[at + half * slots]
        valid = value >= 0
        dev = jnp.where(valid, value >> LEN_BITS, 0) // ST_DEV
        rank = fill[dev]
        fill[dev] = rank + valid.astype(jnp.int32)
        take = valid & (rank >= low) & (rank < low + count)

        @pl.when(take & (core == half))
        def _():
            pltpu.make_async_copy(own.at[at, 2 * core + part], out.at[dev, rank - low], sem).start()

        @pl.when(take & (core != half))
        def _():
            pltpu.make_async_copy(mate.at[at], out.at[dev, rank - low], sem).start()

        return started + take.astype(jnp.int32)

    started = lax.fori_loop(0, slots, functools.partial(place, half=0), 0)
    started = lax.fori_loop(0, slots, functools.partial(place, half=1), started)

    @pl.loop(0, started)
    def _(_):
        pltpu.make_async_copy(mate.at[0], out.at[0, 0], sem).wait()


def pack(part, low, count, wide_count, packed, core, own, mate):
    return pl.pallas_call(
        functools.partial(pack_kernel, part, low, count),
        out_shape=jax.ShapeDtypeStruct((wide_count, count, ROWS, LANES), jnp.bfloat16),
        in_specs=[SMEM, SMEM, ANY, ANY],
        out_specs=ANY,
        scratch_shapes=[pltpu.SMEM((wide_count,), jnp.int32), pltpu.SemaphoreType.DMA],
        cost_estimate=pl.CostEstimate(flops=0, bytes_accessed=wide_count * count * NT * 4, transcendentals=0),
        name="pack",
    )(packed, core, own, mate)


def whiten_kernel(
    part, source, length, picks, got, more, first, twist, second, white, payload, held, spectra, sem
):
    stations = held.shape[0]

    @pl.loop(0, stations)
    def _(station):
        code = source[station]
        over = code - 16 * BASE
        for core in range(2):

            @pl.when(over < 0)
            def _():
                pltpu.make_async_copy(
                    got.at[2 * (code // BASE) + core, code % BASE], held.at[station, core], sem
                ).start()

            @pl.when(over >= 0)
            def _():
                pltpu.make_async_copy(
                    more.at[2 * (over // EXTRA) + core, over % EXTRA], held.at[station, core], sem
                ).start()

    @pl.loop(0, 2 * stations)
    def _(_):
        pltpu.make_async_copy(got.at[0, 0], held.at[0, 0], sem).wait()

    row = lax.broadcasted_iota(jnp.int32, (ROWS, LANES), 0)
    place = row * LANES + lax.broadcasted_iota(jnp.int32, (ROWS, LANES), 1)

    def one_station(station):
        sides = []
        for core in range(2):
            bound = length[station] - (2 * core + part) * NT
            values = held[station, core].astype(jnp.float32)
            sides.append(jnp.where(place < bound, values, 0.0).astype(jnp.bfloat16))
        values = jnp.concatenate(sides, 1)
        values = jnp.concatenate([values, values], 0)
        mixed = jnp.dot(first[...], values, preferred_element_type=jnp.float32)
        parts = []
        for core in range(2):
            real = mixed[:ROWS, core * LANES : (core + 1) * LANES]
            imag = mixed[ROWS:, core * LANES : (core + 1) * LANES]
            turned_re = real * twist[0] + imag * twist[1]
            turned_im = imag * twist[0] - real * twist[1]
            parts.append(jnp.concatenate([turned_re, turned_im], 1))
        turned = jnp.concatenate(parts, 0)
        high = turned.astype(jnp.bfloat16)
        low = (turned - high.astype(jnp.float32)).astype(jnp.bfloat16)
        upper = jnp.dot(high, second[...], preferred_element_type=jnp.float32)
        lower = jnp.dot(low, second[:, :LANES], preferred_element_type=jnp.float32)
        spectrum = upper[:, :LANES] + (upper[:, LANES:] + lower)
        for core in range(2):
            side = spectrum[core * ROWS : (core + 1) * ROWS]
            power = jnp.sum(side * side, axis=0, keepdims=True)
            power = (power + pltpu.roll(power, LANES // 2, 1)) * (1.0 / ROWS)
            scale = 1.0 / jnp.sqrt(power + 1e-06)
            spectra[station, core] = (side * scale).astype(jnp.bfloat16)

    @pl.loop(0, stations // 2)
    def _(pair):
        one_station(2 * pair)
        one_station(2 * pair + 1)

    whole = pltpu.make_async_copy(spectra, white, sem)
    whole.start()
    stops, rows = picks.shape

    @pl.loop(0, stops)
    def _(stop):
        for at in range(rows):
            pltpu.make_async_copy(spectra.at[picks[stop, at]], payload.at[stop, at], sem).start()

    whole.wait()

    @pl.loop(0, stops * rows)
    def _(_):
        pltpu.make_async_copy(spectra.at[0], payload.at[0, 0], sem).wait()


def whiten(part, source, length, picks, got, more, tables):
    stops, rows = picks.shape
    return pl.pallas_call(
        functools.partial(whiten_kernel, part),
        out_shape=(
            jax.ShapeDtypeStruct((ST_DEV, 2, ROWS, LANES), jnp.bfloat16),
            jax.ShapeDtypeStruct((stops, rows, 2, ROWS, LANES), jnp.bfloat16),
        ),
        in_specs=[SMEM, SMEM, SMEM, ANY, ANY, VMEM, VMEM, VMEM],
        out_specs=(ANY, ANY),
        scratch_shapes=[
            pltpu.VMEM((ST_DEV, 2, ROWS, LANES), jnp.bfloat16),
            pltpu.VMEM((ST_DEV, 2, ROWS, LANES), jnp.bfloat16),
            pltpu.SemaphoreType.DMA,
        ],
        cost_estimate=pl.CostEstimate(
            flops=2 * ST_DEV * 2 * ROWS * 256 * 400, bytes_accessed=4 * 1024 * 1024, transcendentals=0
        ),
        name="whiten",
    )(source, length, picks, got, more, *tables)


def lag_kernel(stops, near_pick, far_at, *refs):
    white_a, white_b, home = refs[:3]
    far_a = refs[3 : 2 + stops]
    far_b, table, mask, out, near, far, cross, tables, sem, table_sem = refs[2 + stops :]
    rows = near_pick.shape[1]
    load_table = pltpu.make_async_copy(table, tables, table_sem)
    copies = [
        pltpu.make_async_copy(white_a, near.at[0], sem),
        pltpu.make_async_copy(white_b, near.at[1], sem),
        pltpu.make_async_copy(home.at[0], far.at[0, 0], sem),
    ]
    for stop in range(1, stops):
        copies.append(pltpu.make_async_copy(far_a[stop - 1], far.at[0, stop], sem))
    for stop in range(stops):
        copies.append(pltpu.make_async_copy(far_b.at[far_at[stop]], far.at[1, stop], sem))
    for copy in copies:
        copy.start()
    load_table.start()
    for copy in copies:
        copy.wait()
    step = 16
    side = rows // 2
    left = lax.broadcasted_iota(jnp.int32, (step, LANES), 1) < LANES // 2

    @pl.loop(0, stops * 2)
    def _(block):
        stop = block // 2
        first = (block % 2) * side
        own = [near_pick[stop, first + i] for i in range(side)]

        @pl.loop(0, ROWS // step)
        def _(chunk):
            band = pl.ds(pl.multiple_of(chunk * step, step), step)
            here = [
                [near[s % 2, own[i], s // 2, band, :].astype(jnp.float32) for s in range(SEG)]
                for i in range(side)
            ]
            for j in range(side):
                straight, crossed = [], []
                for s in range(SEG):
                    value = far[s % 2, stop, first + j, s // 2, band, :].astype(jnp.float32)
                    other = pltpu.roll(value, LANES // 2, 1)
                    straight.append(jnp.where(left, value, other))
                    crossed.append(jnp.where(left, -other, value))
                for i in range(side):
                    direct = here[i][0] * straight[0]
                    turned = here[i][0] * crossed[0]
                    for s in range(1, SEG):
                        direct += here[i][s] * straight[s]
                        turned += here[i][s] * crossed[s]
                    pair = (block * side + i) * side + j
                    cross[pl.ds(pl.multiple_of(pair * ROWS + chunk * step, step), step), :] = (
                        direct + pltpu.roll(turned, LANES // 2, 1)
                    )

    load_table.wait()
    pairs = stops * 2 * side * side
    group = 8
    out[...] = jnp.zeros_like(out)

    @pl.loop(0, ROWS // group)
    def _(at):
        slabs = [
            cross[pl.ds(at * group + k, pairs, stride=ROWS), :].astype(jnp.bfloat16) for k in range(group)
        ]
        depth = group * LANES
        out[...] += jnp.dot(
            jnp.concatenate(slabs, 1),
            tables[pl.ds(pl.multiple_of(at * depth, depth), depth), :],
            preferred_element_type=jnp.float32,
        )

    out[...] = out[...] * mask[...]


def lagged(near_pick, far_at, white_a, white_b, home, far_a, far_b, table, mask):
    stops, rows = near_pick.shape
    pairs = mask.shape[0]
    return pl.pallas_call(
        functools.partial(lag_kernel, stops),
        out_shape=jax.ShapeDtypeStruct((pairs, LAGS), jnp.float32),
        in_specs=[SMEM, SMEM] + [ANY] * (stops + 4) + [VMEM],
        out_specs=VMEM,
        scratch_shapes=[
            pltpu.VMEM((2, ST_DEV, 2, ROWS, LANES), jnp.bfloat16),
            pltpu.VMEM((2, stops, rows, 2, ROWS, LANES), jnp.bfloat16),
            pltpu.VMEM((pairs * ROWS, LANES), jnp.float32),
            pltpu.VMEM(table.shape, jnp.bfloat16),
            pltpu.SemaphoreType.DMA,
            pltpu.SemaphoreType.DMA,
        ],
        compiler_params=pltpu.CompilerParams(vmem_limit_bytes=48 * 1024 * 1024),
        cost_estimate=pl.CostEstimate(
            flops=2 * pairs * 2 * NF * LAGS, bytes_accessed=24 * 1024 * 1024, transcendentals=0
        ),
        name="lagged",
    )(near_pick, far_at, white_a, white_b, home, *far_a, far_b, table, mask)


def on_device(records, lengths, owners, own_pick, visit_pick, pair_mask):
    wide_count = lax.axis_size("wide")
    stops = lax.axis_size("blk")
    column = lax.axis_index("wide")
    group = lax.axis_index("blk")
    core = column % 2
    swap = [(i, i ^ 1) for i in range(wide_count)]
    slots = records.shape[1]

    packed = jnp.where(owners[0] >= 0, (owners[0] << LEN_BITS) + lengths[0], -1)
    mate_packed = lax.ppermute(packed, "wide", swap)
    all_packed = lax.all_gather(packed, "wide").reshape(wide_count // 2, 2 * slots)
    all_visits = lax.all_gather(visit_pick[0, 0].reshape(stops, -1), "blk")

    own = records[0].reshape(slots, SEG, ROWS, LANES)
    chip_packed = jnp.where(
        core == 0, jnp.concatenate([packed, mate_packed]), jnp.concatenate([mate_packed, packed])
    )
    core_at = core.reshape(1)
    mates = [
        lax.ppermute(lax.dynamic_index_in_dim(own, 2 * (1 - core) + part, 1, False), "wide", swap)
        for part in range(2)
    ]

    def deliver(low, count, part):
        payload = pack(part, low, count, wide_count, chip_packed, core_at, own, mates[part])
        return lax.all_to_all(payload, "wide", split_axis=0, concat_axis=0, tiled=True)

    got = [deliver(0, BASE, part) for part in range(2)]

    station = all_packed >> LEN_BITS
    owner_dev = station // ST_DEV
    everyone = jnp.arange(wide_count, dtype=jnp.int32)
    counts = jnp.sum((owner_dev[:, :, None] == everyone).astype(jnp.int32), axis=1)
    spilled = lax.pmax(jnp.max(counts), "blk") > BASE
    mine = owner_dev == column
    rank = jnp.cumsum(mine.astype(jnp.int32), axis=1) - 1
    chip = jnp.arange(wide_count // 2, dtype=jnp.int32)[:, None]
    code = jnp.where(rank < BASE, chip * BASE + rank, 16 * BASE + chip * EXTRA + rank - BASE)
    local = column * ST_DEV + jnp.arange(ST_DEV, dtype=jnp.int32)
    chosen = station[None] == local[:, None, None]
    source = jnp.sum(jnp.where(chosen, code[None], 0), axis=(1, 2))
    length = jnp.sum(jnp.where(chosen, (all_packed & ((1 << LEN_BITS) - 1))[None], 0), axis=(1, 2))

    more = lax.cond(
        spilled,
        lambda: tuple(deliver(BASE, EXTRA, part) for part in range(2)),
        lambda: tuple(jnp.zeros((wide_count, EXTRA, ROWS, LANES), jnp.bfloat16) for _ in range(2)),
    )

    steps = jnp.arange(stops, dtype=jnp.int32)
    by_stop = all_visits[(group + steps) % stops, steps]
    by_dest = all_visits[steps, (steps - group) % stops]
    tables = [jnp.asarray(table) for table in transform_tables()]

    white_a, payload_a = whiten(0, source, length, by_stop, got[0], more[0], tables)
    far_a = [
        lax.ppermute(payload_a[stop], "blk", [(i, (i + stop) % stops) for i in range(stops)])
        for stop in range(1, stops)
    ]
    white_b, payload_b = whiten(1, source, length, by_dest, got[1], more[1], tables)
    far_b = lax.all_to_all(payload_b, "blk", split_axis=0, concat_axis=0, tiled=True)

    near_pick = own_pick[0, 0].reshape(stops, -1)
    far_at = (group - steps) % stops
    mask = pair_mask[0, 0].astype(jnp.float32).reshape(-1, 1)
    result = lagged(near_pick, far_at, white_a, white_b, payload_a, far_a, far_b, jnp.asarray(lag_table()), mask)
    return result.reshape((1, 1) + pair_mask.shape[2:] + (LAGS,))


def solution(mesh):
    return jax.shard_map(
        on_device,
        mesh=mesh,
        in_specs=(
            P("blk", "wide", None, None),
            P("blk", "wide"),
            P("blk", "wide"),
            P("blk", "wide", None, None, None),
            P("blk", "wide", None, None, None),
            P("blk", "wide", None, None, None, None),
        ),
        out_specs=P("blk", "wide", None, None, None, None, None),
        check_vma=False,
    )
```

time: 576 us -> 313 us (0.54)
  the two profiles are of different devices: /device:TPU:72 before, /device:TPU:1 now
where the time goes in v1:
time: 313 us; the launch traced here: 310 us
  Pallas kernels  79.7 us (25%)
  blocking collectives  75.6 us (24%)
  waiting for transfers between devices  60.7 us (19%)
  starting transfers between devices  56.6 us (18%)
  local copies, waits for them, and re-layouts  33.2 us (11%)
  other arithmetic  3.55 us (1%)
    all_to_all x2, waiting for transfers between devices, deliver(): lax.all_to_all(payload, 'wide', split_axis=0, concat_axis=0, tiled=True)  38.7 us
    all_gather x1, blocking collectives, on_device(): lax.all_gather(packed, 'wide').reshape(wide_count // 2, 2 * slots)  35.6 us
    pallas_call x2, Pallas kernels, pack(): pl.pallas_call(functools.partial(pack_kernel, part, low, count), out_shap...  32.2 us
    all_to_all x2, starting transfers between devices, deliver(): lax.all_to_all(payload, 'wide', split_axis=0, concat_axis=0, tiled=True)  31 us
    all_gather x1, blocking collectives, on_device(): all_visits = lax.all_gather(visit_pick[0, 0].reshape(stops, -1), 'blk')  28.9 us
    pallas_call x1, Pallas kernels, lagged(): pl.pallas_call(functools.partial(lag_kernel, stops), out_shape=jax.ShapeD...  25.1 us
    pallas_call x2, Pallas kernels, whiten(): pl.pallas_call(functools.partial(whiten_kernel, part), out_shape=(jax.Sha...  22.4 us
    ppermute x7, waiting for transfers between devices, on_device(): lax.ppermute(payload_a[stop], 'blk', [(i, (i + stop) % stops) for i in ra...  22 us
  transfers between devices with their start and end apart: 13, of which 5 were waited for; matrix products, arithmetic and copies ran while one was open for 3% of the time, Pallas kernels for 12%

profile of v1, /device:TPU:1, one launch (start us, length us, event | category | flops | bytes accessed | tf_op | source)
XLA Modules:
  0.0 310.3 jit_solution(5134091103356306809)
XLA Ops:
  0.0 9.6 %reshape_squeeze.7.own = bf16[72,4,64,128]{3,2,1,0:T(8,128)(2,1)} reshape(bf16[1,72,4,8192]{3,2,1,0:T(4,128)(2,1)} %param.12) | data formatting | bytes 9437184 | tf_op jit(solution)/shard_map/reshape;squeeze | solution.py:322
  9.6 3.6 %dynamic-slice_bitcast_fusion = (bf16[72,64,128]{2,1,0:T(8,128)(2,1)}, bf16[72,64,128]{2,1,0:T(8,128)(2,1)}) fusion(bf16[72,4,64,128]{3,2,1,0:T(8,128)(2,1)} %reshape_squeeze.7.own, s32[]{:T(128)S(6)} %select_n.112, s32[]{:T(128)S(6)} %select_n.111), kind=kLoop, calls=%fused_computation.2 | loop fusion | bytes 4718600 | tf_op jit(solution)/shard_map/jit(dynamic_index_in_dim)/squeeze | solution.py:328
  13.2 3.2 %collective-permute-start.2 = (bf16[72,64,128]{2,1,0:T(8,128)(2,1)}, bf16[72,64,128]{2,1,0:T(8,128)(2,1)S(1)}, u32[]{:S(2)}, u32[]{:S(2)}) collective-permute-start(bf16[72,64,128]{2,1,0:T(8,128)(2,1)} %get-tuple-element.38), channel_id=1, source_target_pairs={{0,8},{8,0},{16,24},{24,16},{32,40},{40,32},{48,56},{56,48},{64,72... | collective-permute-start | bytes 3538952 | tf_op jit(solution)/shard_map/ppermute | solution.py:328
  16.4 35.6 %all-gather = s32[32,1,72]{2,1,0:T(1,128)S(1)} all-gather(s32[1,1,72]{2,1,0:T(1,128)S(1)} %fusion.15), channel_id=1, replica_groups=mesh['wide'=32,'blk'=8] {'wide'}, dimensions={0}, use_global_device_ids=true | all-gather | bytes 9504 | tf_op jit(solution)/shard_map/all_gather | solution.py:319
  53.4 11.1 %pmax.7 = s32[]{:T(128)} all-reduce(s32[]{:T(128)} %reduce_max.9), channel_id=1, replica_groups=mesh['wide'=32,'blk'=8] {'blk'}, use_global_device_ids=true, to_apply=%region_6.7 | all-reduce | flops 1 | bytes 8 | tf_op jit(solution)/shard_map/pmax | solution.py:342
  65.3 2.4 conditional.1
  65.3 1.2 broadcast.209.clone
  66.5 1.2 broadcast.209
  67.7 16.1 %pack.7 = bf16[32,4,64,128]{3,2,1,0:T(8,128)(2,1)} custom-call(s32[144]{0:T(256)S(1)} %add_select_fusion.2.packed, s32[1]{0:T(128)} %bitcast.5.core_ref, bf16[72,4,64,128]{3,2,1,0:T(8,128)(2,1)} %reshape_squeeze.7.own, bf16[72,64,128]{2,1,0:T(8,128)(2,1)S(1)} %collective-permute-done.2.mate), custom_call_target="tpu_custom_call" | custom-call | bytes 4194304 | tf_op jit(solution)/shard_map/pack/pallas_call | solution.py:96
  83.8 25.5 %all-to-all-start.3 = ((bf16[32,4,64,128]{3,2,1,0:T(8,128)(2,1)}), bf16[32,4,64,128]{3,2,1,0:T(8,128)(2,1)S(1)}, u32[]{:S(2)}, u32[]{:S(2)}) async-start(bf16[32,4,64,128]{3,2,1,0:T(8,128)(2,1)} %pack.7), calls=%async_computation.3 | async-start | bytes 4194304 | tf_op jit(solution)/shard_map/all_to_all | solution.py:334
  109.3 16.1 %pack.6 = bf16[32,4,64,128]{3,2,1,0:T(8,128)(2,1)} custom-call(s32[144]{0:T(256)S(1)} %add_select_fusion.2.packed, s32[1]{0:T(128)} %bitcast.5.core_ref, bf16[72,4,64,128]{3,2,1,0:T(8,128)(2,1)} %reshape_squeeze.7.own, bf16[72,64,128]{2,1,0:T(8,128)(2,1)S(1)} %collective-permute-done.1.mate), custom_call_target="tpu_custom_call" | custom-call | bytes 4194304 | tf_op jit(solution)/shard_map/pack/pallas_call | solution.py:96
  125.5 33.3 %all-to-all-done.3.got = bf16[32,4,64,128]{3,2,1,0:T(8,128)(2,1)S(1)} async-done(((bf16[32,4,64,128]{3,2,1,0:T(8,128)(2,1)}), bf16[32,4,64,128]{3,2,1,0:T(8,128)(2,1)S(1)}, u32[]{:S(2)}, u32[]{:S(2)}) %all-to-all-start.3) | async-done | bytes 2097184 | tf_op jit(solution)/shard_map/all_to_all | solution.py:334
  158.7 1.3 copy-done.11
  160.1 5.5 %all-to-all-start.2 = ((bf16[32,4,64,128]{3,2,1,0:T(8,128)(2,1)}), bf16[32,4,64,128]{3,2,1,0:T(8,128)(2,1)S(1)}, u32[]{:S(2)}, u32[]{:S(2)}) async-start(bf16[32,4,64,128]{3,2,1,0:T(8,128)(2,1)} %pack.6), calls=%async_computation.2 | async-start | bytes 4194304 | tf_op jit(solution)/shard_map/all_to_all | solution.py:334
  166.6 28.9 %all_gather.8 = s32[8,8,8]{2,1,0:T(8,128)S(1)} all-gather(s32[1,8,8]{2,1,0:T(8,128)S(1)} %copy.28), channel_id=1, replica_groups=mesh['wide'=32,'blk'=8] {'blk'}, dimensions={0}, use_global_device_ids=true | all-gather | bytes 2304 | tf_op jit(solution)/shard_map/all_gather | solution.py:320
  195.5 1.2 gather_fusion.1
  196.8 1.5 fusion.1
  198.3 11.3 %whiten.3 = (bf16[24,2,64,128]{3,2,1,0:T(8,128)(2,1)}, bf16[8,8,2,64,128]{4,3,2,1,0:T(8,128)(2,1)}) custom-call(s32[24]{0:T(128)} %get-tuple-element.33.source, s32[24]{0:T(128)} %get-tuple-element.32.length, s32[8,8]{1,0:T(8,128)} %gather_fusion.1, bf16[32,4,64,128]{3,2,1,0:T(8,128)(2,1)} %copy-done.11, bf16[32,2,64,128]{3,2,1,0:T(8,128)(2,1)} %get-tuple-element.28.more, ...), custom_call_target="tpu_custom_call" | custom-call | flops 629145600 | bytes 4194304 | tf_op jit(solution)/shard_map/whiten/pallas_call | solution.py:189
  209.6 5.4 %all-to-all-done.2.got = bf16[32,4,64,128]{3,2,1,0:T(8,128)(2,1)S(1)} async-done(((bf16[32,4,64,128]{3,2,1,0:T(8,128)(2,1)}), bf16[32,4,64,128]{3,2,1,0:T(8,128)(2,1)S(1)}, u32[]{:S(2)}, u32[]{:S(2)}) %all-to-all-start.2) | async-done | bytes 2097184 | tf_op jit(solution)/shard_map/all_to_all | solution.py:334
  215.0 1.3 copy-done.10
  216.3 5.2 %all-to-all-start.4 = ((bf16[8,8,2,64,128]{4,3,2,1,0:T(8,128)(2,1)}), bf16[8,8,2,64,128]{4,3,2,1,0:T(8,128)(2,1)}, u32[]{:S(2)}, u32[]{:S(2)}) async-start(bf16[8,8,2,64,128]{4,3,2,1,0:T(8,128)(2,1)} %get-tuple-element.31), calls=%async_computation.4 | async-start | bytes 4194304 | tf_op jit(solution)/shard_map/all_to_all | solution.py:369
  221.5 1.2 gather_fusion
  222.7 11.2 %whiten.2 = (bf16[24,2,64,128]{3,2,1,0:T(8,128)(2,1)}, bf16[8,8,2,64,128]{4,3,2,1,0:T(8,128)(2,1)}) custom-call(s32[24]{0:T(128)} %get-tuple-element.33.source, s32[24]{0:T(128)} %get-tuple-element.32.length, s32[8,8]{1,0:T(8,128)} %gather_fusion, bf16[32,4,64,128]{3,2,1,0:T(8,128)(2,1)} %copy-done.10, bf16[32,2,64,128]{3,2,1,0:T(8,128)(2,1)} %get-tuple-element.26.more, ...), custom_call_target="tpu_custom_call" | custom-call | flops 629145600 | bytes 4194304 | tf_op jit(solution)/shard_map/whiten/pallas_call | solution.py:189
  233.9 2.7 slice_bitcast_fusion
  236.6 5.1 %collective-permute-start.9 = (bf16[8,2,64,128]{3,2,1,0:T(8,128)(2,1)S(1)}, bf16[8,2,64,128]{3,2,1,0:T(8,128)(2,1)S(1)}, u32[]{:S(2)}, u32[]{:S(2)}) collective-permute-start(bf16[8,2,64,128]{3,2,1,0:T(8,128)(2,1)S(1)} %get-tuple-element.40), channel_id=1, source_target_pairs={{0,7},{1,0},{2,1},{3,2},{4,3},{5,4},{6,5},{7,6},{8,15},{9,8},{10,9... | collective-permute-start | bytes 786440 | tf_op jit(solution)/shard_map/ppermute | solution.py:365
  242.8 2.7 collective-permute-start.6
  245.5 15.6 %collective-permute-done.9.refs_9_ = bf16[8,2,64,128]{3,2,1,0:T(8,128)(2,1)S(1)} collective-permute-done((bf16[8,2,64,128]{3,2,1,0:T(8,128)(2,1)S(1)}, bf16[8,2,64,128]{3,2,1,0:T(8,128)(2,1)S(1)}, u32[]{:S(2)}, u32[]{:S(2)}) %collective-permute-start.9) | collective-permute-done | bytes 262176 | tf_op jit(solution)/shard_map/ppermute | solution.py:365
  261.1 8.0 %collective-permute-start.3 = (bf16[8,2,64,128]{3,2,1,0:T(8,128)(2,1)}, bf16[8,2,64,128]{3,2,1,0:T(8,128)(2,1)S(1)}, u32[]{:S(2)}, u32[]{:S(2)}) collective-permute-start(bf16[8,2,64,128]{3,2,1,0:T(8,128)(2,1)} %get-tuple-element.46), channel_id=1, source_target_pairs={{0,1},{1,2},{2,3},{3,4},{4,5},{5,6},{6,7},{7,0},{8,9},{9,10},{10,1... | collective-permute-start | bytes 786440 | tf_op jit(solution)/shard_map/ppermute | solution.py:365
  273.5 5.9 %collective-permute-done.3.refs_3_ = bf16[8,2,64,128]{3,2,1,0:T(8,128)(2,1)S(1)} collective-permute-done((bf16[8,2,64,128]{3,2,1,0:T(8,128)(2,1)}, bf16[8,2,64,128]{3,2,1,0:T(8,128)(2,1)S(1)}, u32[]{:S(2)}, u32[]{:S(2)}) %collective-permute-start.3) | collective-permute-done | bytes 262176 | tf_op jit(solution)/shard_map/ppermute | solution.py:365
  281.1 0.9 copy-done.5
  283.9 25.1 %lagged.1 = f32[256,1024]{1,0:T(8,128)S(1)} custom-call(s32[8,8]{1,0:T(8,128)S(1)} %copy.30.near_pick, s32[8]{0:T(128)S(1)} %and_select_fusion.2.far_at, bf16[24,2,64,128]{3,2,1,0:T(8,128)(2,1)S(1)} %copy-done.1, bf16[24,2,64,128]{3,2,1,0:T(8,128)(2,1)S(1)} %copy-done, bf16[8,8,2,64,128]{4,3,2,1,0:T(8,128)(2,1)} %get-tuple-element.30.refs_2_, ...), custom_call_target="tpu_custom_call" | custom-call | flops 4294967296 | bytes 25165824 | tf_op jit(solution)/shard_map/lagged/pallas_call | solution.py:287
  309.0 1.3 reshape.182
  (72 shorter events, 11.7 us)
Async XLA Ops:
  9.6 6.8 %copy-start.15 = (s32[1,72]{1,0:T(1,128)S(1)}, s32[1,72]{1,0:T(1,128)}, u32[]{:S(2)}) copy-start(s32[1,72]{1,0:T(1,128)} %param.13) | copy-start | bytes 868
  9.6 6.8 %copy-start.16 = (s32[1,72]{1,0:T(1,128)S(1)}, s32[1,72]{1,0:T(1,128)}, u32[]{:S(2)}) copy-start(s32[1,72]{1,0:T(1,128)} %param.14) | copy-start | bytes 868
  13.2 52.1 %collective-permute-start.2 = (bf16[72,64,128]{2,1,0:T(8,128)(2,1)}, bf16[72,64,128]{2,1,0:T(8,128)(2,1)S(1)}, u32[]{:S(2)}, u32[]{:S(2)}) collective-permute-start(bf16[72,64,128]{2,1,0:T(8,128)(2,1)} %get-tuple-element.38), channel_id=1, source_target_pairs={{0,8},{8,0},{16,24},{24,16},{32,40},{40,32},{48,56},{56,48},{64,72... | collective-permute-start | bytes 3538952 | tf_op jit(solution)/shard_map/ppermute | solution.py:328
  16.4 48.9 %collective-permute-start.1 = (bf16[72,64,128]{2,1,0:T(8,128)(2,1)}, bf16[72,64,128]{2,1,0:T(8,128)(2,1)S(1)}, u32[]{:S(2)}, u32[]{:S(2)}) collective-permute-start(bf16[72,64,128]{2,1,0:T(8,128)(2,1)} %get-tuple-element.39), channel_id=1, source_target_pairs={{0,8},{8,0},{16,24},{24,16},{32,40},{40,32},{48,56},{56,48},{64,72... | collective-permute-start | bytes 3538952 | tf_op jit(solution)/shard_map/ppermute | solution.py:328
  53.2 12.0 %collective-permute-start = (s32[72]{0:T(128)S(1)}, s32[72]{0:T(128)S(1)}, u32[]{:S(2)}, u32[]{:S(2)}) collective-permute-start(s32[72]{0:T(128)S(1)} %fusion.14), channel_id=1, source_target_pairs={{0,8},{8,0},{16,24},{24,16},{32,40},{40,32},{48,56},{56,48},{64,72... | collective-permute-start | bytes 872 | tf_op jit(solution)/shard_map/ppermute | solution.py:318
  83.8 74.9 %all-to-all-start.3 = ((bf16[32,4,64,128]{3,2,1,0:T(8,128)(2,1)}), bf16[32,4,64,128]{3,2,1,0:T(8,128)(2,1)S(1)}, u32[]{:S(2)}, u32[]{:S(2)}) async-start(bf16[32,4,64,128]{3,2,1,0:T(8,128)(2,1)} %pack.7), calls=%async_computation.3 | async-start | bytes 4194304 | tf_op jit(solution)/shard_map/all_to_all | solution.py:334
  125.4 40.2 %copy-start.13 = (s32[1,1,8,2,4]{2,4,3,1,0:T(4,128)S(1)}, s32[1,1,8,2,4]{2,4,3,1,0:T(4,128)}, u32[]{:S(2)}) copy-start(s32[1,1,8,2,4]{2,4,3,1,0:T(4,128)} %param.16) | copy-start | bytes 772
  158.7 1.3 copy-start.11
  160.1 54.9 %all-to-all-start.2 = ((bf16[32,4,64,128]{3,2,1,0:T(8,128)(2,1)}), bf16[32,4,64,128]{3,2,1,0:T(8,128)(2,1)S(1)}, u32[]{:S(2)}, u32[]{:S(2)}) async-start(bf16[32,4,64,128]{3,2,1,0:T(8,128)(2,1)} %pack.6), calls=%async_computation.2 | async-start | bytes 4194304 | tf_op jit(solution)/shard_map/all_to_all | solution.py:334
  215.0 1.3 copy-start.10
  216.3 63.8 %all-to-all-start.4 = ((bf16[8,8,2,64,128]{4,3,2,1,0:T(8,128)(2,1)}), bf16[8,8,2,64,128]{4,3,2,1,0:T(8,128)(2,1)}, u32[]{:S(2)}, u32[]{:S(2)}) async-start(bf16[8,8,2,64,128]{4,3,2,1,0:T(8,128)(2,1)} %get-tuple-element.31), calls=%async_computation.4 | async-start | bytes 4194304 | tf_op jit(solution)/shard_map/all_to_all | solution.py:369
  233.9 35.2 %copy-start.14 = (s32[1,1,8,2,4]{2,4,3,1,0:T(4,128)S(1)}, s32[1,1,8,2,4]{2,4,3,1,0:T(4,128)}, u32[]{:S(2)}) copy-start(s32[1,1,8,2,4]{2,4,3,1,0:T(4,128)} %param.15) | copy-start | bytes 772
  233.9 35.3 %copy-start.12 = (s32[1,1,8,2,4,4]{2,5,4,3,1,0:T(4,128)S(1)}, s32[1,1,8,2,4,4]{2,5,4,3,1,0:T(4,128)}, u32[]{:S(2)}) copy-start(s32[1,1,8,2,4,4]{2,5,4,3,1,0:T(4,128)} %param.17) | copy-start | bytes 3076
  233.9 46.2 %copy-start = (bf16[24,2,64,128]{3,2,1,0:T(8,128)(2,1)S(1)}, bf16[24,2,64,128]{3,2,1,0:T(8,128)(2,1)}, u32[]{:S(2)}) copy-start(bf16[24,2,64,128]{3,2,1,0:T(8,128)(2,1)} %get-tuple-element.29.refs_1_) | copy-start | bytes 2359300
  233.9 46.2 %copy-start.1 = (bf16[24,2,64,128]{3,2,1,0:T(8,128)(2,1)S(1)}, bf16[24,2,64,128]{3,2,1,0:T(8,128)(2,1)}, u32[]{:S(2)}) copy-start(bf16[24,2,64,128]{3,2,1,0:T(8,128)(2,1)} %get-tuple-element.27.refs_0_) | copy-start | bytes 2359300
  236.6 24.5 %collective-permute-start.9 = (bf16[8,2,64,128]{3,2,1,0:T(8,128)(2,1)S(1)}, bf16[8,2,64,128]{3,2,1,0:T(8,128)(2,1)S(1)}, u32[]{:S(2)}, u32[]{:S(2)}) collective-permute-start(bf16[8,2,64,128]{3,2,1,0:T(8,128)(2,1)S(1)} %get-tuple-element.40), channel_id=1, source_target_pairs={{0,7},{1,0},{2,1},{3,2},{4,3},{5,4},{6,5},{7,6},{8,15},{9,8},{10,9... | collective-permute-start | bytes 786440 | tf_op jit(solution)/shard_map/ppermute | solution.py:365
  241.7 19.4 %collective-permute-start.8 = (bf16[8,2,64,128]{3,2,1,0:T(8,128)(2,1)S(1)}, bf16[8,2,64,128]{3,2,1,0:T(8,128)(2,1)S(1)}, u32[]{:S(2)}, u32[]{:S(2)}) collective-permute-start(bf16[8,2,64,128]{3,2,1,0:T(8,128)(2,1)S(1)} %get-tuple-element.41), channel_id=1, source_target_pairs={{0,6},{1,7},{2,0},{3,1},{4,2},{5,3},{6,4},{7,5},{8,14},{9,15},{10,... | collective-permute-start | bytes 786440 | tf_op jit(solution)/shard_map/ppermute | solution.py:365
  242.3 28.5 %collective-permute-start.7 = (bf16[8,2,64,128]{3,2,1,0:T(8,128)(2,1)}, bf16[8,2,64,128]{3,2,1,0:T(8,128)(2,1)S(1)}, u32[]{:S(2)}, u32[]{:S(2)}) collective-permute-start(bf16[8,2,64,128]{3,2,1,0:T(8,128)(2,1)} %get-tuple-element.42), channel_id=1, source_target_pairs={{0,5},{1,6},{2,7},{3,0},{4,1},{5,2},{6,3},{7,4},{8,13},{9,14},{10,... | collective-permute-start | bytes 786440 | tf_op jit(solution)/shard_map/ppermute | solution.py:365
  242.8 28.0 %collective-permute-start.6 = (bf16[8,2,64,128]{3,2,1,0:T(8,128)(2,1)}, bf16[8,2,64,128]{3,2,1,0:T(8,128)(2,1)S(1)}, u32[]{:S(2)}, u32[]{:S(2)}) collective-permute-start(bf16[8,2,64,128]{3,2,1,0:T(8,128)(2,1)} %get-tuple-element.43), channel_id=1, source_target_pairs={{0,4},{1,5},{2,6},{3,7},{4,0},{5,1},{6,2},{7,3},{8,12},{9,13},{10,... | collective-permute-start | bytes 786440 | tf_op jit(solution)/shard_map/ppermute | solution.py:365
  245.5 26.0 %collective-permute-start.5 = (bf16[8,2,64,128]{3,2,1,0:T(8,128)(2,1)}, bf16[8,2,64,128]{3,2,1,0:T(8,128)(2,1)S(1)}, u32[]{:S(2)}, u32[]{:S(2)}) collective-permute-start(bf16[8,2,64,128]{3,2,1,0:T(8,128)(2,1)} %get-tuple-element.44), channel_id=1, source_target_pairs={{0,3},{1,4},{2,5},{3,6},{4,7},{5,0},{6,1},{7,2},{8,11},{9,12},{10,... | collective-permute-start | bytes 786440 | tf_op jit(solution)/shard_map/ppermute | solution.py:365
  261.1 11.7 %collective-permute-start.4 = (bf16[8,2,64,128]{3,2,1,0:T(8,128)(2,1)}, bf16[8,2,64,128]{3,2,1,0:T(8,128)(2,1)S(1)}, u32[]{:S(2)}, u32[]{:S(2)}) collective-permute-start(bf16[8,2,64,128]{3,2,1,0:T(8,128)(2,1)} %get-tuple-element.45), channel_id=1, source_target_pairs={{0,2},{1,3},{2,4},{3,5},{4,6},{5,7},{6,0},{7,1},{8,10},{9,11},{10,... | collective-permute-start | bytes 786440 | tf_op jit(solution)/shard_map/ppermute | solution.py:365
  261.1 18.3 %collective-permute-start.3 = (bf16[8,2,64,128]{3,2,1,0:T(8,128)(2,1)}, bf16[8,2,64,128]{3,2,1,0:T(8,128)(2,1)S(1)}, u32[]{:S(2)}, u32[]{:S(2)}) collective-permute-start(bf16[8,2,64,128]{3,2,1,0:T(8,128)(2,1)} %get-tuple-element.46), channel_id=1, source_target_pairs={{0,1},{1,2},{2,3},{3,4},{4,5},{5,6},{6,7},{7,0},{8,9},{9,10},{10,1... | collective-permute-start | bytes 786440 | tf_op jit(solution)/shard_map/ppermute | solution.py:365
  270.8 0.7 copy-start.2
  271.5 0.7 copy-start.4
  272.8 0.7 copy-start.6
  279.4 0.7 copy-start.8
  280.1 1.0 copy-start.3
  281.1 0.9 copy-start.5
  282.0 0.9 copy-start.7
  283.0 0.9 copy-start.9

commit v2 on v1

--- a/solution.py
+++ b/solution.py
@@ -16,8 +16,8 @@
 LAGS = 1024
 ROWS = 64
 LANES = 128
-BASE = 4
-EXTRA = 2
+BASE = 2
+EXTRA = 1
 LEN_BITS = 16
 SMEM = pl.BlockSpec(memory_space=pltpu.SMEM)
 VMEM = pl.BlockSpec(memory_space=pltpu.VMEM)
@@ -36,6 +36,7 @@
     half = np.arange(LANES // 2)
     angle = 2.0 * math.pi / ROWS * (first[:, None] * first[None, :] % ROWS)
     wave = np.concatenate([np.cos(angle), -np.sin(angle)], 0)
+    wave = np.einsum("ab,kn->aknb", np.eye(2), wave).reshape(4 * ROWS, 2 * ROWS)
     first_table = np.concatenate(split_bf16(wave), 1)
     twist = 2.0 * math.pi / NT * (first[:, None] * second[None, :] % NT)
     twist_table = np.stack([np.cos(twist), np.sin(twist)]).astype(np.float32)
@@ -58,48 +59,59 @@
     return joined.reshape(ROWS * LANES, LAGS).astype(jnp.bfloat16)
 
 
-def pack_kernel(part, low, count, packed, core_ref, own, mate, out, fill, sem):
+def pack_kernel(low, count, packed, core_ref, own, mate, out, fill, started, sem):
     core = core_ref[0]
-    slots = packed.shape[0] // 2
+    slots = packed.shape[1]
+    started[0] = 0
 
     @pl.loop(0, out.shape[0])
     def _(dev):
         fill[dev] = 0
 
-    def place(at, started, half):
-        value = packed[at + half * slots]
-        valid = value >= 0
-        dev = jnp.where(valid, value >> LEN_BITS, 0) // ST_DEV
-        rank = fill[dev]
-        fill[dev] = rank + valid.astype(jnp.int32)
-        take = valid & (rank >= low) & (rank < low + count)
-
-        @pl.when(take & (core == half))
+    def place(half, source):
+        @pl.loop(0, slots)
+        def _(at):
+            value = packed[half, at]
+
+            @pl.when(value >= 0)
+            def _():
+                dev = ((value >> LEN_BITS) * 2731) >> 16
+                rank = fill[dev]
+                fill[dev] = rank + 1
+                slot = (rank >> 1) - low
+
+                @pl.when(((rank & 1) == core) & (slot >= 0) & (slot < count))
+                def _():
+                    started[0] += 1
+                    pltpu.make_async_copy(source.at[at], out.at[dev, slot], sem).start()
+
+    for half in range(2):
+
+        @pl.when(core == half)
         def _():
-            pltpu.make_async_copy(own.at[at, 2 * core + part], out.at[dev, rank - low], sem).start()
-
-        @pl.when(take & (core != half))
+            place(half, own)
+
+        @pl.when(core != half)
         def _():
-            pltpu.make_async_copy(mate.at[at], out.at[dev, rank - low], sem).start()
-
-        return started + take.astype(jnp.int32)
-
-    started = lax.fori_loop(0, slots, functools.partial(place, half=0), 0)
-    started = lax.fori_loop(0, slots, functools.partial(place, half=1), started)
-
-    @pl.loop(0, started)
+            place(half, mate)
+
+    @pl.loop(0, started[0])
     def _(_):
-        pltpu.make_async_copy(mate.at[0], out.at[0, 0], sem).wait()
-
-
-def pack(part, low, count, wide_count, packed, core, own, mate):
+        pltpu.make_async_copy(own.at[0], out.at[0, 0], sem).wait()
+
+
+def pack(low, count, wide_count, packed, core, own, mate):
     return pl.pallas_call(
-        functools.partial(pack_kernel, part, low, count),
-        out_shape=jax.ShapeDtypeStruct((wide_count, count, ROWS, LANES), jnp.bfloat16),
+        functools.partial(pack_kernel, low, count),
+        out_shape=jax.ShapeDtypeStruct((wide_count, count, 2 * ROWS, LANES), jnp.bfloat16),
         in_specs=[SMEM, SMEM, ANY, ANY],
         out_specs=ANY,
-        scratch_shapes=[pltpu.SMEM((wide_count,), jnp.int32), pltpu.SemaphoreType.DMA],
-        cost_estimate=pl.CostEstimate(flops=0, bytes_accessed=wide_count * count * NT * 4, transcendentals=0),
+        scratch_shapes=[
+            pltpu.SMEM((wide_count,), jnp.int32),
+            pltpu.SMEM((1,), jnp.int32),
+            pltpu.SemaphoreType.DMA,
+        ],
+        cost_estimate=pl.CostEstimate(flops=0, bytes_accessed=wide_count * count * NT * 8, transcendentals=0),
         name="pack",
     )(packed, core, own, mate)
 
@@ -108,65 +120,64 @@
     part, source, length, picks, got, more, first, twist, second, white, payload, held, spectra, sem
 ):
     stations = held.shape[0]
+    first_more = got.shape[0] * BASE
 
     @pl.loop(0, stations)
     def _(station):
         code = source[station]
-        over = code - 16 * BASE
-        for core in range(2):
-
-            @pl.when(over < 0)
-            def _():
-                pltpu.make_async_copy(
-                    got.at[2 * (code // BASE) + core, code % BASE], held.at[station, core], sem
-                ).start()
-
-            @pl.when(over >= 0)
-            def _():
-                pltpu.make_async_copy(
-                    more.at[2 * (over // EXTRA) + core, over % EXTRA], held.at[station, core], sem
-                ).start()
-
-    @pl.loop(0, 2 * stations)
+        over = code - first_more
+
+        @pl.when(over < 0)
+        def _():
+            pltpu.make_async_copy(got.at[code >> 1, code & 1], held.at[station], sem).start()
+
+        @pl.when(over >= 0)
+        def _():
+            pltpu.make_async_copy(more.at[over, 0], held.at[station], sem).start()
+
+    @pl.loop(0, stations)
     def _(_):
-        pltpu.make_async_copy(got.at[0, 0], held.at[0, 0], sem).wait()
-
-    row = lax.broadcasted_iota(jnp.int32, (ROWS, LANES), 0)
-    place = row * LANES + lax.broadcasted_iota(jnp.int32, (ROWS, LANES), 1)
-
-    def one_station(station):
+        pltpu.make_async_copy(got.at[0, 0], held.at[0], sem).wait()
+
+    row = lax.broadcasted_iota(jnp.int32, (2 * ROWS, LANES), 0)
+    lane = lax.broadcasted_iota(jnp.int32, (2 * ROWS, LANES), 1)
+    place = (2 * part + (row & 1)) * NT + (row >> 1) * LANES + lane
+
+    def two_stations(station):
         sides = []
-        for core in range(2):
-            bound = length[station] - (2 * core + part) * NT
-            values = held[station, core].astype(jnp.float32)
-            sides.append(jnp.where(place < bound, values, 0.0).astype(jnp.bfloat16))
+        for at in range(2):
+            values = held[station + at].astype(jnp.float32)
+            sides.append(jnp.where(place < length[station + at], values, 0.0).astype(jnp.bfloat16))
         values = jnp.concatenate(sides, 1)
         values = jnp.concatenate([values, values], 0)
         mixed = jnp.dot(first[...], values, preferred_element_type=jnp.float32)
         parts = []
-        for core in range(2):
-            real = mixed[:ROWS, core * LANES : (core + 1) * LANES]
-            imag = mixed[ROWS:, core * LANES : (core + 1) * LANES]
-            turned_re = real * twist[0] + imag * twist[1]
-            turned_im = imag * twist[0] - real * twist[1]
-            parts.append(jnp.concatenate([turned_re, turned_im], 1))
+        for at in range(2):
+            for seg in range(2):
+                real = mixed[2 * seg * ROWS : (2 * seg + 1) * ROWS, at * LANES : (at + 1) * LANES]
+                imag = mixed[(2 * seg + 1) * ROWS : (2 * seg + 2) * ROWS, at * LANES : (at + 1) * LANES]
+                turned_re = real * twist[0] + imag * twist[1]
+                turned_im = imag * twist[0] - real * twist[1]
+                parts.append(jnp.concatenate([turned_re, turned_im], 1))
         turned = jnp.concatenate(parts, 0)
         high = turned.astype(jnp.bfloat16)
         low = (turned - high.astype(jnp.float32)).astype(jnp.bfloat16)
         upper = jnp.dot(high, second[...], preferred_element_type=jnp.float32)
         lower = jnp.dot(low, second[:, :LANES], preferred_element_type=jnp.float32)
         spectrum = upper[:, :LANES] + (upper[:, LANES:] + lower)
-        for core in range(2):
-            side = spectrum[core * ROWS : (core + 1) * ROWS]
-            power = jnp.sum(side * side, axis=0, keepdims=True)
-            power = (power + pltpu.roll(power, LANES // 2, 1)) * (1.0 / ROWS)
-            scale = 1.0 / jnp.sqrt(power + 1e-06)
-            spectra[station, core] = (side * scale).astype(jnp.bfloat16)
-
-    @pl.loop(0, stations // 2)
-    def _(pair):
-        one_station(2 * pair)
-        one_station(2 * pair + 1)
+        for at in range(2):
+            for seg in range(2):
+                begin = (2 * at + seg) * ROWS
+                side = spectrum[begin : begin + ROWS]
+                power = jnp.sum(side * side, axis=0, keepdims=True)
+                power = (power + pltpu.roll(power, LANES // 2, 1)) * (1.0 / ROWS)
+                scale = 1.0 / jnp.sqrt(power + 1e-06)
+                spectra[station + at, seg] = (side * scale).astype(jnp.bfloat16)
+
+    @pl.loop(0, stations // 4)
+    def _(four):
+        two_stations(4 * four)
+        two_stations(4 * four + 2)
 
     whole = pltpu.make_async_copy(spectra, white, sem)
     whole.start()
@@ -178,10 +189,7 @@
             pltpu.make_async_copy(spectra.at[picks[stop, at]], payload.at[stop, at], sem).start()
 
     whole.wait()
-
-    @pl.loop(0, stops * rows)
-    def _(_):
-        pltpu.make_async_copy(spectra.at[0], payload.at[0, 0], sem).wait()
+    pltpu.make_async_copy(payload, payload, sem).wait()
 
 
 def whiten(part, source, length, picks, got, more, tables):
@@ -195,7 +203,7 @@
         in_specs=[SMEM, SMEM, SMEM, ANY, ANY, VMEM, VMEM, VMEM],
         out_specs=(ANY, ANY),
         scratch_shapes=[
-            pltpu.VMEM((ST_DEV, 2, ROWS, LANES), jnp.bfloat16),
+            pltpu.VMEM((ST_DEV, 2 * ROWS, LANES), jnp.bfloat16),
             pltpu.VMEM((ST_DEV, 2, ROWS, LANES), jnp.bfloat16),
             pltpu.SemaphoreType.DMA,
         ],
@@ -240,13 +248,13 @@
         def _(chunk):
             band = pl.ds(pl.multiple_of(chunk * step, step), step)
             here = [
-                [near[s % 2, own[i], s // 2, band, :].astype(jnp.float32) for s in range(SEG)]
+                [near[s // 2, own[i], s % 2, band, :].astype(jnp.float32) for s in range(SEG)]
                 for i in range(side)
             ]
             for j in range(side):
                 straight, crossed = [], []
                 for s in range(SEG):
-                    value = far[s % 2, stop, first + j, s // 2, band, :].astype(jnp.float32)
+                    value = far[s // 2, stop, first + j, s % 2, band, :].astype(jnp.float32)
                     other = pltpu.roll(value, LANES // 2, 1)
                     straight.append(jnp.where(left, value, other))
                     crossed.append(jnp.where(left, -other, value))
@@ -305,6 +313,15 @@
     )(near_pick, far_at, white_a, white_b, home, *far_a, far_b, table, mask)
 
 
+def empty(shape):
+    return pl.pallas_call(
+        lambda out: None,
+        out_shape=jax.ShapeDtypeStruct(shape, jnp.bfloat16),
+        out_specs=ANY,
+        name="empty",
+    )()
+
+
 def on_device(records, lengths, owners, own_pick, visit_pick, pair_mask):
     wide_count = lax.axis_size("wide")
     stops = lax.axis_size("blk")
@@ -313,59 +330,70 @@
     core = column % 2
     swap = [(i, i ^ 1) for i in range(wide_count)]
     slots = records.shape[1]
+    steps = jnp.arange(stops, dtype=jnp.int32)
 
     packed = jnp.where(owners[0] >= 0, (owners[0] << LEN_BITS) + lengths[0], -1)
-    mate_packed = lax.ppermute(packed, "wide", swap)
-    all_packed = lax.all_gather(packed, "wide").reshape(wide_count // 2, 2 * slots)
-    all_visits = lax.all_gather(visit_pick[0, 0].reshape(stops, -1), "blk")
-
-    own = records[0].reshape(slots, SEG, ROWS, LANES)
-    chip_packed = jnp.where(
-        core == 0, jnp.concatenate([packed, mate_packed]), jnp.concatenate([mate_packed, packed])
-    )
-    core_at = core.reshape(1)
-    mates = [
-        lax.ppermute(lax.dynamic_index_in_dim(own, 2 * (1 - core) + part, 1, False), "wide", swap)
+    spread = jnp.broadcast_to(packed[None], (wide_count, slots))
+    table = lax.all_to_all(spread, "wide", split_axis=0, concat_axis=0, tiled=True)
+    table = table.reshape(wide_count // 2, 2, slots)
+    visits = visit_pick[0, 0].reshape(stops, -1)
+    asked = [visits[0]] + [
+        lax.ppermute(visits[stop], "blk", [(i, (i - stop) % stops) for i in range(stops)])
+        for stop in range(1, stops)
+    ]
+    by_stop = jnp.stack(asked)
+    by_dest = by_stop[(steps - group) % stops]
+
+    tiles = records[0].reshape(slots, SEG, ROWS, LANES)
+    own = [
+        tiles[:, 2 * part : 2 * part + 2].transpose(0, 2, 1, 3).reshape(slots, 2 * ROWS, LANES)
         for part in range(2)
     ]
-
-    def deliver(low, count, part):
-        payload = pack(part, low, count, wide_count, chip_packed, core_at, own, mates[part])
+    mates = [lax.ppermute(half, "wide", swap) for half in own]
+    chip_packed = lax.dynamic_index_in_dim(table, column // 2, 0, False)
+    core_at = core.reshape(1)
+
+    def load(low, count, part):
+        return pack(low, count, wide_count, chip_packed, core_at, own[part], mates[part])
+
+    def send(payload):
         return lax.all_to_all(payload, "wide", split_axis=0, concat_axis=0, tiled=True)
 
-    got = [deliver(0, BASE, part) for part in range(2)]
-
-    station = all_packed >> LEN_BITS
+    station = table.reshape(wide_count // 2, 2 * slots) >> LEN_BITS
     owner_dev = station // ST_DEV
     everyone = jnp.arange(wide_count, dtype=jnp.int32)
     counts = jnp.sum((owner_dev[:, :, None] == everyone).astype(jnp.int32), axis=1)
-    spilled = lax.pmax(jnp.max(counts), "blk") > BASE
+    spilled = lax.pmax(jnp.max(counts), "blk") > 2 * BASE
     mine = owner_dev == column
     rank = jnp.cumsum(mine.astype(jnp.int32), axis=1) - 1
     chip = jnp.arange(wide_count // 2, dtype=jnp.int32)[:, None]
-    code = jnp.where(rank < BASE, chip * BASE + rank, 16 * BASE + chip * EXTRA + rank - BASE)
+    sender = 2 * chip + rank % 2
+    code = jnp.where(rank < 2 * BASE, sender * BASE + rank // 2, wide_count * BASE + sender)
     local = column * ST_DEV + jnp.arange(ST_DEV, dtype=jnp.int32)
     chosen = station[None] == local[:, None, None]
     source = jnp.sum(jnp.where(chosen, code[None], 0), axis=(1, 2))
-    length = jnp.sum(jnp.where(chosen, (all_packed & ((1 << LEN_BITS) - 1))[None], 0), axis=(1, 2))
-
+    length = table.reshape(wide_count // 2, 2 * slots) & ((1 << LEN_BITS) - 1)
+    length = jnp.sum(jnp.where(chosen, length[None], 0), axis=(1, 2))
+
+    load_a = load(0, BASE, 0)
+    got_a = send(load_a)
+    load_b = load(0, BASE, 1)
+    spilled, load_b = lax.optimization_barrier((spilled, load_b))
     more = lax.cond(
         spilled,
-        lambda: tuple(deliver(BASE, EXTRA, part) for part in range(2)),
-        lambda: tuple(jnp.zeros((wide_count, EXTRA, ROWS, LANES), jnp.bfloat16) for _ in range(2)),
+        lambda: tuple(send(load(BASE, EXTRA, part)) for part in range(2)),
+        lambda: tuple(empty((wide_count, EXTRA, 2 * ROWS, LANES)) for _ in range(2)),
     )
-
-    steps = jnp.arange(stops, dtype=jnp.int32)
-    by_stop = all_visits[(group + steps) % stops, steps]
-    by_dest = all_visits[steps, (steps - group) % stops]
+    got_a, load_b = lax.optimization_barrier((got_a, load_b))
+    got_b = send(load_b)
+
     tables = [jnp.asarray(table) for table in transform_tables()]
-
-    white_a, payload_a = whiten(0, source, length, by_stop, got[0], more[0], tables)
+    white_a, payload_a = whiten(0, source, length, by_stop, got_a, more[0], tables)
     far_a = [
         lax.ppermute(payload_a[stop], "blk", [(i, (i + stop) % stops) for i in range(stops)])
         for stop in range(1, stops)
     ]
-    white_b, payload_b = whiten(1, source, length, by_dest, got[1], more[1], tables)
+    white_b, payload_b = whiten(1, source, length, by_dest, got_b, more[1], tables)
     far_b = lax.all_to_all(payload_b, "blk", split_axis=0, concat_axis=0, tiled=True)
 
     near_pick = own_pick[0, 0].reshape(stops, -1)

time: 313 us -> 356 us (1.14)
  starting transfers between devices: 56.6 us -> 116 us
  blocking collectives: 75.6 us -> 111 us
  waiting for transfers between devices: 60.7 us -> 32.1 us
  Pallas kernels: 79.7 us -> 64.5 us
  local copies, waits for them, and re-layouts: 33.2 us -> 27.4 us
    all_to_all x0 -> x1, blocking collectives: none -> 99.9 us  [send(): lax.all_to_all(payload, 'wide', split_axis=0, concat_axis=0, tiled=True)]
    all_gather x2 -> x0, blocking collectives: 64.5 us -> none  [the longest x1 35.6 us: on_device(): lax.all_gather(packed, 'wide').reshape(wide_count // 2, 2 * slots)]
    ppermute x3 -> x9, starting transfers between devices: 3.45 us -> 51 us  [the longest x7 47.8 us: on_device(): lax.ppermute(visits[stop], 'blk', [(i, (i - stop) % stops) for i in range...]
    all_to_all x2, waiting for transfers between devices: 38.7 us -> 7.75 us  [the longest x1 7.74 us: on_device(): lax.all_to_all(spread, 'wide', split_axis=0, concat_axis=0, tiled=True)]
    all_to_all x1, starting transfers between devices: 5.2 us -> 32.2 us  [on_device(): lax.all_to_all(payload_b, 'blk', split_axis=0, concat_axis=0, tiled=True)]
    all_to_all x2, starting transfers between devices: 31 us -> 14.5 us  [the longest x1 8.4 us: on_device(): lax.all_to_all(spread, 'wide', split_axis=0, concat_axis=0, tiled=True)]
    another operation x5 -> x2, local copies, waits for them, and re-layouts: 12.1 us -> 0.03 us  [the longest x1 0.03 us: on_device(): by_stop = jnp.stack(asked)]
    slice x1 -> x4, local copies, waits for them, and re-layouts: 0.18 us -> 11.4 us  [the longest x1 10.7 us: on_device(): tiles[:, 2 * part:2 * part + 2].transpose(0, 2, 1, 3)]
  transfers between devices with their start and end apart: 13 -> 19, of which waited for: 5 -> 6; matrix products, arithmetic and copies ran while one was open for 3% -> 3% of each run, Pallas kernels for 12% -> 8%
where the time goes in v2:
time: 356 us; the launch traced here: 355 us
  starting transfers between devices  116 us (33%)
  blocking collectives  111 us (31%)
  Pallas kernels  64.5 us (18%)
  waiting for transfers between devices  32.1 us (9%)
  local copies, waits for them, and re-layouts  27.4 us (8%)
    all_to_all x1, blocking collectives, send(): lax.all_to_all(payload, 'wide', split_axis=0, concat_axis=0, tiled=True)  99.9 us
    ppermute x7, starting transfers between devices, on_device(): lax.ppermute(visits[stop], 'blk', [(i, (i - stop) % stops) for i in range...  47.8 us
    all_to_all x1, starting transfers between devices, on_device(): lax.all_to_all(payload_b, 'blk', split_axis=0, concat_axis=0, tiled=True)  32.2 us
    pallas_call x1, Pallas kernels, lagged(): pl.pallas_call(functools.partial(lag_kernel, stops), out_shape=jax.ShapeD...  25.1 us
    pallas_call x2, Pallas kernels, pack(): pl.pallas_call(functools.partial(pack_kernel, low, count), out_shape=jax....  22.8 us
    ppermute x7, waiting for transfers between devices, on_device(): lax.ppermute(payload_a[stop], 'blk', [(i, (i + stop) % stops) for i in ra...  18.6 us
    ppermute x7, starting transfers between devices, on_device(): lax.ppermute(payload_a[stop], 'blk', [(i, (i + stop) % stops) for i in ra...  18 us
    pallas_call x2, Pallas kernels, whiten(): pl.pallas_call(functools.partial(whiten_kernel, part), out_shape=(jax.Sha...  16.6 us
  transfers between devices with their start and end apart: 19, of which 6 were waited for; matrix products, arithmetic and copies ran while one was open for 3% of the time, Pallas kernels for 8%

profile of v2, /device:TPU:1, one launch (start us, length us, event | category | flops | bytes accessed | tf_op | source)
XLA Modules:
  0.0 355.2 jit_solution(5975510679274574247)
XLA Ops:
  0.0 10.7 %fusion.14 = (bf16[72,2,64,128]{3,1,2,0:T(2,128)(2,1)}, bf16[72,2,64,128]{3,1,2,0:T(2,128)(2,1)S(1)}) fusion(bf16[72,4,64,128]{3,1,2,0:T(4,128)(2,1)} %bitcast.50), kind=kLoop, calls=%fused_computation.64 | loop fusion | bytes 9437184 | tf_op jit(solution)/shard_map/slice | solution.py:349
  10.7 3.2 collective-permute-start.8
  14.6 8.4 %all-to-all-start.2 = ((s32[32,1,72]{2,1,0:T(1,128)}), s32[32,1,72]{2,1,0:T(1,128)S(1)}, u32[]{:S(2)}, u32[]{:S(2)}) async-start(s32[32,1,72]{2,1,0:T(1,128)} %broadcast_in_dim.37), calls=%async_computation.2 | async-start | bytes 32768 | tf_op jit(solution)/shard_map/all_to_all | solution.py:337
  23.0 7.7 %all-to-all-done.2 = s32[32,1,72]{2,1,0:T(1,128)S(1)} async-done(((s32[32,1,72]{2,1,0:T(1,128)}), s32[32,1,72]{2,1,0:T(1,128)S(1)}, u32[]{:S(2)}, u32[]{:S(2)}) %all-to-all-start.2) | async-done | bytes 9248 | tf_op jit(solution)/shard_map/all_to_all | solution.py:337
  31.9 11.1 %pmax.7 = s32[]{:T(128)} all-reduce(s32[]{:T(128)} %reduce_max.9), channel_id=1, replica_groups=mesh['wide'=32,'blk'=8] {'blk'}, use_global_device_ids=true, to_apply=%region_6.7 | all-reduce | flops 1 | bytes 8 | tf_op jit(solution)/shard_map/pmax | solution.py:366
  43.7 19.3 %pack.7 = bf16[32,2,128,128]{3,2,1,0:T(8,128)(2,1)} custom-call(s32[2,72]{1,0:T(2,128)S(1)} %dynamic-slice_bitcast_fusion.packed, s32[1]{0:T(128)} %bitcast.11.core_ref, bf16[72,128,128]{2,1,0:T(8,128)(2,1)} %bitcast.17.own, bf16[72,128,128]{2,1,0:T(8,128)(2,1)} %collective-permute-done.8.mate), custom_call_target="tpu_custom_call" | custom-call | bytes 4194304 | tf_op jit(solution)/shard_map/pack/pallas_call | solution.py:104
  63.1 3.5 pack.6
  66.6 99.9 %all_to_all.30.got = bf16[32,2,128,128]{3,2,1,0:T(8,128)(2,1)} all-to-all(bf16[32,2,128,128]{3,2,1,0:T(8,128)(2,1)} %pack.6), channel_id=1, replica_groups=mesh['wide'=32,'blk'=8] {'wide'}, dimensions={0} | all-to-all | bytes 4194304 | tf_op jit(solution)/shard_map/all_to_all | solution.py:360
  166.5 6.1 %all-to-all-start.4 = ((bf16[32,2,128,128]{3,2,1,0:T(8,128)(2,1)}), bf16[32,2,128,128]{3,2,1,0:T(8,128)(2,1)S(1)}, u32[]{:S(2)}, u32[]{:S(2)}) async-start(bf16[32,2,128,128]{3,2,1,0:T(8,128)(2,1)} %pack.7), calls=%async_computation.4 | async-start | bytes 4194304 | tf_op jit(solution)/shard_map/all_to_all | solution.py:360
  173.3 25.2 %collective-permute-start.1 = (s32[8]{0:T(128)S(1)}, s32[8]{0:T(128)S(1)}, u32[]{:S(2)}, u32[]{:S(2)}) collective-permute-start(s32[8]{0:T(128)S(1)} %squeeze.51), channel_id=1, source_target_pairs={{0,6},{1,7},{2,0},{3,1},{4,2},{5,3},{6,4},{7,5},{8,14},{9,15},{10,... | collective-permute-start | bytes 104 | tf_op jit(solution)/shard_map/ppermute | solution.py:341
  198.6 8.6 %collective-permute-start.2 = (s32[8]{0:T(128)S(1)}, s32[8]{0:T(128)S(1)}, u32[]{:S(2)}, u32[]{:S(2)}) collective-permute-start(s32[8]{0:T(128)S(1)} %squeeze.52), channel_id=1, source_target_pairs={{0,5},{1,6},{2,7},{3,0},{4,1},{5,2},{6,3},{7,4},{8,13},{9,14},{10,... | collective-permute-start | bytes 104 | tf_op jit(solution)/shard_map/ppermute | solution.py:341
  207.3 10.6 %collective-permute-start.3 = (s32[8]{0:T(128)S(1)}, s32[8]{0:T(128)S(1)}, u32[]{:S(2)}, u32[]{:S(2)}) collective-permute-start(s32[8]{0:T(128)S(1)} %squeeze.53), channel_id=1, source_target_pairs={{0,4},{1,5},{2,6},{3,7},{4,0},{5,1},{6,2},{7,3},{8,12},{9,13},{10,... | collective-permute-start | bytes 104 | tf_op jit(solution)/shard_map/ppermute | solution.py:341
  218.0 2.7 collective-permute-start.4
  221.6 1.3 collective-permute-done.4
  222.9 4.4 %collective-permute-done.5 = s32[8]{0:T(128)S(1)} collective-permute-done((s32[8]{0:T(128)S(1)}, s32[8]{0:T(128)S(1)}, u32[]{:S(2)}, u32[]{:S(2)}) %collective-permute-start.5) | collective-permute-done | bytes 64 | tf_op jit(solution)/shard_map/ppermute | solution.py:341
  229.5 1.6 fusion.1
  231.1 1.4 copy-done.10
  232.4 8.4 %whiten.3 = (bf16[24,2,64,128]{3,2,1,0:T(8,128)(2,1)}, bf16[8,8,2,64,128]{4,3,2,1,0:T(8,128)(2,1)}) custom-call(s32[24]{0:T(128)} %get-tuple-element.44.source, s32[24]{0:T(128)} %get-tuple-element.43.length, s32[8,8]{1,0:T(8,128)} %gather_fusion, bf16[32,2,128,128]{3,2,1,0:T(8,128)(2,1)} %copy-done.10, ...), custom_call_target="tpu_custom_call" | custom-call | flops 629145600 | bytes 4194304 | tf_op jit(solution)/shard_map/whiten/pallas_call | solution.py:197
  240.8 32.2 %all-to-all-start.5 = ((bf16[8,8,2,64,128]{4,3,2,1,0:T(8,128)(2,1)}), bf16[8,8,2,64,128]{4,3,2,1,0:T(8,128)(2,1)}, u32[]{:S(2)}, u32[]{:S(2)}) async-start(bf16[8,8,2,64,128]{4,3,2,1,0:T(8,128)(2,1)} %get-tuple-element.42), calls=%async_computation.5 | async-start | bytes 4194304 | tf_op jit(solution)/shard_map/all_to_all | solution.py:397
  273.0 8.3 %whiten.2 = (bf16[24,2,64,128]{3,2,1,0:T(8,128)(2,1)}, bf16[8,8,2,64,128]{4,3,2,1,0:T(8,128)(2,1)}) custom-call(s32[24]{0:T(128)} %get-tuple-element.44.source, s32[24]{0:T(128)} %get-tuple-element.43.length, s32[8,8]{1,0:T(8,128)} %copy-done.11, bf16[32,2,128,128]{3,2,1,0:T(8,128)(2,1)} %all_to_all.30.got, ...), custom_call_target="tpu_custom_call" | custom-call | flops 629145600 | bytes 4194304 | tf_op jit(solution)/shard_map/whiten/pallas_call | solution.py:197
  281.3 2.6 slice_bitcast_fusion
  284.0 3.0 collective-permute-start.10
  286.9 3.3 collective-permute-start.11
  290.2 1.9 collective-permute-start.12
  292.1 1.4 collective-permute-start.13
  293.5 2.7 collective-permute-start.14
  296.2 10.8 %collective-permute-done.10.refs_4_ = bf16[8,2,64,128]{3,2,1,0:T(8,128)(2,1)S(1)} collective-permute-done((bf16[8,2,64,128]{3,2,1,0:T(8,128)(2,1)S(1)}, bf16[8,2,64,128]{3,2,1,0:T(8,128)(2,1)S(1)}, u32[]{:S(2)}, u32[]{:S(2)}) %collective-permute-start.10) | collective-permute-done | bytes 262176 | tf_op jit(solution)/shard_map/ppermute | solution.py:393
  307.6 4.2 %collective-permute-done.11.refs_5_ = bf16[8,2,64,128]{3,2,1,0:T(8,128)(2,1)S(1)} collective-permute-done((bf16[8,2,64,128]{3,2,1,0:T(8,128)(2,1)S(1)}, bf16[8,2,64,128]{3,2,1,0:T(8,128)(2,1)S(1)}, u32[]{:S(2)}, u32[]{:S(2)}) %collective-permute-start.11) | collective-permute-done | bytes 262176 | tf_op jit(solution)/shard_map/ppermute | solution.py:393
  311.8 5.1 %collective-permute-start.9 = (bf16[8,2,64,128]{3,2,1,0:T(8,128)(2,1)}, bf16[8,2,64,128]{3,2,1,0:T(8,128)(2,1)S(1)}, u32[]{:S(2)}, u32[]{:S(2)}) collective-permute-start(bf16[8,2,64,128]{3,2,1,0:T(8,128)(2,1)} %get-tuple-element.65), channel_id=1, source_target_pairs={{0,1},{1,2},{2,3},{3,4},{4,5},{5,6},{6,7},{7,0},{8,9},{9,10},{10,1... | collective-permute-start | bytes 786440 | tf_op jit(solution)/shard_map/ppermute | solution.py:393
  320.0 3.6 %collective-permute-done.15.refs_9_ = bf16[8,2,64,128]{3,2,1,0:T(8,128)(2,1)S(1)} collective-permute-done((bf16[8,2,64,128]{3,2,1,0:T(8,128)(2,1)}, bf16[8,2,64,128]{3,2,1,0:T(8,128)(2,1)S(1)}, u32[]{:S(2)}, u32[]{:S(2)}) %collective-permute-start.15) | collective-permute-done | bytes 262176 | tf_op jit(solution)/shard_map/ppermute | solution.py:393
  328.8 25.1 %lagged.1 = f32[256,1024]{1,0:T(8,128)S(1)} custom-call(s32[8,8]{1,0:T(8,128)S(1)} %copy.34.near_pick, s32[8]{0:T(128)S(1)} %and_select_fusion.1.far_at, bf16[24,2,64,128]{3,2,1,0:T(8,128)(2,1)S(1)} %copy-done.1, bf16[24,2,64,128]{3,2,1,0:T(8,128)(2,1)S(1)} %copy-done, bf16[8,8,2,64,128]{4,3,2,1,0:T(8,128)(2,1)} %get-tuple-element.41.refs_2_, ...), custom_call_target="tpu_custom_call" | custom-call | flops 4294967296 | bytes 25165824 | tf_op jit(solution)/shard_map/lagged/pallas_call | solution.py:295
  353.9 1.3 reshape.156
  (90 shorter events, 14.8 us)
Async XLA Ops:
  0.0 14.0 %copy-start.15 = (s32[1,72]{1,0:T(1,128)S(1)}, s32[1,72]{1,0:T(1,128)}, u32[]{:S(2)}) copy-start(s32[1,72]{1,0:T(1,128)} %param.14) | copy-start | bytes 868
  0.0 14.0 %copy-start.16 = (s32[1,72]{1,0:T(1,128)S(1)}, s32[1,72]{1,0:T(1,128)}, u32[]{:S(2)}) copy-start(s32[1,72]{1,0:T(1,128)} %param.13) | copy-start | bytes 868
  10.7 33.0 %collective-permute-start.8 = (bf16[72,128,128]{2,1,0:T(8,128)(2,1)}, bf16[72,128,128]{2,1,0:T(8,128)(2,1)}, u32[]{:S(2)}, u32[]{:S(2)}) collective-permute-start(bf16[72,128,128]{2,1,0:T(8,128)(2,1)} %bitcast.17.own), channel_id=1, source_target_pairs={{0,8},{8,0},{16,24},{24,16},{32,40},{40,32},{48,56},{56,48},{64,72... | collective-permute-start | bytes 7077896 | tf_op jit(solution)/shard_map/ppermute | solution.py:352
  14.0 49.1 %collective-permute-start.7 = (bf16[72,128,128]{2,1,0:T(8,128)(2,1)S(1)}, bf16[72,128,128]{2,1,0:T(8,128)(2,1)}, u32[]{:S(2)}, u32[]{:S(2)}) collective-permute-start(bf16[72,128,128]{2,1,0:T(8,128)(2,1)S(1)} %bitcast.47), channel_id=1, source_target_pairs={{0,8},{8,0},{16,24},{24,16},{32,40},{40,32},{48,56},{56,48},{64,72... | collective-permute-start | bytes 7077896 | tf_op jit(solution)/shard_map/ppermute | solution.py:352
  14.6 16.2 %all-to-all-start.2 = ((s32[32,1,72]{2,1,0:T(1,128)}), s32[32,1,72]{2,1,0:T(1,128)S(1)}, u32[]{:S(2)}, u32[]{:S(2)}) async-start(s32[32,1,72]{2,1,0:T(1,128)} %broadcast_in_dim.37), calls=%async_computation.2 | async-start | bytes 32768 | tf_op jit(solution)/shard_map/all_to_all | solution.py:337
  166.5 6.1 %copy-start.12 = (s32[1,1,8,2,4]{2,4,3,1,0:T(4,128)S(1)}, s32[1,1,8,2,4]{2,4,3,1,0:T(4,128)}, u32[]{:S(2)}) copy-start(s32[1,1,8,2,4]{2,4,3,1,0:T(4,128)} %param.16) | copy-start | bytes 772
  166.5 64.6 %all-to-all-start.4 = ((bf16[32,2,128,128]{3,2,1,0:T(8,128)(2,1)}), bf16[32,2,128,128]{3,2,1,0:T(8,128)(2,1)S(1)}, u32[]{:S(2)}, u32[]{:S(2)}) async-start(bf16[32,2,128,128]{3,2,1,0:T(8,128)(2,1)} %pack.7), calls=%async_computation.4 | async-start | bytes 4194304 | tf_op jit(solution)/shard_map/all_to_all | solution.py:360
  173.2 47.7 %collective-permute-start = (s32[8]{0:T(128)S(1)}, s32[8]{0:T(128)S(1)}, u32[]{:S(2)}, u32[]{:S(2)}) collective-permute-start(s32[8]{0:T(128)S(1)} %squeeze.50), channel_id=1, source_target_pairs={{0,7},{1,0},{2,1},{3,2},{4,3},{5,4},{6,5},{7,6},{8,15},{9,8},{10,9... | collective-permute-start | bytes 104 | tf_op jit(solution)/shard_map/ppermute | solution.py:341
  173.3 47.7 %collective-permute-start.1 = (s32[8]{0:T(128)S(1)}, s32[8]{0:T(128)S(1)}, u32[]{:S(2)}, u32[]{:S(2)}) collective-permute-start(s32[8]{0:T(128)S(1)} %squeeze.51), channel_id=1, source_target_pairs={{0,6},{1,7},{2,0},{3,1},{4,2},{5,3},{6,4},{7,5},{8,14},{9,15},{10,... | collective-permute-start | bytes 104 | tf_op jit(solution)/shard_map/ppermute | solution.py:341
  198.6 23.0 %collective-permute-start.2 = (s32[8]{0:T(128)S(1)}, s32[8]{0:T(128)S(1)}, u32[]{:S(2)}, u32[]{:S(2)}) collective-permute-start(s32[8]{0:T(128)S(1)} %squeeze.52), channel_id=1, source_target_pairs={{0,5},{1,6},{2,7},{3,0},{4,1},{5,2},{6,3},{7,4},{8,13},{9,14},{10,... | collective-permute-start | bytes 104 | tf_op jit(solution)/shard_map/ppermute | solution.py:341
  207.3 14.3 %collective-permute-start.3 = (s32[8]{0:T(128)S(1)}, s32[8]{0:T(128)S(1)}, u32[]{:S(2)}, u32[]{:S(2)}) collective-permute-start(s32[8]{0:T(128)S(1)} %squeeze.53), channel_id=1, source_target_pairs={{0,4},{1,5},{2,6},{3,7},{4,0},{5,1},{6,2},{7,3},{8,12},{9,13},{10,... | collective-permute-start | bytes 104 | tf_op jit(solution)/shard_map/ppermute | solution.py:341
  218.0 4.9 %collective-permute-start.4 = (s32[8]{0:T(128)S(1)}, s32[8]{0:T(128)S(1)}, u32[]{:S(2)}, u32[]{:S(2)}) collective-permute-start(s32[8]{0:T(128)S(1)} %squeeze.54), channel_id=1, source_target_pairs={{0,3},{1,4},{2,5},{3,6},{4,7},{5,0},{6,1},{7,2},{8,11},{9,12},{10,... | collective-permute-start | bytes 104 | tf_op jit(solution)/shard_map/ppermute | solution.py:341
  220.9 6.4 %collective-permute-start.5 = (s32[8]{0:T(128)S(1)}, s32[8]{0:T(128)S(1)}, u32[]{:S(2)}, u32[]{:S(2)}) collective-permute-start(s32[8]{0:T(128)S(1)} %squeeze.55), channel_id=1, source_target_pairs={{0,2},{1,3},{2,4},{3,5},{4,6},{5,7},{6,0},{7,1},{8,10},{9,11},{10,... | collective-permute-start | bytes 104 | tf_op jit(solution)/shard_map/ppermute | solution.py:341
  221.0 6.3 %collective-permute-start.6 = (s32[8]{0:T(128)S(1)}, s32[8]{0:T(128)S(1)}, u32[]{:S(2)}, u32[]{:S(2)}) collective-permute-start(s32[8]{0:T(128)S(1)} %squeeze.56), channel_id=1, source_target_pairs={{0,1},{1,2},{2,3},{3,4},{4,5},{5,6},{6,7},{7,0},{8,9},{9,10},{10,1... | collective-permute-start | bytes 104 | tf_op jit(solution)/shard_map/ppermute | solution.py:341
  227.3 13.5 %copy-start.11 = (s32[8,8]{1,0:T(8,128)}, s32[8,8]{1,0:T(8,128)S(1)}, u32[]{:S(2)}) copy-start(s32[8,8]{1,0:T(8,128)S(1)} %stack.31.picks) | copy-start | bytes 772
  231.1 1.4 copy-start.10
  240.8 84.2 %all-to-all-start.5 = ((bf16[8,8,2,64,128]{4,3,2,1,0:T(8,128)(2,1)}), bf16[8,8,2,64,128]{4,3,2,1,0:T(8,128)(2,1)}, u32[]{:S(2)}, u32[]{:S(2)}) async-start(bf16[8,8,2,64,128]{4,3,2,1,0:T(8,128)(2,1)} %get-tuple-element.42), calls=%async_computation.5 | async-start | bytes 4194304 | tf_op jit(solution)/shard_map/all_to_all | solution.py:397
  281.3 35.6 %copy-start.13 = (s32[1,1,8,2,4,4]{2,5,4,3,1,0:T(4,128)S(1)}, s32[1,1,8,2,4,4]{2,5,4,3,1,0:T(4,128)}, u32[]{:S(2)}) copy-start(s32[1,1,8,2,4,4]{2,5,4,3,1,0:T(4,128)} %param.17) | copy-start | bytes 3076
  281.3 37.2 %copy-start.14 = (s32[1,1,8,2,4]{2,4,3,1,0:T(4,128)S(1)}, s32[1,1,8,2,4]{2,4,3,1,0:T(4,128)}, u32[]{:S(2)}) copy-start(s32[1,1,8,2,4]{2,4,3,1,0:T(4,128)} %param.15) | copy-start | bytes 772
  281.3 43.7 %copy-start = (bf16[24,2,64,128]{3,2,1,0:T(8,128)(2,1)S(1)}, bf16[24,2,64,128]{3,2,1,0:T(8,128)(2,1)}, u32[]{:S(2)}) copy-start(bf16[24,2,64,128]{3,2,1,0:T(8,128)(2,1)} %get-tuple-element.40.refs_1_) | copy-start | bytes 2359300
  281.3 43.7 %copy-start.1 = (bf16[24,2,64,128]{3,2,1,0:T(8,128)(2,1)S(1)}, bf16[24,2,64,128]{3,2,1,0:T(8,128)(2,1)}, u32[]{:S(2)}) copy-start(bf16[24,2,64,128]{3,2,1,0:T(8,128)(2,1)} %get-tuple-element.37.refs_0_) | copy-start | bytes 2359300
  284.0 23.0 %collective-permute-start.10 = (bf16[8,2,64,128]{3,2,1,0:T(8,128)(2,1)S(1)}, bf16[8,2,64,128]{3,2,1,0:T(8,128)(2,1)S(1)}, u32[]{:S(2)}, u32[]{:S(2)}) collective-permute-start(bf16[8,2,64,128]{3,2,1,0:T(8,128)(2,1)S(1)} %get-tuple-element.64), channel_id=1, source_target_pairs={{0,2},{1,3},{2,4},{3,5},{4,6},{5,7},{6,0},{7,1},{8,10},{9,11},{10,... | collective-permute-start | bytes 786440 | tf_op jit(solution)/shard_map/ppermute | solution.py:393
  286.9 24.9 %collective-permute-start.11 = (bf16[8,2,64,128]{3,2,1,0:T(8,128)(2,1)S(1)}, bf16[8,2,64,128]{3,2,1,0:T(8,128)(2,1)S(1)}, u32[]{:S(2)}, u32[]{:S(2)}) collective-permute-start(bf16[8,2,64,128]{3,2,1,0:T(8,128)(2,1)S(1)} %get-tuple-element.63), channel_id=1, source_target_pairs={{0,3},{1,4},{2,5},{3,6},{4,7},{5,0},{6,1},{7,2},{8,11},{9,12},{10,... | collective-permute-start | bytes 786440 | tf_op jit(solution)/shard_map/ppermute | solution.py:393
  290.2 28.4 %collective-permute-start.12 = (bf16[8,2,64,128]{3,2,1,0:T(8,128)(2,1)}, bf16[8,2,64,128]{3,2,1,0:T(8,128)(2,1)S(1)}, u32[]{:S(2)}, u32[]{:S(2)}) collective-permute-start(bf16[8,2,64,128]{3,2,1,0:T(8,128)(2,1)} %get-tuple-element.62), channel_id=1, source_target_pairs={{0,4},{1,5},{2,6},{3,7},{4,0},{5,1},{6,2},{7,3},{8,12},{9,13},{10,... | collective-permute-start | bytes 786440 | tf_op jit(solution)/shard_map/ppermute | solution.py:393
  292.1 26.5 %collective-permute-start.13 = (bf16[8,2,64,128]{3,2,1,0:T(8,128)(2,1)}, bf16[8,2,64,128]{3,2,1,0:T(8,128)(2,1)S(1)}, u32[]{:S(2)}, u32[]{:S(2)}) collective-permute-start(bf16[8,2,64,128]{3,2,1,0:T(8,128)(2,1)} %get-tuple-element.61), channel_id=1, source_target_pairs={{0,5},{1,6},{2,7},{3,0},{4,1},{5,2},{6,3},{7,4},{8,13},{9,14},{10,... | collective-permute-start | bytes 786440 | tf_op jit(solution)/shard_map/ppermute | solution.py:393
  293.5 25.8 %collective-permute-start.14 = (bf16[8,2,64,128]{3,2,1,0:T(8,128)(2,1)}, bf16[8,2,64,128]{3,2,1,0:T(8,128)(2,1)S(1)}, u32[]{:S(2)}, u32[]{:S(2)}) collective-permute-start(bf16[8,2,64,128]{3,2,1,0:T(8,128)(2,1)} %get-tuple-element.60), channel_id=1, source_target_pairs={{0,6},{1,7},{2,0},{3,1},{4,2},{5,3},{6,4},{7,5},{8,14},{9,15},{10,... | collective-permute-start | bytes 786440 | tf_op jit(solution)/shard_map/ppermute | solution.py:393
  306.9 16.7 %collective-permute-start.15 = (bf16[8,2,64,128]{3,2,1,0:T(8,128)(2,1)}, bf16[8,2,64,128]{3,2,1,0:T(8,128)(2,1)S(1)}, u32[]{:S(2)}, u32[]{:S(2)}) collective-permute-start(bf16[8,2,64,128]{3,2,1,0:T(8,128)(2,1)} %get-tuple-element.59), channel_id=1, source_target_pairs={{0,7},{1,0},{2,1},{3,2},{4,3},{5,4},{6,5},{7,6},{8,15},{9,8},{10,9... | collective-permute-start | bytes 786440 | tf_op jit(solution)/shard_map/ppermute | solution.py:393
  311.8 12.5 %collective-permute-start.9 = (bf16[8,2,64,128]{3,2,1,0:T(8,128)(2,1)}, bf16[8,2,64,128]{3,2,1,0:T(8,128)(2,1)S(1)}, u32[]{:S(2)}, u32[]{:S(2)}) collective-permute-start(bf16[8,2,64,128]{3,2,1,0:T(8,128)(2,1)} %get-tuple-element.65), channel_id=1, source_target_pairs={{0,1},{1,2},{2,3},{3,4},{4,5},{5,6},{6,7},{7,0},{8,9},{9,10},{10,1... | collective-permute-start | bytes 786440 | tf_op jit(solution)/shard_map/ppermute | solution.py:393
  325.0 1.0 copy-start.3
  326.0 0.9 copy-start.5
  326.9 0.9 copy-start.7
  327.9 0.9 copy-start.9
  (4 other events, 2.8 us)

commit v3 on v2

--- a/solution.py
+++ b/solution.py
@@ -59,10 +59,11 @@
     return joined.reshape(ROWS * LANES, LAGS).astype(jnp.bfloat16)
 
 
-def pack_kernel(low, count, packed, core_ref, own, mate, out, fill, started, sem):
+def pack_kernel(low, count, packed, core_ref, own, mate, after, out, flag, fill, started, sem):
     core = core_ref[0]
     slots = packed.shape[1]
     started[0] = 0
+    flag[0] = 0
 
     @pl.loop(0, out.shape[0])
     def _(dev):
@@ -85,6 +86,10 @@
                     started[0] += 1
                     pltpu.make_async_copy(source.at[at], out.at[dev, slot], sem).start()
 
+                @pl.when(slot >= count)
+                def _():
+                    flag[0] = 1
+
     for half in range(2):
 
         @pl.when(core == half)
@@ -100,12 +105,15 @@
         pltpu.make_async_copy(own.at[0], out.at[0, 0], sem).wait()
 
 
-def pack(low, count, wide_count, packed, core, own, mate):
+def pack(low, count, wide_count, packed, core, own, mate, after):
     return pl.pallas_call(
         functools.partial(pack_kernel, low, count),
-        out_shape=jax.ShapeDtypeStruct((wide_count, count, 2 * ROWS, LANES), jnp.bfloat16),
-        in_specs=[SMEM, SMEM, ANY, ANY],
-        out_specs=ANY,
+        out_shape=(
+            jax.ShapeDtypeStruct((wide_count, count, 2 * ROWS, LANES), jnp.bfloat16),
+            jax.ShapeDtypeStruct((1,), jnp.int32),
+        ),
+        in_specs=[SMEM, SMEM, ANY, ANY, ANY],
+        out_specs=(VMEM, SMEM),
         scratch_shapes=[
             pltpu.SMEM((wide_count,), jnp.int32),
             pltpu.SMEM((1,), jnp.int32),
@@ -113,12 +121,13 @@
         ],
         cost_estimate=pl.CostEstimate(flops=0, bytes_accessed=wide_count * count * NT * 8, transcendentals=0),
         name="pack",
-    )(packed, core, own, mate)
+    )(packed, core, own, mate, after)
 
 
 def whiten_kernel(
-    part, source, length, picks, got, more, first, twist, second, white, payload, held, spectra, sem
+    part, source, length, picks, got, more, first, twist, second, *refs
 ):
+    white, payload, held, spectra, sem = refs[-5:]
     stations = held.shape[0]
     first_more = got.shape[0] * BASE
 
@@ -192,7 +201,7 @@
     pltpu.make_async_copy(payload, payload, sem).wait()
 
 
-def whiten(part, source, length, picks, got, more, tables):
+def whiten(part, source, length, picks, got, more, tables, after):
     stops, rows = picks.shape
     return pl.pallas_call(
         functools.partial(whiten_kernel, part),
@@ -200,7 +209,7 @@
             jax.ShapeDtypeStruct((ST_DEV, 2, ROWS, LANES), jnp.bfloat16),
             jax.ShapeDtypeStruct((stops, rows, 2, ROWS, LANES), jnp.bfloat16),
         ),
-        in_specs=[SMEM, SMEM, SMEM, ANY, ANY, VMEM, VMEM, VMEM],
+        in_specs=[SMEM, SMEM, SMEM, ANY, ANY, VMEM, VMEM, VMEM] + [ANY] * len(after),
         out_specs=(ANY, ANY),
         scratch_shapes=[
             pltpu.VMEM((ST_DEV, 2 * ROWS, LANES), jnp.bfloat16),
@@ -211,66 +220,97 @@
             flops=2 * ST_DEV * 2 * ROWS * 256 * 400, bytes_accessed=4 * 1024 * 1024, transcendentals=0
         ),
         name="whiten",
-    )(source, length, picks, got, more, *tables)
-
-
-def lag_kernel(stops, near_pick, far_at, *refs):
-    white_a, white_b, home = refs[:3]
-    far_a = refs[3 : 2 + stops]
-    far_b, table, mask, out, near, far, cross, tables, sem, table_sem = refs[2 + stops :]
-    rows = near_pick.shape[1]
+    )(source, length, picks, got, more, *tables, *after)
+
+
+def cross_rows(near_pick, near, far, cross, fresh):
+    stops, rows = near_pick.shape
+    side = rows // 2
+    step = 16
+    left = lax.broadcasted_iota(jnp.int32, (step, LANES), 1) < LANES // 2
+
+    @pl.loop(0, stops * 2)
+    def _(block):
+        stop = block // 2
+        first = (block % 2) * side
+        own = [near_pick[stop, first + i] for i in range(side)]
+
+        @pl.loop(0, ROWS // step)
+        def _(chunk):
+            band = pl.ds(pl.multiple_of(chunk * step, step), step)
+            here = [[near[own[i], s, band, :].astype(jnp.float32) for s in range(2)] for i in range(side)]
+            for j in range(side):
+                straight, crossed = [], []
+                for s in range(2):
+                    value = far[stop, first + j, s, band, :].astype(jnp.float32)
+                    other = pltpu.roll(value, LANES // 2, 1)
+                    straight.append(jnp.where(left, value, other))
+                    crossed.append(jnp.where(left, -other, value))
+                for i in range(side):
+                    direct = here[i][0] * straight[0] + here[i][1] * straight[1]
+                    turned = here[i][0] * crossed[0] + here[i][1] * crossed[1]
+                    total = direct + pltpu.roll(turned, LANES // 2, 1)
+                    pair = (block * side + i) * side + j
+                    at = pl.ds(pl.multiple_of(pair * ROWS + chunk * step, step), step)
+                    if fresh:
+                        cross[at, :] = total
+                    else:
+                        cross[at, :] += total
+
+
+def cross_kernel(stops, near_pick, white, home, *refs):
+    far_in = refs[: stops - 1]
+    out, near, far, cross, sem, out_sem = refs[stops - 1 :]
+    copies = [pltpu.make_async_copy(white, near, sem), pltpu.make_async_copy(home.at[0], far.at[0], sem)]
+    for stop in range(1, stops):
+        copies.append(pltpu.make_async_copy(far_in[stop - 1], far.at[stop], sem))
+    for copy in copies:
+        copy.start()
+    for copy in copies:
+        copy.wait()
+    cross_rows(near_pick, near, far, cross, True)
+    copy = pltpu.make_async_copy(cross, out, out_sem)
+    copy.start()
+    copy.wait()
+
+
+def cross_first(near_pick, white, home, far):
+    stops, rows = near_pick.shape
+    pairs = stops * rows * rows // 2
+    return pl.pallas_call(
+        functools.partial(cross_kernel, stops),
+        out_shape=jax.ShapeDtypeStruct((pairs * ROWS, LANES), jnp.float32),
+        in_specs=[SMEM] + [ANY] * (stops + 1),
+        out_specs=ANY,
+        scratch_shapes=[
+            pltpu.VMEM(white.shape, jnp.bfloat16),
+            pltpu.VMEM(home.shape, jnp.bfloat16),
+            pltpu.VMEM((pairs * ROWS, LANES), jnp.float32),
+            pltpu.SemaphoreType.DMA,
+            pltpu.SemaphoreType.DMA,
+        ],
+        compiler_params=pltpu.CompilerParams(vmem_limit_bytes=20 * 1024 * 1024),
+        cost_estimate=pl.CostEstimate(
+            flops=pairs * ROWS * LANES * 16, bytes_accessed=24 * 1024 * 1024, transcendentals=0
+        ),
+        name="cross_first",
+    )(near_pick, white, home, *far)
+
+
+def lag_kernel(near_pick, far_at, begun, white, far_in, table, mask, out, near, far, cross, tables, sem, table_sem):
+    stops = near_pick.shape[0]
     load_table = pltpu.make_async_copy(table, tables, table_sem)
-    copies = [
-        pltpu.make_async_copy(white_a, near.at[0], sem),
-        pltpu.make_async_copy(white_b, near.at[1], sem),
-        pltpu.make_async_copy(home.at[0], far.at[0, 0], sem),
-    ]
-    for stop in range(1, stops):
-        copies.append(pltpu.make_async_copy(far_a[stop - 1], far.at[0, stop], sem))
+    copies = [pltpu.make_async_copy(white, near, sem), pltpu.make_async_copy(begun, cross, sem)]
     for stop in range(stops):
-        copies.append(pltpu.make_async_copy(far_b.at[far_at[stop]], far.at[1, stop], sem))
+        copies.append(pltpu.make_async_copy(far_in.at[far_at[stop]], far.at[stop], sem))
     for copy in copies:
         copy.start()
     load_table.start()
     for copy in copies:
         copy.wait()
-    step = 16
-    side = rows // 2
-    left = lax.broadcasted_iota(jnp.int32, (step, LANES), 1) < LANES // 2
-
-    @pl.loop(0, stops * 2)
-    def _(block):
-        stop = block // 2
-        first = (block % 2) * side
-        own = [near_pick[stop, first + i] for i in range(side)]
-
-        @pl.loop(0, ROWS // step)
-        def _(chunk):
-            band = pl.ds(pl.multiple_of(chunk * step, step), step)
-            here = [
-                [near[s // 2, own[i], s % 2, band, :].astype(jnp.float32) for s in range(SEG)]
-                for i in range(side)
-            ]
-            for j in range(side):
-                straight, crossed = [], []
-                for s in range(SEG):
-                    value = far[s // 2, stop, first + j, s % 2, band, :].astype(jnp.float32)
-                    other = pltpu.roll(value, LANES // 2, 1)
-                    straight.append(jnp.where(left, value, other))
-                    crossed.append(jnp.where(left, -other, value))
-                for i in range(side):
-                    direct = here[i][0] * straight[0]
-                    turned = here[i][0] * crossed[0]
-                    for s in range(1, SEG):
-                        direct += here[i][s] * straight[s]
-                        turned += here[i][s] * crossed[s]
-                    pair = (block * side + i) * side + j
-                    cross[pl.ds(pl.multiple_of(pair * ROWS + chunk * step, step), step), :] = (
-                        direct + pltpu.roll(turned, LANES // 2, 1)
-                    )
-
+    cross_rows(near_pick, near, far, cross, False)
     load_table.wait()
-    pairs = stops * 2 * side * side
+    pairs = out.shape[0]
     group = 8
     out[...] = jnp.zeros_like(out)
 
@@ -289,17 +329,16 @@
     out[...] = out[...] * mask[...]
 
 
-def lagged(near_pick, far_at, white_a, white_b, home, far_a, far_b, table, mask):
-    stops, rows = near_pick.shape
+def lagged(near_pick, far_at, begun, white, far, table, mask):
     pairs = mask.shape[0]
     return pl.pallas_call(
-        functools.partial(lag_kernel, stops),
+        lag_kernel,
         out_shape=jax.ShapeDtypeStruct((pairs, LAGS), jnp.float32),
-        in_specs=[SMEM, SMEM] + [ANY] * (stops + 4) + [VMEM],
+        in_specs=[SMEM, SMEM] + [ANY] * 4 + [VMEM],
         out_specs=VMEM,
         scratch_shapes=[
-            pltpu.VMEM((2, ST_DEV, 2, ROWS, LANES), jnp.bfloat16),
-            pltpu.VMEM((2, stops, rows, 2, ROWS, LANES), jnp.bfloat16),
+            pltpu.VMEM(white.shape, jnp.bfloat16),
+            pltpu.VMEM(far.shape, jnp.bfloat16),
             pltpu.VMEM((pairs * ROWS, LANES), jnp.float32),
             pltpu.VMEM(table.shape, jnp.bfloat16),
             pltpu.SemaphoreType.DMA,
@@ -310,7 +349,7 @@
             flops=2 * pairs * 2 * NF * LAGS, bytes_accessed=24 * 1024 * 1024, transcendentals=0
         ),
         name="lagged",
-    )(near_pick, far_at, white_a, white_b, home, *far_a, far_b, table, mask)
+    )(near_pick, far_at, begun, white, far, table, mask)
 
 
 def empty(shape):
@@ -336,35 +375,48 @@
     spread = jnp.broadcast_to(packed[None], (wide_count, slots))
     table = lax.all_to_all(spread, "wide", split_axis=0, concat_axis=0, tiled=True)
     table = table.reshape(wide_count // 2, 2, slots)
-    visits = visit_pick[0, 0].reshape(stops, -1)
-    asked = [visits[0]] + [
-        lax.ppermute(visits[stop], "blk", [(i, (i - stop) % stops) for i in range(stops)])
-        for stop in range(1, stops)
-    ]
-    by_stop = jnp.stack(asked)
-    by_dest = by_stop[(steps - group) % stops]
-
-    tiles = records[0].reshape(slots, SEG, ROWS, LANES)
-    own = [
-        tiles[:, 2 * part : 2 * part + 2].transpose(0, 2, 1, 3).reshape(slots, 2 * ROWS, LANES)
-        for part in range(2)
-    ]
-    mates = [lax.ppermute(half, "wide", swap) for half in own]
     chip_packed = lax.dynamic_index_in_dim(table, column // 2, 0, False)
     core_at = core.reshape(1)
 
-    def load(low, count, part):
-        return pack(low, count, wide_count, chip_packed, core_at, own[part], mates[part])
+    tiles = records[0].reshape(slots, SEG, ROWS, LANES)
+
+    def halves(part):
+        return tiles[:, 2 * part : 2 * part + 2].transpose(0, 2, 1, 3).reshape(slots, 2 * ROWS, LANES)
 
     def send(payload):
         return lax.all_to_all(payload, "wide", split_axis=0, concat_axis=0, tiled=True)
 
-    station = table.reshape(wide_count // 2, 2 * slots) >> LEN_BITS
-    owner_dev = station // ST_DEV
-    everyone = jnp.arange(wide_count, dtype=jnp.int32)
-    counts = jnp.sum((owner_dev[:, :, None] == everyone).astype(jnp.int32), axis=1)
-    spilled = lax.pmax(jnp.max(counts), "blk") > 2 * BASE
-    mine = owner_dev == column
+    own_a = halves(0)
+    mate_a = lax.ppermute(own_a, "wide", swap)
+    load_a, flag_a = pack(0, BASE, wide_count, chip_packed, core_at, own_a, mate_a, core_at)
+    got_a = send(load_a)
+    own_b = jnp.where(flag_a[0] >= 0, halves(1), 0.0)
+    mate_b = lax.ppermute(own_b, "wide", swap)
+    load_b, flag_b = pack(0, BASE, wide_count, chip_packed, core_at, own_b, mate_b, load_a)
+    got_b = send(load_b)
+
+    def late():
+        rows = [
+            pack(BASE, EXTRA, wide_count, chip_packed, core_at, own, mate, core_at)[0]
+            for own, mate in ((own_a, mate_a), (own_b, mate_b))
+        ]
+        return tuple(send(row) for row in rows)
+
+    more = lax.cond(
+        lax.pmax(flag_b[0], ("blk", "wide")) > 0,
+        late,
+        lambda: tuple(empty((wide_count, EXTRA, 2 * ROWS, LANES)) for _ in range(2)),
+    )
+
+    visits = visit_pick[0, 0].reshape(stops, -1)[(group - steps) % stops]
+    visits = jnp.where(flag_b[0] >= 0, visits, 0)
+    by_dest = lax.all_to_all(visits, "blk", split_axis=0, concat_axis=0, tiled=True)
+    by_stop = by_dest[(group + steps) % stops]
+
+    flat = table.reshape(wide_count // 2, 2 * slots)
+    flat = jnp.where(flag_a[0] >= 0, flat, 0)
+    station = flat >> LEN_BITS
+    mine = (station // ST_DEV) == column
     rank = jnp.cumsum(mine.astype(jnp.int32), axis=1) - 1
     chip = jnp.arange(wide_count // 2, dtype=jnp.int32)[:, None]
     sender = 2 * chip + rank % 2
@@ -372,34 +424,23 @@
     local = column * ST_DEV + jnp.arange(ST_DEV, dtype=jnp.int32)
     chosen = station[None] == local[:, None, None]
     source = jnp.sum(jnp.where(chosen, code[None], 0), axis=(1, 2))
-    length = table.reshape(wide_count // 2, 2 * slots) & ((1 << LEN_BITS) - 1)
+    length = flat & ((1 << LEN_BITS) - 1)
     length = jnp.sum(jnp.where(chosen, length[None], 0), axis=(1, 2))
 
-    load_a = load(0, BASE, 0)
-    got_a = send(load_a)
-    load_b = load(0, BASE, 1)
-    spilled, load_b = lax.optimization_barrier((spilled, load_b))
-    more = lax.cond(
-        spilled,
-        lambda: tuple(send(load(BASE, EXTRA, part)) for part in range(2)),
-        lambda: tuple(empty((wide_count, EXTRA, 2 * ROWS, LANES)) for _ in range(2)),
-    )
-    got_a, load_b = lax.optimization_barrier((got_a, load_b))
-    got_b = send(load_b)
-
     tables = [jnp.asarray(table) for table in transform_tables()]
-    white_a, payload_a = whiten(0, source, length, by_stop, got_a, more[0], tables)
+    near_pick = own_pick[0, 0].reshape(stops, -1)
+    white_a, payload_a = whiten(0, source, length, by_stop, got_a, more[0], tables, [])
     far_a = [
         lax.ppermute(payload_a[stop], "blk", [(i, (i + stop) % stops) for i in range(stops)])
         for stop in range(1, stops)
     ]
-    white_b, payload_b = whiten(1, source, length, by_dest, got_b, more[1], tables)
+    white_b, payload_b = whiten(1, source, length, by_dest, got_b, more[1], tables, far_a)
     far_b = lax.all_to_all(payload_b, "blk", split_axis=0, concat_axis=0, tiled=True)
 
-    near_pick = own_pick[0, 0].reshape(stops, -1)
+    begun = cross_first(near_pick, white_a, payload_a, far_a)
     far_at = (group - steps) % stops
     mask = pair_mask[0, 0].astype(jnp.float32).reshape(-1, 1)
-    result = lagged(near_pick, far_at, white_a, white_b, payload_a, far_a, far_b, jnp.asarray(lag_table()), mask)
+    result = lagged(near_pick, far_at, begun, white_b, far_b, jnp.asarray(lag_table()), mask)
     return result.reshape((1, 1) + pair_mask.shape[2:] + (LAGS,))
 
 

time: 356 us -> 325 us (0.913)
  starting transfers between devices: 116 us -> 32.9 us
  blocking collectives: 111 us -> 140 us
  waiting for transfers between devices: 32.1 us -> 52.3 us
  other arithmetic: 3.46 us -> 10 us
  local copies, waits for them, and re-layouts: 27.4 us -> 21.7 us
    pmax x1, blocking collectives: 11.1 us -> 75.1 us  [on_device(): lax.pmax(flag_b[0], ('blk', 'wide')) > 0]
    ppermute x9 -> x2, starting transfers between devices: 51 us -> 6.01 us  [the longest x1 3.33 us: on_device(): mate_a = lax.ppermute(own_a, 'wide', swap)]
    all_to_all x1, blocking collectives: 99.9 us -> 55.6 us  [send(): lax.all_to_all(payload, 'wide', split_axis=0, concat_axis=0, tiled=True)]
    all_to_all x1, starting transfers between devices: 32.2 us -> 5.35 us  [on_device(): lax.all_to_all(payload_b, 'blk', split_axis=0, concat_axis=0, tiled=True)]
    ppermute x7, waiting for transfers between devices: 18.6 us -> 34.8 us  [on_device(): lax.ppermute(payload_a[stop], 'blk', [(i, (i + stop) % stops) for i in ra...]
    ppermute x7, starting transfers between devices: 18 us -> 7 us  [on_device(): lax.ppermute(payload_a[stop], 'blk', [(i, (i + stop) % stops) for i in ra...]
    all_to_all x0 -> x1, blocking collectives: none -> 9.34 us  [on_device(): lax.all_to_all(visits, 'blk', split_axis=0, concat_axis=0, tiled=True)]
    select_n x1 -> x4, other arithmetic: 0.01 us -> 7.46 us  [the longest x1 7.43 us: on_device(): own_b = jnp.where(flag_a[0] >= 0, halves(1), 0.0)]
  transfers between devices with their start and end apart: 19 -> 12, of which waited for: 6 -> 6; matrix products, arithmetic and copies ran while one was open for 3% -> 3% of each run, Pallas kernels for 8% -> 7%
where the time goes in v3:
time: 325 us; the launch traced here: 323 us
  blocking collectives  140 us (43%)
  Pallas kernels  63.6 us (20%)
  waiting for transfers between devices  52.3 us (16%)
  starting transfers between devices  32.9 us (10%)
  local copies, waits for them, and re-layouts  21.7 us (7%)
  other arithmetic  10 us (3%)
    pmax x1, blocking collectives, on_device(): lax.pmax(flag_b[0], ('blk', 'wide')) > 0  75.1 us
    all_to_all x1, blocking collectives, send(): lax.all_to_all(payload, 'wide', split_axis=0, concat_axis=0, tiled=True)  55.6 us
    ppermute x7, waiting for transfers between devices, on_device(): lax.ppermute(payload_a[stop], 'blk', [(i, (i + stop) % stops) for i in ra...  34.8 us
    pallas_call x1, Pallas kernels, lagged(): pl.pallas_call(lag_kernel, out_shape=jax.ShapeDtypeStruct((pairs, LAGS),...  24.5 us
    pallas_call x2, Pallas kernels, whiten(): pl.pallas_call(functools.partial(whiten_kernel, part), out_shape=(jax.Sha...  16.7 us
    pallas_call x1, Pallas kernels, cross_first(): pl.pallas_call(functools.partial(cross_kernel, stops), out_shape=jax.Shap...  13 us
    unnamed x48, local copies, waits for them, and re-layouts  9.98 us
    pallas_call x2, Pallas kernels, pack(): pl.pallas_call(functools.partial(pack_kernel, low, count), out_shape=(jax...  9.47 us
  transfers between devices with their start and end apart: 12, of which 6 were waited for; matrix products, arithmetic and copies ran while one was open for 3% of the time, Pallas kernels for 7%

profile of v3, /device:TPU:1, one launch (start us, length us, event | category | flops | bytes accessed | tf_op | source)
XLA Modules:
  0.0 322.9 jit_solution(12966991059388777639)
XLA Ops:
  0.0 4.5 %slice.52 = bf16[72,2,64,128]{3,1,2,0:T(2,128)(2,1)S(1)} slice(bf16[72,4,64,128]{3,1,2,0:T(4,128)(2,1)} %bitcast.52), slice={[0:72], [0:2], [0:64], [0:128]} | slice | bytes 4718592 | tf_op jit(solution)/shard_map/slice | solution.py:384
  4.5 3.3 %collective-permute-start = (bf16[72,128,128]{2,1,0:T(8,128)(2,1)S(1)}, bf16[72,128,128]{2,1,0:T(8,128)(2,1)}, u32[]{:S(2)}, u32[]{:S(2)}) collective-permute-start(bf16[72,128,128]{2,1,0:T(8,128)(2,1)S(1)} %bitcast.49), channel_id=1, source_target_pairs={{0,8},{8,0},{16,24},{24,16},{32,40},{40,32},{48,56},{56,48},{64,72... | collective-permute-start | bytes 7077896 | tf_op jit(solution)/shard_map/ppermute | solution.py:390
  8.5 8.0 %all-to-all-start.2 = ((s32[32,1,72]{2,1,0:T(1,128)}), s32[32,1,72]{2,1,0:T(1,128)S(1)}, u32[]{:S(2)}, u32[]{:S(2)}) async-start(s32[32,1,72]{2,1,0:T(1,128)} %broadcast_in_dim.50), calls=%async_computation.2 | async-start | bytes 32768 | tf_op jit(solution)/shard_map/all_to_all | solution.py:376
  16.5 7.7 %all-to-all-done.2 = s32[32,1,72]{2,1,0:T(1,128)S(1)} async-done(((s32[32,1,72]{2,1,0:T(1,128)}), s32[32,1,72]{2,1,0:T(1,128)S(1)}, u32[]{:S(2)}, u32[]{:S(2)}) %all-to-all-start.2) | async-done | bytes 9248 | tf_op jit(solution)/shard_map/all_to_all | solution.py:376
  24.2 4.5 %pack.6 = (bf16[32,2,128,128]{3,2,1,0:T(8,128)(2,1)}, s32[1]{0:T(128)}) custom-call(s32[2,72]{1,0:T(2,128)S(1)} %dynamic-slice_bitcast_fusion.packed, s32[1]{0:T(128)} %bitcast.4.core_ref.after, bf16[72,128,128]{2,1,0:T(8,128)(2,1)S(1)} %bitcast.50, bf16[72,128,128]{2,1,0:T(8,128)(2,1)} %collective-permute-done.mate, s32[1]{0:T(128)} %bitcast.4.core_ref.after), custom_call_target="tpu_custom_call" | custom-call | bytes 4194304 | tf_op jit(solution)/shard_map/pack/pallas_call | solution.py:109
  29.5 7.4 %broadcast_select_fusion = bf16[72,2,64,128]{3,1,2,0:T(2,128)(2,1)} fusion(pred[]{:T(512)} %bitcast.9, bf16[72,4,64,128]{3,1,2,0:T(4,128)(2,1)} %bitcast.53), kind=kLoop, calls=%fused_computation.2 | loop fusion | flops 1179648 | bytes 4718593 | tf_op jit(solution)/shard_map/jit(_where)/select_n | solution.py:393
  36.9 2.7 collective-permute-start.1
  40.2 3.8 %collective-permute-done.1.mate = bf16[72,128,128]{2,1,0:T(8,128)(2,1)} collective-permute-done((bf16[72,128,128]{2,1,0:T(8,128)(2,1)}, bf16[72,128,128]{2,1,0:T(8,128)(2,1)}, u32[]{:S(2)}, u32[]{:S(2)}) %collective-permute-start.1) | collective-permute-done | bytes 2359328 | tf_op jit(solution)/shard_map/ppermute | solution.py:394
  44.1 4.9 %pack.7 = (bf16[32,2,128,128]{3,2,1,0:T(8,128)(2,1)}, s32[1]{0:T(128)}) custom-call(s32[2,72]{1,0:T(2,128)S(1)} %dynamic-slice_bitcast_fusion.packed, s32[1]{0:T(128)} %bitcast.4.core_ref.after, bf16[72,128,128]{2,1,0:T(8,128)(2,1)} %bitcast.11.own, bf16[72,128,128]{2,1,0:T(8,128)(2,1)} %collective-permute-done.1.mate, ...), custom_call_target="tpu_custom_call" | custom-call | bytes 4194304 | tf_op jit(solution)/shard_map/pack/pallas_call | solution.py:109
  49.7 75.1 %pmax.7 = s32[]{:T(128)} all-reduce(s32[]{:T(128)} %bitcast.13), channel_id=1, replica_groups=mesh['wide'=32,'blk'=8] {'blk','wide'}, use_global_device_ids=true, to_apply=%region_4.5 | all-reduce | flops 1 | bytes 8 | tf_op jit(solution)/shard_map/pmax | solution.py:406
  125.5 9.3 %all_to_all.38 = s32[8,1,8]{2,1,0:T(1,128)S(1)} all-to-all(s32[8,1,8]{2,1,0:T(1,128)S(1)} %bitcast.57), channel_id=1, replica_groups=mesh['wide'=32,'blk'=8] {'blk'}, dimensions={0} | all-to-all | bytes 512 | tf_op jit(solution)/shard_map/all_to_all | solution.py:413
  134.8 55.6 %all_to_all.39.got = bf16[32,2,128,128]{3,2,1,0:T(8,128)(2,1)} all-to-all(bf16[32,2,128,128]{3,2,1,0:T(8,128)(2,1)} %get-tuple-element.36.after), channel_id=1, replica_groups=mesh['wide'=32,'blk'=8] {'wide'}, dimensions={0} | all-to-all | bytes 4194304 | tf_op jit(solution)/shard_map/all_to_all | solution.py:387
  190.4 6.5 %all-to-all-start.5 = ((bf16[32,2,128,128]{3,2,1,0:T(8,128)(2,1)}), bf16[32,2,128,128]{3,2,1,0:T(8,128)(2,1)}, u32[]{:S(2)}, u32[]{:S(2)}) async-start(bf16[32,2,128,128]{3,2,1,0:T(8,128)(2,1)} %get-tuple-element.41), calls=%async_computation.5 | async-start | bytes 4194304 | tf_op jit(solution)/shard_map/all_to_all | solution.py:387
  198.3 1.6 fusion.1
  199.9 1.1 gather_fusion.1
  201.1 8.3 %whiten.2 = (bf16[24,2,64,128]{3,2,1,0:T(8,128)(2,1)}, bf16[8,8,2,64,128]{4,3,2,1,0:T(8,128)(2,1)}) custom-call(s32[24]{0:T(128)} %get-tuple-element.46.source, s32[24]{0:T(128)} %get-tuple-element.45.length, s32[8,8]{1,0:T(8,128)} %gather_fusion.1, bf16[32,2,128,128]{3,2,1,0:T(8,128)(2,1)} %all_to_all.39.got, ...), custom_call_target="tpu_custom_call" | custom-call | flops 629145600 | bytes 4194304 | tf_op jit(solution)/shard_map/whiten/pallas_call | solution.py:206
  209.3 1.6 slice_bitcast_fusion
  211.3 1.8 collective-permute-start.3
  213.1 1.5 collective-permute-start.4
  214.6 2.1 collective-permute-start.5
  216.6 1.2 collective-permute-start.6
  217.8 20.8 %collective-permute-done.2.refs_0_ = bf16[8,2,64,128]{3,2,1,0:T(8,128)(2,1)S(1)} collective-permute-done((bf16[8,2,64,128]{3,2,1,0:T(8,128)(2,1)S(1)}, bf16[8,2,64,128]{3,2,1,0:T(8,128)(2,1)S(1)}, u32[]{:S(2)}, u32[]{:S(2)}) %collective-permute-start.2) | collective-permute-done | bytes 262176 | tf_op jit(solution)/shard_map/ppermute | solution.py:434
  238.8 3.4 %collective-permute-done.4.refs_2_ = bf16[8,2,64,128]{3,2,1,0:T(8,128)(2,1)S(1)} collective-permute-done((bf16[8,2,64,128]{3,2,1,0:T(8,128)(2,1)S(1)}, bf16[8,2,64,128]{3,2,1,0:T(8,128)(2,1)S(1)}, u32[]{:S(2)}, u32[]{:S(2)}) %collective-permute-start.4) | collective-permute-done | bytes 262176 | tf_op jit(solution)/shard_map/ppermute | solution.py:434
  242.1 10.6 %collective-permute-done.5.refs_3_ = bf16[8,2,64,128]{3,2,1,0:T(8,128)(2,1)S(1)} collective-permute-done((bf16[8,2,64,128]{3,2,1,0:T(8,128)(2,1)S(1)}, bf16[8,2,64,128]{3,2,1,0:T(8,128)(2,1)S(1)}, u32[]{:S(2)}, u32[]{:S(2)}) %collective-permute-start.5) | collective-permute-done | bytes 262176 | tf_op jit(solution)/shard_map/ppermute | solution.py:434
  253.7 8.4 %whiten.3 = (bf16[24,2,64,128]{3,2,1,0:T(8,128)(2,1)}, bf16[8,8,2,64,128]{4,3,2,1,0:T(8,128)(2,1)}) custom-call(s32[24]{0:T(128)} %get-tuple-element.46.source, s32[24]{0:T(128)} %get-tuple-element.45.length, s32[8,8]{1,0:T(8,128)} %bitcast.55, bf16[32,2,128,128]{3,2,1,0:T(8,128)(2,1)} %all-to-all-done.5.got, ...), custom_call_target="tpu_custom_call" | custom-call | flops 629145600 | bytes 4194304 | tf_op jit(solution)/shard_map/whiten/pallas_call | solution.py:206
  262.2 5.3 %all-to-all-start.6 = ((bf16[8,8,2,64,128]{4,3,2,1,0:T(8,128)(2,1)}), bf16[8,8,2,64,128]{4,3,2,1,0:T(8,128)(2,1)S(1)}, u32[]{:S(2)}, u32[]{:S(2)}) async-start(bf16[8,8,2,64,128]{4,3,2,1,0:T(8,128)(2,1)} %get-tuple-element.44), calls=%async_computation.6 | async-start | bytes 4194304 | tf_op jit(solution)/shard_map/all_to_all | solution.py:438
  269.3 1.6 copy-done.1
  273.9 13.0 %cross_first.1.begun = f32[16384,128]{1,0:T(8,128)S(1)} custom-call(s32[8,8]{1,0:T(8,128)S(1)} %copy.44.near_pick, bf16[24,2,64,128]{3,2,1,0:T(8,128)(2,1)S(1)} %copy-done.16, bf16[8,8,2,64,128]{4,3,2,1,0:T(8,128)(2,1)S(1)} %copy-done.1, bf16[8,2,64,128]{3,2,1,0:T(8,128)(2,1)S(1)} %copy-done.3, bf16[8,2,64,128]{3,2,1,0:T(8,128)(2,1)S(1)} %copy-done.5, ...), custom_call_target="tpu_custom_call" | custom-call | flops 33554432 | bytes 25165824 | tf_op jit(solution)/shard_map/cross_first/pallas_call | solution.py:280
  286.9 3.3 %copy-done = f32[16384,128]{1,0:T(8,128)} copy-done((f32[16384,128]{1,0:T(8,128)}, f32[16384,128]{1,0:T(8,128)S(1)}, u32[]{:S(2)}) %copy-start) | copy-done | bytes 8388632
  290.2 5.9 %all-to-all-done.6.far_in = bf16[8,8,2,64,128]{4,3,2,1,0:T(8,128)(2,1)S(1)} async-done(((bf16[8,8,2,64,128]{4,3,2,1,0:T(8,128)(2,1)}), bf16[8,8,2,64,128]{4,3,2,1,0:T(8,128)(2,1)S(1)}, u32[]{:S(2)}, u32[]{:S(2)}) %all-to-all-start.6) | async-done | bytes 2097184 | tf_op jit(solution)/shard_map/all_to_all | solution.py:438
  297.2 24.5 %lagged.1 = f32[256,1024]{1,0:T(8,128)S(1)} custom-call(s32[8,8]{1,0:T(8,128)S(1)} %copy.44.near_pick, s32[8]{0:T(128)S(1)} %and_select_fusion.2.far_at, f32[16384,128]{1,0:T(8,128)} %copy-done, bf16[24,2,64,128]{3,2,1,0:T(8,128)(2,1)S(1)} %copy-done.17, bf16[8,8,2,64,128]{4,3,2,1,0:T(8,128)(2,1)S(1)} %all-to-all-done.6.far_in, ...), custom_call_target="tpu_custom_call" | custom-call | flops 4294967296 | bytes 25165824 | tf_op jit(solution)/shard_map/lagged/pallas_call | solution.py:334
  321.7 1.3 reshape.193
  (86 shorter events, 9.9 us)
Async XLA Ops:
  0.0 7.8 %copy-start.22 = (s32[1,72]{1,0:T(1,128)S(1)}, s32[1,72]{1,0:T(1,128)}, u32[]{:S(2)}) copy-start(s32[1,72]{1,0:T(1,128)} %param.14) | copy-start | bytes 868
  0.0 7.8 %copy-start.23 = (s32[1,72]{1,0:T(1,128)S(1)}, s32[1,72]{1,0:T(1,128)}, u32[]{:S(2)}) copy-start(s32[1,72]{1,0:T(1,128)} %param.13) | copy-start | bytes 868
  4.5 19.7 %collective-permute-start = (bf16[72,128,128]{2,1,0:T(8,128)(2,1)S(1)}, bf16[72,128,128]{2,1,0:T(8,128)(2,1)}, u32[]{:S(2)}, u32[]{:S(2)}) collective-permute-start(bf16[72,128,128]{2,1,0:T(8,128)(2,1)S(1)} %bitcast.49), channel_id=1, source_target_pairs={{0,8},{8,0},{16,24},{24,16},{32,40},{40,32},{48,56},{56,48},{64,72... | collective-permute-start | bytes 7077896 | tf_op jit(solution)/shard_map/ppermute | solution.py:390
  8.5 15.8 %all-to-all-start.2 = ((s32[32,1,72]{2,1,0:T(1,128)}), s32[32,1,72]{2,1,0:T(1,128)S(1)}, u32[]{:S(2)}, u32[]{:S(2)}) async-start(s32[32,1,72]{2,1,0:T(1,128)} %broadcast_in_dim.50), calls=%async_computation.2 | async-start | bytes 32768 | tf_op jit(solution)/shard_map/all_to_all | solution.py:376
  29.4 10.1 %copy-start.20 = (s32[1,1,8,2,4]{2,4,3,1,0:T(4,128)S(1)}, s32[1,1,8,2,4]{2,4,3,1,0:T(4,128)}, u32[]{:S(2)}) copy-start(s32[1,1,8,2,4]{2,4,3,1,0:T(4,128)} %param.16) | copy-start | bytes 772
  36.9 7.2 %collective-permute-start.1 = (bf16[72,128,128]{2,1,0:T(8,128)(2,1)}, bf16[72,128,128]{2,1,0:T(8,128)(2,1)}, u32[]{:S(2)}, u32[]{:S(2)}) collective-permute-start(bf16[72,128,128]{2,1,0:T(8,128)(2,1)} %bitcast.11.own), channel_id=1, source_target_pairs={{0,8},{8,0},{16,24},{24,16},{32,40},{40,32},{48,56},{56,48},{64,72... | collective-permute-start | bytes 7077896 | tf_op jit(solution)/shard_map/ppermute | solution.py:394
  134.8 65.1 %copy-start.18 = (s32[8,1,8]{2,1,0:T(1,128)}, s32[8,1,8]{2,1,0:T(1,128)S(1)}, u32[]{:S(2)}) copy-start(s32[8,1,8]{2,1,0:T(1,128)S(1)} %all_to_all.38) | copy-start | bytes 772
  190.4 62.3 %all-to-all-start.5 = ((bf16[32,2,128,128]{3,2,1,0:T(8,128)(2,1)}), bf16[32,2,128,128]{3,2,1,0:T(8,128)(2,1)}, u32[]{:S(2)}, u32[]{:S(2)}) async-start(bf16[32,2,128,128]{3,2,1,0:T(8,128)(2,1)} %get-tuple-element.41), calls=%async_computation.5 | async-start | bytes 4194304 | tf_op jit(solution)/shard_map/all_to_all | solution.py:387
  210.9 27.7 %collective-permute-start.2 = (bf16[8,2,64,128]{3,2,1,0:T(8,128)(2,1)S(1)}, bf16[8,2,64,128]{3,2,1,0:T(8,128)(2,1)S(1)}, u32[]{:S(2)}, u32[]{:S(2)}) collective-permute-start(bf16[8,2,64,128]{3,2,1,0:T(8,128)(2,1)S(1)} %get-tuple-element.55), channel_id=1, source_target_pairs={{0,1},{1,2},{2,3},{3,4},{4,5},{5,6},{6,7},{7,0},{8,9},{9,10},{10,1... | collective-permute-start | bytes 786440 | tf_op jit(solution)/shard_map/ppermute | solution.py:434
  211.3 27.4 %collective-permute-start.3 = (bf16[8,2,64,128]{3,2,1,0:T(8,128)(2,1)S(1)}, bf16[8,2,64,128]{3,2,1,0:T(8,128)(2,1)S(1)}, u32[]{:S(2)}, u32[]{:S(2)}) collective-permute-start(bf16[8,2,64,128]{3,2,1,0:T(8,128)(2,1)S(1)} %get-tuple-element.54), channel_id=1, source_target_pairs={{0,2},{1,3},{2,4},{3,5},{4,6},{5,7},{6,0},{7,1},{8,10},{9,11},{10,... | collective-permute-start | bytes 786440 | tf_op jit(solution)/shard_map/ppermute | solution.py:434
  213.1 29.1 %collective-permute-start.4 = (bf16[8,2,64,128]{3,2,1,0:T(8,128)(2,1)S(1)}, bf16[8,2,64,128]{3,2,1,0:T(8,128)(2,1)S(1)}, u32[]{:S(2)}, u32[]{:S(2)}) collective-permute-start(bf16[8,2,64,128]{3,2,1,0:T(8,128)(2,1)S(1)} %get-tuple-element.53), channel_id=1, source_target_pairs={{0,3},{1,4},{2,5},{3,6},{4,7},{5,0},{6,1},{7,2},{8,11},{9,12},{10,... | collective-permute-start | bytes 786440 | tf_op jit(solution)/shard_map/ppermute | solution.py:434
  214.6 38.1 %collective-permute-start.5 = (bf16[8,2,64,128]{3,2,1,0:T(8,128)(2,1)S(1)}, bf16[8,2,64,128]{3,2,1,0:T(8,128)(2,1)S(1)}, u32[]{:S(2)}, u32[]{:S(2)}) collective-permute-start(bf16[8,2,64,128]{3,2,1,0:T(8,128)(2,1)S(1)} %get-tuple-element.52), channel_id=1, source_target_pairs={{0,4},{1,5},{2,6},{3,7},{4,0},{5,1},{6,2},{7,3},{8,12},{9,13},{10,... | collective-permute-start | bytes 786440 | tf_op jit(solution)/shard_map/ppermute | solution.py:434
  216.6 36.1 %collective-permute-start.6 = (bf16[8,2,64,128]{3,2,1,0:T(8,128)(2,1)S(1)}, bf16[8,2,64,128]{3,2,1,0:T(8,128)(2,1)S(1)}, u32[]{:S(2)}, u32[]{:S(2)}) collective-permute-start(bf16[8,2,64,128]{3,2,1,0:T(8,128)(2,1)S(1)} %get-tuple-element.51), channel_id=1, source_target_pairs={{0,5},{1,6},{2,7},{3,0},{4,1},{5,2},{6,3},{7,4},{8,13},{9,14},{10,... | collective-permute-start | bytes 786440 | tf_op jit(solution)/shard_map/ppermute | solution.py:434
  238.7 14.1 %copy-start.2 = (bf16[8,2,64,128]{3,2,1,0:T(8,128)(2,1)}, bf16[8,2,64,128]{3,2,1,0:T(8,128)(2,1)S(1)}, u32[]{:S(2)}) copy-start(bf16[8,2,64,128]{3,2,1,0:T(8,128)(2,1)S(1)} %collective-permute-done.2.refs_0_) | copy-start | bytes 786436
  238.7 14.1 %collective-permute-start.7 = (bf16[8,2,64,128]{3,2,1,0:T(8,128)(2,1)S(1)}, bf16[8,2,64,128]{3,2,1,0:T(8,128)(2,1)S(1)}, u32[]{:S(2)}, u32[]{:S(2)}) collective-permute-start(bf16[8,2,64,128]{3,2,1,0:T(8,128)(2,1)S(1)} %get-tuple-element.50), channel_id=1, source_target_pairs={{0,6},{1,7},{2,0},{3,1},{4,2},{5,3},{6,4},{7,5},{8,14},{9,15},{10,... | collective-permute-start | bytes 786440 | tf_op jit(solution)/shard_map/ppermute | solution.py:434
  238.7 14.1 %copy-start.4 = (bf16[8,2,64,128]{3,2,1,0:T(8,128)(2,1)}, bf16[8,2,64,128]{3,2,1,0:T(8,128)(2,1)S(1)}, u32[]{:S(2)}) copy-start(bf16[8,2,64,128]{3,2,1,0:T(8,128)(2,1)S(1)} %collective-permute-done.3.refs_1_) | copy-start | bytes 786436
  238.7 14.1 %collective-permute-start.8 = (bf16[8,2,64,128]{3,2,1,0:T(8,128)(2,1)S(1)}, bf16[8,2,64,128]{3,2,1,0:T(8,128)(2,1)S(1)}, u32[]{:S(2)}, u32[]{:S(2)}) collective-permute-start(bf16[8,2,64,128]{3,2,1,0:T(8,128)(2,1)S(1)} %get-tuple-element.49), channel_id=1, source_target_pairs={{0,7},{1,0},{2,1},{3,2},{4,3},{5,4},{6,5},{7,6},{8,15},{9,8},{10,9... | collective-permute-start | bytes 786440 | tf_op jit(solution)/shard_map/ppermute | solution.py:434
  242.1 10.6 %copy-start.6 = (bf16[8,2,64,128]{3,2,1,0:T(8,128)(2,1)}, bf16[8,2,64,128]{3,2,1,0:T(8,128)(2,1)S(1)}, u32[]{:S(2)}) copy-start(bf16[8,2,64,128]{3,2,1,0:T(8,128)(2,1)S(1)} %collective-permute-done.4.refs_2_) | copy-start | bytes 786436
  262.1 5.4 %copy-start.21 = (s32[1,1,8,2,4]{2,4,3,1,0:T(4,128)S(1)}, s32[1,1,8,2,4]{2,4,3,1,0:T(4,128)}, u32[]{:S(2)}) copy-start(s32[1,1,8,2,4]{2,4,3,1,0:T(4,128)} %param.15) | copy-start | bytes 772
  262.1 5.5 %copy-start.19 = (s32[1,1,8,2,4,4]{2,5,4,3,1,0:T(4,128)S(1)}, s32[1,1,8,2,4,4]{2,5,4,3,1,0:T(4,128)}, u32[]{:S(2)}) copy-start(s32[1,1,8,2,4,4]{2,5,4,3,1,0:T(4,128)} %param.17) | copy-start | bytes 3076
  262.1 7.1 %copy-start.3 = (bf16[8,2,64,128]{3,2,1,0:T(8,128)(2,1)S(1)}, bf16[8,2,64,128]{3,2,1,0:T(8,128)(2,1)}, u32[]{:S(2)}) copy-start(bf16[8,2,64,128]{3,2,1,0:T(8,128)(2,1)} %copy-done.2) | copy-start | bytes 786436
  262.1 7.1 %copy-start.5 = (bf16[8,2,64,128]{3,2,1,0:T(8,128)(2,1)S(1)}, bf16[8,2,64,128]{3,2,1,0:T(8,128)(2,1)}, u32[]{:S(2)}) copy-start(bf16[8,2,64,128]{3,2,1,0:T(8,128)(2,1)} %copy-done.4) | copy-start | bytes 786436
  262.1 7.1 %copy-start.7 = (bf16[8,2,64,128]{3,2,1,0:T(8,128)(2,1)S(1)}, bf16[8,2,64,128]{3,2,1,0:T(8,128)(2,1)}, u32[]{:S(2)}) copy-start(bf16[8,2,64,128]{3,2,1,0:T(8,128)(2,1)} %copy-done.6) | copy-start | bytes 786436
  262.2 7.1 %copy-start.9 = (bf16[8,2,64,128]{3,2,1,0:T(8,128)(2,1)S(1)}, bf16[8,2,64,128]{3,2,1,0:T(8,128)(2,1)}, u32[]{:S(2)}) copy-start(bf16[8,2,64,128]{3,2,1,0:T(8,128)(2,1)} %copy-done.8) | copy-start | bytes 786436
  262.2 7.1 %copy-start.11 = (bf16[8,2,64,128]{3,2,1,0:T(8,128)(2,1)S(1)}, bf16[8,2,64,128]{3,2,1,0:T(8,128)(2,1)}, u32[]{:S(2)}) copy-start(bf16[8,2,64,128]{3,2,1,0:T(8,128)(2,1)} %copy-done.10) | copy-start | bytes 786436
  262.2 33.9 %all-to-all-start.6 = ((bf16[8,8,2,64,128]{4,3,2,1,0:T(8,128)(2,1)}), bf16[8,8,2,64,128]{4,3,2,1,0:T(8,128)(2,1)S(1)}, u32[]{:S(2)}, u32[]{:S(2)}) async-start(bf16[8,8,2,64,128]{4,3,2,1,0:T(8,128)(2,1)} %get-tuple-element.44), calls=%async_computation.6 | async-start | bytes 4194304 | tf_op jit(solution)/shard_map/all_to_all | solution.py:438
  269.3 1.6 copy-start.1
  270.9 0.9 copy-start.13
  271.8 0.9 copy-start.15
  272.8 1.1 copy-start.16
  286.9 3.3 %copy-start = (f32[16384,128]{1,0:T(8,128)}, f32[16384,128]{1,0:T(8,128)S(1)}, u32[]{:S(2)}) copy-start(f32[16384,128]{1,0:T(8,128)S(1)} %cross_first.1.begun) | copy-start | bytes 25165828
  296.1 1.1 copy-start.17
  (4 other events, 3.3 us)

commit v4 on v3

v4 whole, which is shorter than its diff:
```python
import functools
import math

import jax
import jax.numpy as jnp
import numpy as np
from jax import lax
from jax.experimental import pallas as pl
from jax.experimental.pallas import tpu as pltpu
from jax.sharding import PartitionSpec as P

ST_DEV = 24
SEG = 4
NT = 8192
NF = 4096
LAGS = 1024
ROWS = 64
LANES = 128
BASE = 2
EXTRA = 1
LEN_BITS = 16
NOTES = 16
SMEM = pl.BlockSpec(memory_space=pltpu.SMEM)
VMEM = pl.BlockSpec(memory_space=pltpu.VMEM)
ANY = pl.BlockSpec(memory_space=pl.ANY)


def split_bf16(values):
    high = values.astype(jnp.bfloat16)
    low = (values - high.astype(np.float64)).astype(jnp.bfloat16)
    return high, low


def transform_tables():
    first = np.arange(ROWS)
    second = np.arange(LANES)
    half = np.arange(LANES // 2)
    angle = 2.0 * math.pi / ROWS * (first[:, None] * first[None, :] % ROWS)
    wave = np.concatenate([np.cos(angle), -np.sin(angle)], 0)
    wave = np.einsum("ab,kn->aknb", np.eye(2), wave).reshape(4 * ROWS, 2 * ROWS)
    first_table = np.concatenate(split_bf16(wave), 1)
    twist = 2.0 * math.pi / NT * (first[:, None] * second[None, :] % NT)
    twist_table = np.stack([np.cos(twist), np.sin(twist)]).astype(np.float32)
    angle = 2.0 * math.pi / LANES * (second[:, None] * half[None, :] % LANES)
    cos, sin = np.cos(angle), np.sin(angle)
    wave = np.concatenate([np.concatenate([cos, -sin], 1), np.concatenate([sin, cos], 1)], 0)
    second_table = np.concatenate(split_bf16(wave), 1)
    return first_table, twist_table, second_table


def lag_tables():
    row = np.arange(ROWS // 2, dtype=np.int64)
    lane = np.arange(LANES, dtype=np.int64)
    bins = (row[:, None] + ROWS // 2 * (lane // ROWS)) + ROWS * (lane % ROWS)
    bins = bins.reshape(-1)
    weight = np.where(bins == 0, 0.5, 1.0).astype(np.float32) / np.float32(math.sqrt(NF * SEG))

    def at(delay):
        phase = bins[:, None] * delay[None, :] % NT
        return phase.astype(np.float32) * np.float32(2.0 * math.pi / NT)

    ahead = at(np.arange(LAGS // 2, dtype=np.int64))
    edge = at(np.array([NT - LAGS // 2], dtype=np.int64))
    cos = weight[:, None] * np.cos(ahead)
    sin = -weight[:, None] * np.sin(ahead)
    sin[:, :1] = -weight[:, None] * np.sin(edge)
    last = (weight[:, None] * np.cos(edge)).reshape(ROWS // 2, 1, LANES)
    return (
        np.concatenate([cos, sin], 0).astype(jnp.bfloat16),
        last.astype(jnp.bfloat16).astype(np.float32),
    )


def pack_kernel(low, count, noted, packed, core_ref, own, mate, after, out, flag, fill, notes, started, sem):
    core = core_ref[0]
    slots = packed.shape[1]
    devices = out.shape[0]
    started[0] = 0
    flag[0] = 0

    @pl.loop(0, devices)
    def _(dev):
        fill[dev] = 0
        for slot in range(count):
            notes[dev, slot] = -1

    def place(half, source):
        @pl.loop(0, slots)
        def _(at):
            value = packed[half, at]

            @pl.when(value >= 0)
            def _():
                dev = ((value >> LEN_BITS) * 2731) >> 16
                rank = fill[dev]
                fill[dev] = rank + 1
                slot = (rank >> 1) - low

                @pl.when(((rank & 1) == core) & (slot >= 0) & (slot < count))
                def _():
                    started[0] += 1
                    notes[dev, slot] = value - ((dev * ST_DEV) << LEN_BITS)
                    place_at = pl.ds(pl.multiple_of(slot * 2 * ROWS, 2 * ROWS), 2 * ROWS)
                    pltpu.make_async_copy(source.at[at], out.at[dev, place_at], sem).start()

                @pl.when(slot >= count)
                def _():
                    flag[0] = 1

    for half in range(2):

        @pl.when(core == half)
        def _():
            place(half, own)

        @pl.when(core != half)
        def _():
            place(half, mate)

    if noted:
        row = lax.broadcasted_iota(jnp.int32, (NOTES, LANES), 0)

        @pl.loop(0, devices)
        def _(dev):
            tile = jnp.where(row == 4 * count, flag[0], 0)
            for slot in range(count):
                value = notes[dev, slot]
                tile = jnp.where(row == 4 * slot, (value >> LEN_BITS) + 1, tile)
                tile = jnp.where(row == 4 * slot + 1, (value & 0xFFFF) >> 8, tile)
                tile = jnp.where(row == 4 * slot + 2, value & 0xFF, tile)
            out[dev, count * 2 * ROWS :, :] = tile.astype(jnp.float32).astype(jnp.bfloat16)

    @pl.loop(0, started[0])
    def _(_):
        pltpu.make_async_copy(own.at[0], out.at[0, pl.ds(0, 2 * ROWS)], sem).wait()


def pack(low, count, noted, wide_count, packed, core, own, mate, after):
    height = count * 2 * ROWS + (NOTES if noted else 0)
    return pl.pallas_call(
        functools.partial(pack_kernel, low, count, noted),
        out_shape=(
            jax.ShapeDtypeStruct((wide_count, height, LANES), jnp.bfloat16),
            jax.ShapeDtypeStruct((1,), jnp.int32),
        ),
        in_specs=[SMEM, SMEM, ANY, ANY, ANY],
        out_specs=(VMEM, SMEM),
        scratch_shapes=[
            pltpu.SMEM((wide_count,), jnp.int32),
            pltpu.SMEM((wide_count, count), jnp.int32),
            pltpu.SMEM((1,), jnp.int32),
            pltpu.SemaphoreType.DMA,
        ],
        cost_estimate=pl.CostEstimate(flops=0, bytes_accessed=wide_count * count * NT * 8, transcendentals=0),
        name="pack",
    )(packed, core, own, mate, after)


def read_notes(rows, count):
    notes = rows[:, count * 2 * ROWS :, 0].astype(jnp.float32).astype(jnp.int32)
    fields = notes[:, : 4 * count].reshape(-1, count, 4)
    return fields[..., 0] - 1, fields[..., 1] * 256 + fields[..., 2], notes[:, 4 * count]


def whiten_kernel(
    part, source, length, picks, got, more, first, twist, second, *refs
):
    white, payload, held, spectra, sem, sems = refs[-6:]
    stations = held.shape[0]
    first_more = got.shape[0] * BASE
    batch = 4

    @pl.loop(0, stations)
    def _(station):
        code = source[station]
        over = code - first_more

        @pl.when(over < 0)
        def _():
            place_at = pl.ds(pl.multiple_of((code & 1) * 2 * ROWS, 2 * ROWS), 2 * ROWS)
            pltpu.make_async_copy(got.at[code >> 1, place_at], held.at[station], sems.at[station // batch]).start()

        @pl.when(over >= 0)
        def _():
            place_at = pl.ds(0, 2 * ROWS)
            pltpu.make_async_copy(more.at[over, place_at], held.at[station], sems.at[station // batch]).start()

    row = lax.broadcasted_iota(jnp.int32, (2 * ROWS, LANES), 0)
    lane = lax.broadcasted_iota(jnp.int32, (2 * ROWS, LANES), 1)
    left = lax.broadcasted_iota(jnp.int32, (ROWS // 2, LANES), 1) < ROWS
    place = (2 * part + (row & 1)) * NT + (row >> 1) * LANES + lane

    def two_stations(station):
        sides = []
        for at in range(2):
            values = held[station + at].astype(jnp.float32)
            sides.append(jnp.where(place < length[station + at], values, 0.0).astype(jnp.bfloat16))
        values = jnp.concatenate(sides, 1)
        values = jnp.concatenate([values, values], 0)
        mixed = jnp.dot(first[...], values, preferred_element_type=jnp.float32)
        parts = []
        for at in range(2):
            for seg in range(2):
                real = mixed[2 * seg * ROWS : (2 * seg + 1) * ROWS, at * LANES : (at + 1) * LANES]
                imag = mixed[(2 * seg + 1) * ROWS : (2 * seg + 2) * ROWS, at * LANES : (at + 1) * LANES]
                turned_re = real * twist[0] + imag * twist[1]
                turned_im = imag * twist[0] - real * twist[1]
                parts.append(jnp.concatenate([turned_re, turned_im], 1))
        turned = jnp.concatenate(parts, 0)
        high = turned.astype(jnp.bfloat16)
        low = (turned - high.astype(jnp.float32)).astype(jnp.bfloat16)
        upper = jnp.dot(high, second[...], preferred_element_type=jnp.float32)
        lower = jnp.dot(low, second[:, :LANES], preferred_element_type=jnp.float32)
        spectrum = upper[:, :LANES] + (upper[:, LANES:] + lower)
        for at in range(2):
            for seg in range(2):
                begin = (2 * at + seg) * ROWS
                side = spectrum[begin : begin + ROWS]
                power = jnp.sum(side * side, axis=0, keepdims=True)
                power = (power + pltpu.roll(power, LANES // 2, 1)) * (1.0 / ROWS)
                scale = 1.0 / jnp.sqrt(power + 1e-06)
                side = side * scale
                upper, lower = side[: ROWS // 2], side[ROWS // 2 :]
                real = jnp.where(left, upper, pltpu.roll(lower, ROWS, 1))
                imag = jnp.where(left, pltpu.roll(upper, ROWS, 1), lower)
                spectra[station + at, seg, : ROWS // 2] = real.astype(jnp.bfloat16)
                spectra[station + at, seg, ROWS // 2 :] = imag.astype(jnp.bfloat16)

    @pl.loop(0, stations // batch)
    def _(at):
        these = held.at[pl.ds(at * batch, batch)]
        pltpu.make_async_copy(these, these, sems.at[at]).wait()
        for two in range(0, batch, 2):
            two_stations(batch * at + two)

    stops, rows = picks.shape

    @pl.loop(0, stops)
    def _(stop):
        for at in range(rows):
            pltpu.make_async_copy(spectra.at[picks[stop, at]], payload.at[stop, at], sem).start()

    whole = pltpu.make_async_copy(spectra, white, sems.at[0])
    whole.start()
    pltpu.make_async_copy(payload, payload, sem).wait()
    whole.wait()


def whiten(part, source, length, picks, got, more, tables, after):
    stops, rows = picks.shape
    return pl.pallas_call(
        functools.partial(whiten_kernel, part),
        out_shape=(
            jax.ShapeDtypeStruct((ST_DEV, 2, ROWS, LANES), jnp.bfloat16),
            jax.ShapeDtypeStruct((stops, rows, 2, ROWS, LANES), jnp.bfloat16),
        ),
        in_specs=[SMEM, SMEM, SMEM, ANY, ANY, VMEM, VMEM, VMEM] + [ANY] * len(after),
        out_specs=(ANY, ANY),
        scratch_shapes=[
            pltpu.VMEM((ST_DEV, 2 * ROWS, LANES), jnp.bfloat16),
            pltpu.VMEM((ST_DEV, 2, ROWS, LANES), jnp.bfloat16),
            pltpu.SemaphoreType.DMA,
            pltpu.SemaphoreType.DMA((ST_DEV // 4,)),
        ],
        cost_estimate=pl.CostEstimate(
            flops=2 * ST_DEV * 2 * ROWS * 256 * 400, bytes_accessed=4 * 1024 * 1024, transcendentals=0
        ),
        name="whiten",
    )(source, length, picks, got, more, *tables, *after)


def cross_rows(near_pick, near, far, cross, fresh, ready):
    stops, rows = near_pick.shape
    side = rows // 2
    step = 16
    half = ROWS // 2

    @pl.loop(0, stops)
    def _(stop):
        ready(stop)
        for two in range(2):
            first = two * side
            own = [near_pick[stop, first + i] for i in range(side)]

            @pl.loop(0, half // step)
            def _(chunk):
                real = pl.ds(pl.multiple_of(chunk * step, step), step)
                imag = pl.ds(pl.multiple_of(half + chunk * step, step), step)

                def both(ref, row):
                    return [
                        (ref[row, s, real, :].astype(jnp.float32), ref[row, s, imag, :].astype(jnp.float32))
                        for s in range(2)
                    ]

                here = [both(near, own[i]) for i in range(side)]
                for j in range(side):
                    there = both(far.at[stop], first + j)
                    for i in range(side):
                        pair = ((stop * 2 + two) * side + i) * side + j
                        total_re = sum(n[0] * f[0] + n[1] * f[1] for n, f in zip(here[i], there))
                        total_im = sum(n[1] * f[0] - n[0] * f[1] for n, f in zip(here[i], there))
                        for total, add in ((total_re, 0), (total_im, half)):
                            at = pl.ds(pl.multiple_of(pair * ROWS + add + chunk * step, step), step)
                            if fresh:
                                cross[at, :] = total
                            else:
                                cross[at, :] += total


def cross_kernel(stops, near_pick, white, home, *refs):
    far_in = refs[: stops - 1]
    out, near, far, cross, sem, sems, out_sem = refs[stops - 1 :]
    load = pltpu.make_async_copy(white, near, sem)
    load.start()
    pltpu.make_async_copy(home.at[0], far.at[0], sems.at[0]).start()
    for stop in range(1, stops):
        pltpu.make_async_copy(far_in[stop - 1], far.at[stop], sems.at[stop]).start()
    load.wait()

    def ready(stop):
        pltpu.make_async_copy(far.at[stop], far.at[stop], sems.at[stop]).wait()

    cross_rows(near_pick, near, far, cross, True, ready)
    copy = pltpu.make_async_copy(cross, out, out_sem)
    copy.start()
    copy.wait()


def cross_first(near_pick, white, home, far):
    stops, rows = near_pick.shape
    pairs = stops * rows * rows // 2
    return pl.pallas_call(
        functools.partial(cross_kernel, stops),
        out_shape=jax.ShapeDtypeStruct((pairs * ROWS, LANES), jnp.float32),
        in_specs=[SMEM] + [ANY] * (stops + 1),
        out_specs=ANY,
        scratch_shapes=[
            pltpu.VMEM(white.shape, jnp.bfloat16),
            pltpu.VMEM(home.shape, jnp.bfloat16),
            pltpu.VMEM((pairs * ROWS, LANES), jnp.float32),
            pltpu.SemaphoreType.DMA,
            pltpu.SemaphoreType.DMA((stops,)),
            pltpu.SemaphoreType.DMA,
        ],
        compiler_params=pltpu.CompilerParams(vmem_limit_bytes=20 * 1024 * 1024),
        cost_estimate=pl.CostEstimate(
            flops=pairs * ROWS * LANES * 16, bytes_accessed=24 * 1024 * 1024, transcendentals=0
        ),
        name="cross_first",
    )(near_pick, white, home, *far)


def lag_kernel(
    near_pick, far_at, begun, white, far_in, table, last, mask, out, near, far, cross, tables, sem, sems, table_sem
):
    stops = near_pick.shape[0]
    pairs = out.shape[0]
    rows = pairs * ROWS // stops
    load = pltpu.make_async_copy(white, near, sem)
    load.start()
    for stop in range(stops):
        these = pl.ds(stop * rows, rows)
        pltpu.make_async_copy(far_in.at[far_at[stop]], far.at[stop], sems.at[0, stop]).start()
        pltpu.make_async_copy(begun.at[these], cross.at[these], sems.at[1, stop]).start()
    load_table = pltpu.make_async_copy(table, tables, table_sem)
    load_table.start()
    load.wait()

    def ready(stop):
        these = cross.at[pl.ds(pl.multiple_of(stop * rows, rows), rows)]
        pltpu.make_async_copy(far.at[stop], far.at[stop], sems.at[0, stop]).wait()
        pltpu.make_async_copy(these, these, sems.at[1, stop]).wait()

    cross_rows(near_pick, near, far, cross, False, ready)
    load_table.wait()
    group = 8
    depth = group * LANES
    half = LAGS // 2
    turns = ROWS // 2 // group

    def product(turn, edge):
        base = turn * group
        slabs = [
            cross[pl.ds(base + k, pairs, stride=ROWS), :].astype(jnp.bfloat16) for k in range(group)
        ]
        if edge is not None:
            for k in range(group):
                edge += slabs[k].astype(jnp.float32) * last[base + k]
        part = jnp.dot(
            jnp.concatenate(slabs, 1),
            tables[pl.ds(pl.multiple_of(base * LANES, depth), depth), :],
            preferred_element_type=jnp.float32,
        )
        return part, edge

    out[:, :half] = jnp.zeros((pairs, half), jnp.float32)
    out[:, half:] = jnp.zeros((pairs, half), jnp.float32)

    def even_step(turn, edge):
        part, edge = product(turn, edge)
        out[:, :half] += part
        return edge

    edge = lax.fori_loop(0, turns, even_step, jnp.zeros((pairs, LANES), jnp.float32))

    @pl.loop(turns, 2 * turns)
    def _(turn):
        out[:, half:] += product(turn, None)[0]

    edge = jnp.sum(edge, axis=1, keepdims=True)
    lane = lax.broadcasted_iota(jnp.int32, (pairs, LANES), 1)
    mirror = (LANES - lane) % LANES
    first = lane == 0
    listed = mask[...]
    count = half // LANES
    before, after = [], []
    for block in range(count):
        even = out[:, block * LANES : (block + 1) * LANES]
        odd = out[:, half + block * LANES : half + (block + 1) * LANES]
        if block == 0:
            edge = edge + odd
            odd = jnp.where(first, 0.0, odd)
        before.append(even - odd)
        after.append(even + odd)
    for block in range(count):
        turned = jnp.take_along_axis(before[count - 1 - block], mirror, axis=1)
        start = edge if block == 0 else before[count - block]
        out[:, block * LANES : (block + 1) * LANES] = jnp.where(first, start, turned) * listed
        out[:, half + block * LANES : half + (block + 1) * LANES] = after[block] * listed


def lagged(near_pick, far_at, begun, white, far, table, last, mask):
    pairs = mask.shape[0]
    stops = near_pick.shape[0]
    return pl.pallas_call(
        lag_kernel,
        out_shape=jax.ShapeDtypeStruct((pairs, LAGS), jnp.float32),
        in_specs=[SMEM, SMEM] + [ANY] * 4 + [VMEM, VMEM],
        out_specs=VMEM,
        scratch_shapes=[
            pltpu.VMEM(white.shape, jnp.bfloat16),
            pltpu.VMEM(far.shape, jnp.bfloat16),
            pltpu.VMEM((pairs * ROWS, LANES), jnp.float32),
            pltpu.VMEM(table.shape, jnp.bfloat16),
            pltpu.SemaphoreType.DMA,
            pltpu.SemaphoreType.DMA((2, stops)),
            pltpu.SemaphoreType.DMA,
        ],
        compiler_params=pltpu.CompilerParams(vmem_limit_bytes=40 * 1024 * 1024),
        cost_estimate=pl.CostEstimate(
            flops=2 * pairs * NF * LAGS, bytes_accessed=24 * 1024 * 1024, transcendentals=0
        ),
        name="lagged",
    )(near_pick, far_at, begun, white, far, table, last, mask)


def empty(shape):
    return pl.pallas_call(
        lambda out: None,
        out_shape=jax.ShapeDtypeStruct(shape, jnp.bfloat16),
        out_specs=ANY,
        name="empty",
    )()


def on_device(records, lengths, owners, own_pick, visit_pick, pair_mask):
    wide_count = lax.axis_size("wide")
    stops = lax.axis_size("blk")
    column = lax.axis_index("wide")
    group = lax.axis_index("blk")
    core = column % 2
    swap = [(i, i ^ 1) for i in range(wide_count)]
    slots = records.shape[1]
    steps = jnp.arange(stops, dtype=jnp.int32)

    packed = jnp.where(owners[0] >= 0, (owners[0] << LEN_BITS) + lengths[0], -1)
    mate_packed = lax.ppermute(packed, "wide", swap)
    chip_packed = jnp.where(core == 0, jnp.stack([packed, mate_packed]), jnp.stack([mate_packed, packed]))
    core_at = core.reshape(1)

    tiles = records[0].reshape(slots, SEG, ROWS, LANES)

    def halves(part):
        return tiles[:, 2 * part : 2 * part + 2].transpose(0, 2, 1, 3).reshape(slots, 2 * ROWS, LANES)

    def send(payload):
        return lax.all_to_all(payload, "wide", split_axis=0, concat_axis=0, tiled=True)

    own_a = halves(0)
    mate_a = lax.ppermute(own_a, "wide", swap)
    load_a, flag_a = pack(0, BASE, True, wide_count, chip_packed, core_at, own_a, mate_a, core_at)
    got_a = send(load_a)
    own_b = jnp.where(flag_a[0] >= 0, halves(1), 0.0)
    mate_b = lax.ppermute(own_b, "wide", swap)
    load_b, flag_b = pack(0, BASE, False, wide_count, chip_packed, core_at, own_b, mate_b, load_a)
    got_b = send(load_b)
    visits = jnp.where(flag_a[0] >= 0, visit_pick[0, 0].reshape(stops, -1), 0)
    by_stop = jnp.stack(
        [visits[0]]
        + [
            lax.ppermute(visits[stop], "blk", [(i, (i - stop) % stops) for i in range(stops)])
            for stop in range(1, stops)
        ]
    )
    by_dest = by_stop[(steps - group) % stops]

    station, length, spilled = read_notes(got_a, BASE)
    spilled = jnp.max(spilled) > 0

    def late():
        rows = [
            pack(BASE, EXTRA, True, wide_count, chip_packed, core_at, own, mate, core_at)[0]
            for own, mate in ((own_a, mate_a), (own_b, mate_b))
        ]
        return tuple(send(row) for row in rows)

    more = lax.cond(
        spilled,
        late,
        lambda: tuple(empty((wide_count, EXTRA * 2 * ROWS + NOTES, LANES)) for _ in range(2)),
    )
    more_station, more_length, _ = read_notes(more[0], EXTRA)
    station = jnp.concatenate([station.reshape(-1), jnp.where(spilled, more_station.reshape(-1), -1)])
    length = jnp.concatenate([length.reshape(-1), more_length.reshape(-1)])
    chosen = station[None, :] == jnp.arange(ST_DEV, dtype=jnp.int32)[:, None]
    codes = jnp.arange(station.shape[0], dtype=jnp.int32)
    source = jnp.sum(jnp.where(chosen, codes[None], 0), axis=1)
    length = jnp.sum(jnp.where(chosen, length[None], 0), axis=1)

    tables = [jnp.asarray(table) for table in transform_tables()]
    near_pick = own_pick[0, 0].reshape(stops, -1)
    white_a, payload_a = whiten(0, source, length, by_stop, got_a, more[0], tables, [])
    far_a = [
        lax.ppermute(payload_a[stop], "blk", [(i, (i + stop) % stops) for i in range(stops)])
        for stop in range(1, stops)
    ]
    white_b, payload_b = whiten(1, source, length, by_dest, got_b, more[1], tables, far_a)
    far_b = lax.all_to_all(payload_b, "blk", split_axis=0, concat_axis=0, tiled=True)

    begun = cross_first(near_pick, white_a, payload_a, far_a)
    far_at = (group - steps) % stops
    mask = pair_mask[0, 0].astype(jnp.float32).reshape(-1, 1)
    table, last = lag_tables()
    result = lagged(near_pick, far_at, begun, white_b, far_b, jnp.asarray(table), jnp.asarray(last), mask)
    return result.reshape((1, 1) + pair_mask.shape[2:] + (LAGS,))


def solution(mesh):
    return jax.shard_map(
        on_device,
        mesh=mesh,
        in_specs=(
            P("blk", "wide", None, None),
            P("blk", "wide"),
            P("blk", "wide"),
            P("blk", "wide", None, None, None),
            P("blk", "wide", None, None, None),
            P("blk", "wide", None, None, None, None),
        ),
        out_specs=P("blk", "wide", None, None, None, None, None),
        check_vma=False,
    )
```

time: 325 us -> 225 us (0.69)
  blocking collectives: 140 us -> 0 us
  waiting for transfers between devices: 52.3 us -> 84.9 us
  Pallas kernels: 63.6 us -> 44.2 us
  local copies, waits for them, and re-layouts: 21.7 us -> 39 us
  starting transfers between devices: 32.9 us -> 44.6 us
    pmax x1 -> x0, blocking collectives: 75.1 us -> none  [on_device(): lax.pmax(flag_b[0], ('blk', 'wide')) > 0]
    all_to_all x2 -> x0, blocking collectives: 65 us -> none  [the longest x1 55.6 us: send(): lax.all_to_all(payload, 'wide', split_axis=0, concat_axis=0, tiled=True)]
    all_to_all x1 -> x2, waiting for transfers between devices: 0.01 us -> 34.3 us  [send(): lax.all_to_all(payload, 'wide', split_axis=0, concat_axis=0, tiled=True)]
    ppermute x7, waiting for transfers between devices: 34.8 us -> 21.2 us  [on_device(): lax.ppermute(payload_a[stop], 'blk', [(i, (i + stop) % stops) for i in ra...]
    pallas_call x1, Pallas kernels: 24.5 us -> 11.3 us  [lagged(): pl.pallas_call(lag_kernel, out_shape=jax.ShapeDtypeStruct((pairs, LAGS),...]
    ppermute x0 -> x8, starting transfers between devices: none -> 12.8 us  [the longest x7 12.7 us: on_device(): lax.ppermute(visits[stop], 'blk', [(i, (i - stop) % stops) for i in range...]
    cond x0 -> x1, local copies, waits for them, and re-layouts: none -> 10.1 us  [on_device(): lax.cond(spilled, late, lambda: tuple((empty((wide_count, EXTRA * 2 * ROW...]
    ppermute x0 -> x8, waiting for transfers between devices: none -> 9.85 us  [the longest x7 6 us: on_device(): lax.ppermute(visits[stop], 'blk', [(i, (i - stop) % stops) for i in range...]
  transfers between devices with their start and end apart: 12 -> 20, of which waited for: 6 -> 10; matrix products, arithmetic and copies ran while one was open for 3% -> 11% of each run, Pallas kernels for 7% -> 8%
where the time goes in v4:
time: 225 us; the launch traced here: 224 us
  waiting for transfers between devices  84.9 us (38%)
  starting transfers between devices  44.6 us (20%)
  Pallas kernels  44.2 us (20%)
  local copies, waits for them, and re-layouts  39 us (17%)
  other arithmetic  9.16 us (4%)
    all_to_all x2, waiting for transfers between devices, send(): lax.all_to_all(payload, 'wide', split_axis=0, concat_axis=0, tiled=True)  34.3 us
    ppermute x7, waiting for transfers between devices, on_device(): lax.ppermute(payload_a[stop], 'blk', [(i, (i + stop) % stops) for i in ra...  21.2 us
    pallas_call x2, Pallas kernels, whiten(): pl.pallas_call(functools.partial(whiten_kernel, part), out_shape=(jax.Sha...  16.8 us
    unnamed x54, local copies, waits for them, and re-layouts  15.5 us
    all_to_all x1, waiting for transfers between devices, on_device(): lax.all_to_all(payload_b, 'blk', split_axis=0, concat_axis=0, tiled=True)  14.9 us
    all_to_all x2, starting transfers between devices, send(): lax.all_to_all(payload, 'wide', split_axis=0, concat_axis=0, tiled=True)  13.8 us
    ppermute x7, starting transfers between devices, on_device(): lax.ppermute(visits[stop], 'blk', [(i, (i - stop) % stops) for i in range...  12.7 us
    pallas_call x2, Pallas kernels, pack(): pl.pallas_call(functools.partial(pack_kernel, low, count, noted), out_sha...  12.1 us
  transfers between devices with their start and end apart: 20, of which 10 were waited for; matrix products, arithmetic and copies ran while one was open for 11% of the time, Pallas kernels for 8%

profile of v4, /device:TPU:1, one launch (start us, length us, event | category | flops | bytes accessed | tf_op | source)
XLA Modules:
  0.0 223.5 jit_solution(15728460800957382147)
XLA Ops:
  0.0 4.5 %slice.125 = bf16[72,2,64,128]{3,1,2,0:T(2,128)(2,1)S(1)} slice(bf16[72,4,64,128]{3,1,2,0:T(4,128)(2,1)} %bitcast.56), slice={[0:72], [0:2], [0:64], [0:128]} | slice | bytes 4718592 | tf_op jit(solution)/shard_map/slice | solution.py:485
  4.5 3.3 %collective-permute-start.1 = (bf16[72,128,128]{2,1,0:T(8,128)(2,1)S(1)}, bf16[72,128,128]{2,1,0:T(8,128)(2,1)}, u32[]{:S(2)}, u32[]{:S(2)}) collective-permute-start(bf16[72,128,128]{2,1,0:T(8,128)(2,1)S(1)} %bitcast.50), channel_id=1, source_target_pairs={{0,8},{8,0},{16,24},{24,16},{32,40},{40,32},{48,56},{56,48},{64,72... | collective-permute-start | bytes 7077896 | tf_op jit(solution)/shard_map/ppermute | solution.py:491
  8.0 3.9 %collective-permute-done = s32[72]{0:T(128)S(1)} collective-permute-done((s32[72]{0:T(128)S(1)}, s32[72]{0:T(128)S(1)}, u32[]{:S(2)}, u32[]{:S(2)}) %collective-permute-start) | collective-permute-done | bytes 320 | tf_op jit(solution)/shard_map/ppermute | solution.py:478
  12.1 6.7 %pack.6 = (bf16[32,272,128]{2,1,0:T(8,128)(2,1)}, s32[1]{0:T(128)}) custom-call(s32[2,72]{1,0:T(2,128)S(1)} %add_select_fusion.packed, s32[1]{0:T(128)} %bitcast.3.core_ref.after, bf16[72,128,128]{2,1,0:T(8,128)(2,1)S(1)} %bitcast.51, bf16[72,128,128]{2,1,0:T(8,128)(2,1)} %collective-permute-done.1.mate, s32[1]{0:T(128)} %bitcast.3.core_ref.after), custom_call_target="tpu_custom_call" | custom-call | bytes 4194304 | tf_op jit(solution)/shard_map/pack/pallas_call | solution.py:140
  18.8 8.2 %all-to-all-start.2 = ((bf16[32,272,128]{2,1,0:T(8,128)(2,1)}), bf16[32,272,128]{2,1,0:T(8,128)(2,1)}, u32[]{:S(2)}, u32[]{:S(2)}) async-start(bf16[32,272,128]{2,1,0:T(8,128)(2,1)} %get-tuple-element.34.after), calls=%async_computation.2 | async-start | bytes 4456448 | tf_op jit(solution)/shard_map/all_to_all | solution.py:488
  27.7 6.0 %broadcast_select_fusion = bf16[72,2,64,128]{3,1,2,0:T(2,128)(2,1)S(1)} fusion(pred[]{:T(512)} %bitcast.10, bf16[72,4,64,128]{3,1,2,0:T(4,128)(2,1)} %bitcast.57), kind=kLoop, calls=%fused_computation.1 | loop fusion | flops 1179648 | bytes 4718593 | tf_op jit(solution)/shard_map/jit(_where)/select_n | solution.py:494
  33.7 1.4 copy-done.20
  35.4 4.4 %collective-permute-done.2.mate = bf16[72,128,128]{2,1,0:T(8,128)(2,1)} collective-permute-done((bf16[72,128,128]{2,1,0:T(8,128)(2,1)S(1)}, bf16[72,128,128]{2,1,0:T(8,128)(2,1)}, u32[]{:S(2)}, u32[]{:S(2)}) %collective-permute-start.2) | collective-permute-done | bytes 2359328 | tf_op jit(solution)/shard_map/ppermute | solution.py:495
  39.7 5.4 %pack.7 = (bf16[32,256,128]{2,1,0:T(8,128)(2,1)}, s32[1]{0:T(128)}) custom-call(s32[2,72]{1,0:T(2,128)S(1)} %add_select_fusion.packed, s32[1]{0:T(128)} %bitcast.3.core_ref.after, bf16[72,128,128]{2,1,0:T(8,128)(2,1)} %bitcast.54, bf16[72,128,128]{2,1,0:T(8,128)(2,1)} %collective-permute-done.2.mate, bf16[32,272,128]{2,1,0:T(8,128)(2,1)} %get-tuple-element.34.after), custom_call_target="tpu_custom_call" | custom-call | bytes 4194304 | tf_op jit(solution)/shard_map/pack/pallas_call | solution.py:140
  45.1 34.3 %all-to-all-done.2.got = bf16[32,272,128]{2,1,0:T(8,128)(2,1)} async-done(((bf16[32,272,128]{2,1,0:T(8,128)(2,1)}), bf16[32,272,128]{2,1,0:T(8,128)(2,1)}, u32[]{:S(2)}, u32[]{:S(2)}) %all-to-all-start.2) | async-done | bytes 2228256 | tf_op jit(solution)/shard_map/all_to_all | solution.py:488
  81.9 5.6 %all-to-all-start.3 = ((bf16[32,256,128]{2,1,0:T(8,128)(2,1)}), bf16[32,256,128]{2,1,0:T(8,128)(2,1)}, u32[]{:S(2)}, u32[]{:S(2)}) async-start(bf16[32,256,128]{2,1,0:T(8,128)(2,1)} %get-tuple-element.39), calls=%async_computation.3 | async-start | bytes 4194304 | tf_op jit(solution)/shard_map/all_to_all | solution.py:488
  88.0 4.4 %collective-permute-start.3 = (s32[8]{0:T(128)S(1)}, s32[8]{0:T(128)S(1)}, u32[]{:S(2)}, u32[]{:S(2)}) collective-permute-start(s32[8]{0:T(128)S(1)} %squeeze.28), channel_id=1, source_target_pairs={{0,7},{1,0},{2,1},{3,2},{4,3},{5,4},{6,5},{7,6},{8,15},{9,8},{10,9... | collective-permute-start | bytes 104 | tf_op jit(solution)/shard_map/ppermute | solution.py:502
  94.6 2.7 %collective-permute-start.6 = (s32[8]{0:T(128)S(1)}, s32[8]{0:T(128)S(1)}, u32[]{:S(2)}, u32[]{:S(2)}) collective-permute-start(s32[8]{0:T(128)S(1)} %squeeze.60), channel_id=1, source_target_pairs={{0,4},{1,5},{2,6},{3,7},{4,0},{5,1},{6,2},{7,3},{8,12},{9,13},{10,... | collective-permute-start | bytes 104 | tf_op jit(solution)/shard_map/ppermute | solution.py:502
  97.6 3.7 %collective-permute-start.8 = (s32[8]{0:T(128)S(1)}, s32[8]{0:T(128)S(1)}, u32[]{:S(2)}, u32[]{:S(2)}) collective-permute-start(s32[8]{0:T(128)S(1)} %squeeze.62), channel_id=1, source_target_pairs={{0,2},{1,3},{2,4},{3,5},{4,6},{5,7},{6,0},{7,1},{8,10},{9,11},{10,... | collective-permute-start | bytes 104 | tf_op jit(solution)/shard_map/ppermute | solution.py:502
  102.1 1.8 collective-permute-done.8
  103.9 3.4 %collective-permute-done.9 = s32[8]{0:T(128)S(1)} collective-permute-done((s32[8]{0:T(128)S(1)}, s32[8]{0:T(128)S(1)}, u32[]{:S(2)}, u32[]{:S(2)}) %collective-permute-start.9) | collective-permute-done | bytes 64 | tf_op jit(solution)/shard_map/ppermute | solution.py:502
  107.9 10.1 %copy.46 = bf16[32,144,128]{0,1,2:T(8,128)(2,1)} copy(bf16[32,144,128]{2,1,0:T(8,128)(2,1)} %get-tuple-element.36.more) | data formatting | bytes 2359296 | tf_op jit(solution)/shard_map/cond | solution.py:518
  119.9 8.4 %whiten.2 = (bf16[24,2,64,128]{3,2,1,0:T(8,128)(2,1)}, bf16[8,8,2,64,128]{4,3,2,1,0:T(8,128)(2,1)}) custom-call(s32[24]{0:T(128)} %get-tuple-element.52.source, s32[24]{0:T(128)} %get-tuple-element.51.length, s32[8,8]{1,0:T(8,128)} %stack.46.picks, bf16[32,272,128]{2,1,0:T(8,128)(2,1)} %all-to-all-done.2.got, bf16[32,144,128]{2,1,0:T(8,128)(2,1)} %get-tuple-element.36.more, ...), custom_call_target="tpu_custom_call" | custom-call | flops 629145600 | bytes 4194304 | tf_op jit(solution)/shard_map/whiten/pallas_call | solution.py:251
  128.3 2.5 %slice_bitcast_fusion = (bf16[8,2,64,128]{3,2,1,0:T(8,128)(2,1)S(1)}, bf16[8,2,64,128]{3,2,1,0:T(8,128)(2,1)}, bf16[8,2,64,128]{3,2,1,0:T(8,128)(2,1)}, bf16[8,2...) fusion(bf16[8,8,2,64,128]{4,3,2,1,0:T(8,128)(2,1)} %get-tuple-e, ...), kind=kLoop, calls=%fused_computation.2 | loop fusion | bytes 3670016 | tf_op jit(solution)/shard_map/squeeze | solution.py:535
  131.4 3.8 %collective-permute-start.12 = (bf16[8,2,64,128]{3,2,1,0:T(8,128)(2,1)}, bf16[8,2,64,128]{3,2,1,0:T(8,128)(2,1)S(1)}, u32[]{:S(2)}, u32[]{:S(2)}) collective-permute-start(bf16[8,2,64,128]{3,2,1,0:T(8,128)(2,1)} %get-tuple-element.57), channel_id=1, source_target_pairs={{0,3},{1,4},{2,5},{3,6},{4,7},{5,0},{6,1},{7,2},{8,11},{9,12},{10,... | collective-permute-start | bytes 786440 | tf_op jit(solution)/shard_map/ppermute | solution.py:535
  136.2 2.3 %collective-permute-start.14 = (bf16[8,2,64,128]{3,2,1,0:T(8,128)(2,1)}, bf16[8,2,64,128]{3,2,1,0:T(8,128)(2,1)S(1)}, u32[]{:S(2)}, u32[]{:S(2)}) collective-permute-start(bf16[8,2,64,128]{3,2,1,0:T(8,128)(2,1)} %get-tuple-element.55), channel_id=1, source_target_pairs={{0,5},{1,6},{2,7},{3,0},{4,1},{5,2},{6,3},{7,4},{8,13},{9,14},{10,... | collective-permute-start | bytes 786440 | tf_op jit(solution)/shard_map/ppermute | solution.py:535
  138.4 14.0 %collective-permute-done.10.refs_0_ = bf16[8,2,64,128]{3,2,1,0:T(8,128)(2,1)S(1)} collective-permute-done((bf16[8,2,64,128]{3,2,1,0:T(8,128)(2,1)S(1)}, bf16[8,2,64,128]{3,2,1,0:T(8,128)(2,1)S(1)}, u32[]{:S(2)}, u32[]{:S(2)}) %collective-permute-start.10) | collective-permute-done | bytes 262176 | tf_op jit(solution)/shard_map/ppermute | solution.py:535
  153.7 7.2 %collective-permute-done.13.refs_3_ = bf16[8,2,64,128]{3,2,1,0:T(8,128)(2,1)S(1)} collective-permute-done((bf16[8,2,64,128]{3,2,1,0:T(8,128)(2,1)}, bf16[8,2,64,128]{3,2,1,0:T(8,128)(2,1)S(1)}, u32[]{:S(2)}, u32[]{:S(2)}) %collective-permute-start.13) | collective-permute-done | bytes 262176 | tf_op jit(solution)/shard_map/ppermute | solution.py:535
  161.9 8.4 %whiten.3 = (bf16[24,2,64,128]{3,2,1,0:T(8,128)(2,1)}, bf16[8,8,2,64,128]{4,3,2,1,0:T(8,128)(2,1)}) custom-call(s32[24]{0:T(128)} %get-tuple-element.52.source, s32[24]{0:T(128)} %get-tuple-element.51.length, s32[8,8]{1,0:T(8,128)} %gather_fusion, bf16[32,256,128]{2,1,0:T(8,128)(2,1)} %all-to-all-done.3.got, ...), custom_call_target="tpu_custom_call" | custom-call | flops 629145600 | bytes 4194304 | tf_op jit(solution)/shard_map/whiten/pallas_call | solution.py:251
  170.4 6.7 %all-to-all-start.4 = ((bf16[8,8,2,64,128]{4,3,2,1,0:T(8,128)(2,1)}), bf16[8,8,2,64,128]{4,3,2,1,0:T(8,128)(2,1)S(1)}, u32[]{:S(2)}, u32[]{:S(2)}) async-start(bf16[8,8,2,64,128]{4,3,2,1,0:T(8,128)(2,1)} %get-tuple-element.42), calls=%async_computation.4 | async-start | bytes 4194304 | tf_op jit(solution)/shard_map/all_to_all | solution.py:539
  178.9 1.6 copy-done.2
  183.5 3.9 %cross_first.1.begun = f32[16384,128]{1,0:T(8,128)S(1)} custom-call(s32[8,8]{1,0:T(8,128)S(1)} %copy.50.near_pick, bf16[24,2,64,128]{3,2,1,0:T(8,128)(2,1)S(1)} %copy-done.18, bf16[8,8,2,64,128]{4,3,2,1,0:T(8,128)(2,1)S(1)} %copy-done.2, bf16[8,2,64,128]{3,2,1,0:T(8,128)(2,1)S(1)} %copy-done.4, bf16[8,2,64,128]{3,2,1,0:T(8,128)(2,1)S(1)} %copy-done.6, ...), custom_call_target="tpu_custom_call" | custom-call | flops 33554432 | bytes 25165824 | tf_op jit(solution)/shard_map/cross_first/pallas_call | solution.py:333
  187.4 3.3 %copy-done = f32[16384,128]{1,0:T(8,128)} copy-done((f32[16384,128]{1,0:T(8,128)}, f32[16384,128]{1,0:T(8,128)S(1)}, u32[]{:S(2)}) %copy-start) | copy-done | bytes 8388632
  190.8 14.9 %all-to-all-done.4.far_in = bf16[8,8,2,64,128]{4,3,2,1,0:T(8,128)(2,1)S(1)} async-done(((bf16[8,8,2,64,128]{4,3,2,1,0:T(8,128)(2,1)}), bf16[8,8,2,64,128]{4,3,2,1,0:T(8,128)(2,1)S(1)}, u32[]{:S(2)}, u32[]{:S(2)}) %all-to-all-start.4) | async-done | bytes 2097184 | tf_op jit(solution)/shard_map/all_to_all | solution.py:539
  205.7 3.4 %copy-done.1 = f32[16384,128]{1,0:T(8,128)S(1)} copy-done((f32[16384,128]{1,0:T(8,128)S(1)}, f32[16384,128]{1,0:T(8,128)}, u32[]{:S(2)}) %copy-start.1) | copy-done | bytes 8388632
  210.9 11.3 %lagged.1 = f32[256,1024]{1,0:T(8,128)S(1)} custom-call(s32[8,8]{1,0:T(8,128)S(1)} %copy.50.near_pick, s32[8]{0:T(128)S(1)} %and_select_fusion.1.far_at, f32[16384,128]{1,0:T(8,128)S(1)} %copy-done.1, bf16[24,2,64,128]{3,2,1,0:T(8,128)(2,1)S(1)} %copy-done.17, bf16[8,8,2,64,128]{4,3,2,1,0:T(8,128)(2,1)S(1)} %all-to-all-done.4.far_in, ...), custom_call_target="tpu_custom_call" | custom-call | flops 2147483648 | bytes 25165824 | tf_op jit(solution)/shard_map/lagged/pallas_call | solution.py:436
  222.2 1.3 reshape.149
  (112 shorter events, 19.3 us)
Async XLA Ops:
  0.0 7.8 %copy-start.26 = (s32[1,72]{1,0:T(1,128)S(1)}, s32[1,72]{1,0:T(1,128)}, u32[]{:S(2)}) copy-start(s32[1,72]{1,0:T(1,128)} %param.15) | copy-start | bytes 868
  0.0 7.8 %copy-start.27 = (s32[1,72]{1,0:T(1,128)S(1)}, s32[1,72]{1,0:T(1,128)}, u32[]{:S(2)}) copy-start(s32[1,72]{1,0:T(1,128)} %param.14) | copy-start | bytes 868
  4.5 7.6 %collective-permute-start.1 = (bf16[72,128,128]{2,1,0:T(8,128)(2,1)S(1)}, bf16[72,128,128]{2,1,0:T(8,128)(2,1)}, u32[]{:S(2)}, u32[]{:S(2)}) collective-permute-start(bf16[72,128,128]{2,1,0:T(8,128)(2,1)S(1)} %bitcast.50), channel_id=1, source_target_pairs={{0,8},{8,0},{16,24},{24,16},{32,40},{40,32},{48,56},{56,48},{64,72... | collective-permute-start | bytes 7077896 | tf_op jit(solution)/shard_map/ppermute | solution.py:491
  7.8 4.0 %collective-permute-start = (s32[72]{0:T(128)S(1)}, s32[72]{0:T(128)S(1)}, u32[]{:S(2)}, u32[]{:S(2)}) collective-permute-start(s32[72]{0:T(128)S(1)} %bitcast.68), channel_id=1, source_target_pairs={{0,8},{8,0},{16,24},{24,16},{32,40},{40,32},{48,56},{56,48},{64,72... | collective-permute-start | bytes 872 | tf_op jit(solution)/shard_map/ppermute | solution.py:478
  18.8 60.5 %all-to-all-start.2 = ((bf16[32,272,128]{2,1,0:T(8,128)(2,1)}), bf16[32,272,128]{2,1,0:T(8,128)(2,1)}, u32[]{:S(2)}, u32[]{:S(2)}) async-start(bf16[32,272,128]{2,1,0:T(8,128)(2,1)} %get-tuple-element.34.after), calls=%async_computation.2 | async-start | bytes 4456448 | tf_op jit(solution)/shard_map/all_to_all | solution.py:488
  35.1 4.7 %collective-permute-start.2 = (bf16[72,128,128]{2,1,0:T(8,128)(2,1)S(1)}, bf16[72,128,128]{2,1,0:T(8,128)(2,1)}, u32[]{:S(2)}, u32[]{:S(2)}) collective-permute-start(bf16[72,128,128]{2,1,0:T(8,128)(2,1)S(1)} %bitcast.53), channel_id=1, source_target_pairs={{0,8},{8,0},{16,24},{24,16},{32,40},{40,32},{48,56},{56,48},{64,72... | collective-permute-start | bytes 7077896 | tf_op jit(solution)/shard_map/ppermute | solution.py:495
  81.9 79.1 %all-to-all-start.3 = ((bf16[32,256,128]{2,1,0:T(8,128)(2,1)}), bf16[32,256,128]{2,1,0:T(8,128)(2,1)}, u32[]{:S(2)}, u32[]{:S(2)}) async-start(bf16[32,256,128]{2,1,0:T(8,128)(2,1)} %get-tuple-element.39), calls=%async_computation.3 | async-start | bytes 4194304 | tf_op jit(solution)/shard_map/all_to_all | solution.py:488
  88.0 9.6 %collective-permute-start.3 = (s32[8]{0:T(128)S(1)}, s32[8]{0:T(128)S(1)}, u32[]{:S(2)}, u32[]{:S(2)}) collective-permute-start(s32[8]{0:T(128)S(1)} %squeeze.28), channel_id=1, source_target_pairs={{0,7},{1,0},{2,1},{3,2},{4,3},{5,4},{6,5},{7,6},{8,15},{9,8},{10,9... | collective-permute-start | bytes 104 | tf_op jit(solution)/shard_map/ppermute | solution.py:502
  92.5 8.7 %collective-permute-start.4 = (s32[8]{0:T(128)S(1)}, s32[8]{0:T(128)S(1)}, u32[]{:S(2)}, u32[]{:S(2)}) collective-permute-start(s32[8]{0:T(128)S(1)} %squeeze.58), channel_id=1, source_target_pairs={{0,6},{1,7},{2,0},{3,1},{4,2},{5,3},{6,4},{7,5},{8,14},{9,15},{10,... | collective-permute-start | bytes 104 | tf_op jit(solution)/shard_map/ppermute | solution.py:502
  93.8 7.4 %collective-permute-start.5 = (s32[8]{0:T(128)S(1)}, s32[8]{0:T(128)S(1)}, u32[]{:S(2)}, u32[]{:S(2)}) collective-permute-start(s32[8]{0:T(128)S(1)} %squeeze.59), channel_id=1, source_target_pairs={{0,5},{1,6},{2,7},{3,0},{4,1},{5,2},{6,3},{7,4},{8,13},{9,14},{10,... | collective-permute-start | bytes 104 | tf_op jit(solution)/shard_map/ppermute | solution.py:502
  94.6 6.7 %collective-permute-start.6 = (s32[8]{0:T(128)S(1)}, s32[8]{0:T(128)S(1)}, u32[]{:S(2)}, u32[]{:S(2)}) collective-permute-start(s32[8]{0:T(128)S(1)} %squeeze.60), channel_id=1, source_target_pairs={{0,4},{1,5},{2,6},{3,7},{4,0},{5,1},{6,2},{7,3},{8,12},{9,13},{10,... | collective-permute-start | bytes 104 | tf_op jit(solution)/shard_map/ppermute | solution.py:502
  97.3 4.8 %collective-permute-start.7 = (s32[8]{0:T(128)S(1)}, s32[8]{0:T(128)S(1)}, u32[]{:S(2)}, u32[]{:S(2)}) collective-permute-start(s32[8]{0:T(128)S(1)} %squeeze.61), channel_id=1, source_target_pairs={{0,3},{1,4},{2,5},{3,6},{4,7},{5,0},{6,1},{7,2},{8,11},{9,12},{10,... | collective-permute-start | bytes 104 | tf_op jit(solution)/shard_map/ppermute | solution.py:502
  97.6 6.3 %collective-permute-start.8 = (s32[8]{0:T(128)S(1)}, s32[8]{0:T(128)S(1)}, u32[]{:S(2)}, u32[]{:S(2)}) collective-permute-start(s32[8]{0:T(128)S(1)} %squeeze.62), channel_id=1, source_target_pairs={{0,2},{1,3},{2,4},{3,5},{4,6},{5,7},{6,0},{7,1},{8,10},{9,11},{10,... | collective-permute-start | bytes 104 | tf_op jit(solution)/shard_map/ppermute | solution.py:502
  101.3 6.0 %collective-permute-start.9 = (s32[8]{0:T(128)S(1)}, s32[8]{0:T(128)S(1)}, u32[]{:S(2)}, u32[]{:S(2)}) collective-permute-start(s32[8]{0:T(128)S(1)} %squeeze.63), channel_id=1, source_target_pairs={{0,1},{1,2},{2,3},{3,4},{4,5},{5,6},{6,7},{7,0},{8,9},{9,10},{10,1... | collective-permute-start | bytes 104 | tf_op jit(solution)/shard_map/ppermute | solution.py:502
  128.3 24.3 %copy-start.22 = (s32[8,8]{1,0:T(8,128)S(1)}, s32[8,8]{1,0:T(8,128)}, u32[]{:S(2)}) copy-start(s32[8,8]{1,0:T(8,128)} %stack.46.picks) | copy-start | bytes 772
  130.8 21.6 %collective-permute-start.10 = (bf16[8,2,64,128]{3,2,1,0:T(8,128)(2,1)S(1)}, bf16[8,2,64,128]{3,2,1,0:T(8,128)(2,1)S(1)}, u32[]{:S(2)}, u32[]{:S(2)}) collective-permute-start(bf16[8,2,64,128]{3,2,1,0:T(8,128)(2,1)S(1)} %get-tuple-element.59), channel_id=1, source_target_pairs={{0,1},{1,2},{2,3},{3,4},{4,5},{5,6},{6,7},{7,0},{8,9},{9,10},{10,1... | collective-permute-start | bytes 786440 | tf_op jit(solution)/shard_map/ppermute | solution.py:535
  130.8 21.6 %collective-permute-start.11 = (bf16[8,2,64,128]{3,2,1,0:T(8,128)(2,1)S(1)}, bf16[8,2,64,128]{3,2,1,0:T(8,128)(2,1)S(1)}, u32[]{:S(2)}, u32[]{:S(2)}) collective-permute-start(bf16[8,2,64,128]{3,2,1,0:T(8,128)(2,1)S(1)} %get-tuple-element.58), channel_id=1, source_target_pairs={{0,2},{1,3},{2,4},{3,5},{4,6},{5,7},{6,0},{7,1},{8,10},{9,11},{10,... | collective-permute-start | bytes 786440 | tf_op jit(solution)/shard_map/ppermute | solution.py:535
  131.4 22.3 %collective-permute-start.12 = (bf16[8,2,64,128]{3,2,1,0:T(8,128)(2,1)}, bf16[8,2,64,128]{3,2,1,0:T(8,128)(2,1)S(1)}, u32[]{:S(2)}, u32[]{:S(2)}) collective-permute-start(bf16[8,2,64,128]{3,2,1,0:T(8,128)(2,1)} %get-tuple-element.57), channel_id=1, source_target_pairs={{0,3},{1,4},{2,5},{3,6},{4,7},{5,0},{6,1},{7,2},{8,11},{9,12},{10,... | collective-permute-start | bytes 786440 | tf_op jit(solution)/shard_map/ppermute | solution.py:535
  135.2 25.8 %collective-permute-start.13 = (bf16[8,2,64,128]{3,2,1,0:T(8,128)(2,1)}, bf16[8,2,64,128]{3,2,1,0:T(8,128)(2,1)S(1)}, u32[]{:S(2)}, u32[]{:S(2)}) collective-permute-start(bf16[8,2,64,128]{3,2,1,0:T(8,128)(2,1)} %get-tuple-element.56), channel_id=1, source_target_pairs={{0,4},{1,5},{2,6},{3,7},{4,0},{5,1},{6,2},{7,3},{8,12},{9,13},{10,... | collective-permute-start | bytes 786440 | tf_op jit(solution)/shard_map/ppermute | solution.py:535
  136.2 24.8 %collective-permute-start.14 = (bf16[8,2,64,128]{3,2,1,0:T(8,128)(2,1)}, bf16[8,2,64,128]{3,2,1,0:T(8,128)(2,1)S(1)}, u32[]{:S(2)}, u32[]{:S(2)}) collective-permute-start(bf16[8,2,64,128]{3,2,1,0:T(8,128)(2,1)} %get-tuple-element.55), channel_id=1, source_target_pairs={{0,5},{1,6},{2,7},{3,0},{4,1},{5,2},{6,3},{7,4},{8,13},{9,14},{10,... | collective-permute-start | bytes 786440 | tf_op jit(solution)/shard_map/ppermute | solution.py:535
  152.4 8.6 %copy-start.3 = (bf16[8,2,64,128]{3,2,1,0:T(8,128)(2,1)}, bf16[8,2,64,128]{3,2,1,0:T(8,128)(2,1)S(1)}, u32[]{:S(2)}) copy-start(bf16[8,2,64,128]{3,2,1,0:T(8,128)(2,1)S(1)} %collective-permute-done.10.refs_0_) | copy-start | bytes 786436
  152.4 8.6 %collective-permute-start.15 = (bf16[8,2,64,128]{3,2,1,0:T(8,128)(2,1)}, bf16[8,2,64,128]{3,2,1,0:T(8,128)(2,1)S(1)}, u32[]{:S(2)}, u32[]{:S(2)}) collective-permute-start(bf16[8,2,64,128]{3,2,1,0:T(8,128)(2,1)} %get-tuple-element.54), channel_id=1, source_target_pairs={{0,6},{1,7},{2,0},{3,1},{4,2},{5,3},{6,4},{7,5},{8,14},{9,15},{10,... | collective-permute-start | bytes 786440 | tf_op jit(solution)/shard_map/ppermute | solution.py:535
  152.4 8.6 %copy-start.5 = (bf16[8,2,64,128]{3,2,1,0:T(8,128)(2,1)}, bf16[8,2,64,128]{3,2,1,0:T(8,128)(2,1)S(1)}, u32[]{:S(2)}) copy-start(bf16[8,2,64,128]{3,2,1,0:T(8,128)(2,1)S(1)} %collective-permute-done.11.refs_1_) | copy-start | bytes 786436
  152.4 8.6 %collective-permute-start.16 = (bf16[8,2,64,128]{3,2,1,0:T(8,128)(2,1)S(1)}, bf16[8,2,64,128]{3,2,1,0:T(8,128)(2,1)S(1)}, u32[]{:S(2)}, u32[]{:S(2)}) collective-permute-start(bf16[8,2,64,128]{3,2,1,0:T(8,128)(2,1)S(1)} %get-tuple-element.53), channel_id=1, source_target_pairs={{0,7},{1,0},{2,1},{3,2},{4,3},{5,4},{6,5},{7,6},{8,15},{9,8},{10,9... | collective-permute-start | bytes 786440 | tf_op jit(solution)/shard_map/ppermute | solution.py:535
  153.7 7.3 %copy-start.7 = (bf16[8,2,64,128]{3,2,1,0:T(8,128)(2,1)}, bf16[8,2,64,128]{3,2,1,0:T(8,128)(2,1)S(1)}, u32[]{:S(2)}) copy-start(bf16[8,2,64,128]{3,2,1,0:T(8,128)(2,1)S(1)} %collective-permute-done.12.refs_2_) | copy-start | bytes 786436
  170.4 6.8 %copy-start.23 = (s32[1,1,8,2,4,4]{2,5,4,3,1,0:T(4,128)S(1)}, s32[1,1,8,2,4,4]{2,5,4,3,1,0:T(4,128)}, u32[]{:S(2)}) copy-start(s32[1,1,8,2,4,4]{2,5,4,3,1,0:T(4,128)} %param.18) | copy-start | bytes 3076
  170.4 8.4 %copy-start.4 = (bf16[8,2,64,128]{3,2,1,0:T(8,128)(2,1)S(1)}, bf16[8,2,64,128]{3,2,1,0:T(8,128)(2,1)}, u32[]{:S(2)}) copy-start(bf16[8,2,64,128]{3,2,1,0:T(8,128)(2,1)} %copy-done.3) | copy-start | bytes 786436
  170.4 8.4 %copy-start.6 = (bf16[8,2,64,128]{3,2,1,0:T(8,128)(2,1)S(1)}, bf16[8,2,64,128]{3,2,1,0:T(8,128)(2,1)}, u32[]{:S(2)}) copy-start(bf16[8,2,64,128]{3,2,1,0:T(8,128)(2,1)} %copy-done.5) | copy-start | bytes 786436
  170.4 8.4 %copy-start.8 = (bf16[8,2,64,128]{3,2,1,0:T(8,128)(2,1)S(1)}, bf16[8,2,64,128]{3,2,1,0:T(8,128)(2,1)}, u32[]{:S(2)}) copy-start(bf16[8,2,64,128]{3,2,1,0:T(8,128)(2,1)} %copy-done.7) | copy-start | bytes 786436
  170.4 8.4 %copy-start.10 = (bf16[8,2,64,128]{3,2,1,0:T(8,128)(2,1)S(1)}, bf16[8,2,64,128]{3,2,1,0:T(8,128)(2,1)}, u32[]{:S(2)}) copy-start(bf16[8,2,64,128]{3,2,1,0:T(8,128)(2,1)} %copy-done.9) | copy-start | bytes 786436
  170.4 8.4 %copy-start.12 = (bf16[8,2,64,128]{3,2,1,0:T(8,128)(2,1)S(1)}, bf16[8,2,64,128]{3,2,1,0:T(8,128)(2,1)}, u32[]{:S(2)}) copy-start(bf16[8,2,64,128]{3,2,1,0:T(8,128)(2,1)} %copy-done.11) | copy-start | bytes 786436
  170.4 35.2 %all-to-all-start.4 = ((bf16[8,8,2,64,128]{4,3,2,1,0:T(8,128)(2,1)}), bf16[8,8,2,64,128]{4,3,2,1,0:T(8,128)(2,1)S(1)}, u32[]{:S(2)}, u32[]{:S(2)}) async-start(bf16[8,8,2,64,128]{4,3,2,1,0:T(8,128)(2,1)} %get-tuple-element.42), calls=%async_computation.4 | async-start | bytes 4194304 | tf_op jit(solution)/shard_map/all_to_all | solution.py:539
  (15 other events, 30.3 us)

commit v5 on v4

--- a/solution.py
+++ b/solution.py
@@ -20,6 +20,7 @@
 EXTRA = 1
 LEN_BITS = 16
 NOTES = 16
+ALL_VMEM = 60 * 1024 * 1024
 SMEM = pl.BlockSpec(memory_space=pltpu.SMEM)
 VMEM = pl.BlockSpec(memory_space=pltpu.VMEM)
 ANY = pl.BlockSpec(memory_space=pl.ANY)
@@ -168,7 +169,7 @@
     white, payload, held, spectra, sem, sems = refs[-6:]
     stations = held.shape[0]
     first_more = got.shape[0] * BASE
-    batch = 4
+    batch = 8
 
     @pl.loop(0, stations)
     def _(station):
@@ -260,7 +261,7 @@
             pltpu.VMEM((ST_DEV, 2 * ROWS, LANES), jnp.bfloat16),
             pltpu.VMEM((ST_DEV, 2, ROWS, LANES), jnp.bfloat16),
             pltpu.SemaphoreType.DMA,
-            pltpu.SemaphoreType.DMA((ST_DEV // 4,)),
+            pltpu.SemaphoreType.DMA((ST_DEV // 8,)),
         ],
         cost_estimate=pl.CostEstimate(
             flops=2 * ST_DEV * 2 * ROWS * 256 * 400, bytes_accessed=4 * 1024 * 1024, transcendentals=0
@@ -343,7 +344,7 @@
             pltpu.SemaphoreType.DMA((stops,)),
             pltpu.SemaphoreType.DMA,
         ],
-        compiler_params=pltpu.CompilerParams(vmem_limit_bytes=20 * 1024 * 1024),
+        compiler_params=pltpu.CompilerParams(vmem_limit_bytes=ALL_VMEM),
         cost_estimate=pl.CostEstimate(
             flops=pairs * ROWS * LANES * 16, bytes_accessed=24 * 1024 * 1024, transcendentals=0
         ),
@@ -447,7 +448,7 @@
             pltpu.SemaphoreType.DMA((2, stops)),
             pltpu.SemaphoreType.DMA,
         ],
-        compiler_params=pltpu.CompilerParams(vmem_limit_bytes=40 * 1024 * 1024),
+        compiler_params=pltpu.CompilerParams(vmem_limit_bytes=ALL_VMEM),
         cost_estimate=pl.CostEstimate(
             flops=2 * pairs * NF * LAGS, bytes_accessed=24 * 1024 * 1024, transcendentals=0
         ),
@@ -493,8 +494,6 @@
     got_a = send(load_a)
     own_b = jnp.where(flag_a[0] >= 0, halves(1), 0.0)
     mate_b = lax.ppermute(own_b, "wide", swap)
-    load_b, flag_b = pack(0, BASE, False, wide_count, chip_packed, core_at, own_b, mate_b, load_a)
-    got_b = send(load_b)
     visits = jnp.where(flag_a[0] >= 0, visit_pick[0, 0].reshape(stops, -1), 0)
     by_stop = jnp.stack(
         [visits[0]]
@@ -503,6 +502,8 @@
             for stop in range(1, stops)
         ]
     )
+    load_b, _ = pack(0, BASE, False, wide_count, chip_packed, core_at, own_b, mate_b, by_stop)
+    got_b = send(load_b)
     by_dest = by_stop[(steps - group) % stops]
 
     station, length, spilled = read_notes(got_a, BASE)
@@ -510,19 +511,19 @@
 
     def late():
         rows = [
-            pack(BASE, EXTRA, True, wide_count, chip_packed, core_at, own, mate, core_at)[0]
+            send(pack(BASE, EXTRA, True, wide_count, chip_packed, core_at, own, mate, core_at)[0])
             for own, mate in ((own_a, mate_a), (own_b, mate_b))
         ]
-        return tuple(send(row) for row in rows)
-
-    more = lax.cond(
-        spilled,
-        late,
-        lambda: tuple(empty((wide_count, EXTRA * 2 * ROWS + NOTES, LANES)) for _ in range(2)),
-    )
-    more_station, more_length, _ = read_notes(more[0], EXTRA)
-    station = jnp.concatenate([station.reshape(-1), jnp.where(spilled, more_station.reshape(-1), -1)])
-    length = jnp.concatenate([length.reshape(-1), more_length.reshape(-1)])
+        more_station, more_length, _ = read_notes(rows[0], EXTRA)
+        return rows[0], rows[1], more_station.reshape(-1), more_length.reshape(-1)
+
+    def never():
+        rows = [empty((wide_count, EXTRA * 2 * ROWS + NOTES, LANES)) for _ in range(2)]
+        return rows[0], rows[1], jnp.full((wide_count * EXTRA,), -1), jnp.zeros((wide_count * EXTRA,), jnp.int32)
+
+    more_a, more_b, more_station, more_length = lax.cond(spilled, late, never)
+    station = jnp.concatenate([station.reshape(-1), more_station])
+    length = jnp.concatenate([length.reshape(-1), more_length])
     chosen = station[None, :] == jnp.arange(ST_DEV, dtype=jnp.int32)[:, None]
     codes = jnp.arange(station.shape[0], dtype=jnp.int32)
     source = jnp.sum(jnp.where(chosen, codes[None], 0), axis=1)
@@ -530,12 +531,12 @@
 
     tables = [jnp.asarray(table) for table in transform_tables()]
     near_pick = own_pick[0, 0].reshape(stops, -1)
-    white_a, payload_a = whiten(0, source, length, by_stop, got_a, more[0], tables, [])
+    white_a, payload_a = whiten(0, source, length, by_stop, got_a, more_a, tables, [])
     far_a = [
         lax.ppermute(payload_a[stop], "blk", [(i, (i + stop) % stops) for i in range(stops)])
         for stop in range(1, stops)
     ]
-    white_b, payload_b = whiten(1, source, length, by_dest, got_b, more[1], tables, far_a)
+    white_b, payload_b = whiten(1, source, length, by_dest, got_b, more_b, tables, far_a)
     far_b = lax.all_to_all(payload_b, "blk", split_axis=0, concat_axis=0, tiled=True)
 
     begun = cross_first(near_pick, white_a, payload_a, far_a)

time: 225 us -> 207 us (0.920)
  local copies, waits for them, and re-layouts: 39 us -> 17.2 us
  waiting for transfers between devices: 84.9 us -> 74.8 us
  Pallas kernels: 44.2 us -> 51.1 us
  starting transfers between devices: 44.6 us -> 50.7 us
    all_to_all x2, waiting for transfers between devices: 34.3 us -> 18.2 us  [send(): lax.all_to_all(payload, 'wide', split_axis=0, concat_axis=0, tiled=True)]
    unnamed x54 -> x26, local copies, waits for them, and re-layouts: 15.5 us -> 2.73 us
    cond x1 -> x0, local copies, waits for them, and re-layouts: 10.1 us -> none  [on_device(): lax.cond(spilled, late, lambda: tuple((empty((wide_count, EXTRA * 2 * ROW...]
    ppermute x7, starting transfers between devices: 7.74 us -> 17.1 us  [on_device(): lax.ppermute(payload_a[stop], 'blk', [(i, (i + stop) % stops) for i in ra...]
    ppermute x7, waiting for transfers between devices: 21.2 us -> 28.6 us  [on_device(): lax.ppermute(payload_a[stop], 'blk', [(i, (i + stop) % stops) for i in ra...]
    ppermute x1, waiting for transfers between devices: 4.36 us -> 0.01 us  [on_device(): mate_b = lax.ppermute(own_b, 'wide', swap)]
    pallas_call x1, Pallas kernels: 3.93 us -> 8.22 us  [cross_first(): pl.pallas_call(functools.partial(cross_kernel, stops), out_shape=jax.Shap...]
    pallas_call x1, Pallas kernels: 11.3 us -> 15.4 us  [lagged(): pl.pallas_call(lag_kernel, out_shape=jax.ShapeDtypeStruct((pairs, LAGS),...]
  transfers between devices with their start and end apart: 20 -> 20, of which waited for: 10 -> 10; matrix products, arithmetic and copies ran while one was open for 11% -> 8% of each run, Pallas kernels for 8% -> 10%
where the time goes in v5:
time: 207 us; the launch traced here: 206 us
  waiting for transfers between devices  74.8 us (36%)
  Pallas kernels  51.1 us (25%)
  starting transfers between devices  50.7 us (24%)
  local copies, waits for them, and re-layouts  17.2 us (8%)
  other arithmetic  10.5 us (5%)
    ppermute x7, waiting for transfers between devices, on_device(): lax.ppermute(payload_a[stop], 'blk', [(i, (i + stop) % stops) for i in ra...  28.6 us
    all_to_all x2, waiting for transfers between devices, send(): lax.all_to_all(payload, 'wide', split_axis=0, concat_axis=0, tiled=True)  18.2 us
    all_to_all x1, waiting for transfers between devices, on_device(): lax.all_to_all(payload_b, 'blk', split_axis=0, concat_axis=0, tiled=True)  17.9 us
    ppermute x7, starting transfers between devices, on_device(): lax.ppermute(payload_a[stop], 'blk', [(i, (i + stop) % stops) for i in ra...  17.1 us
    pallas_call x1, Pallas kernels, lagged(): pl.pallas_call(lag_kernel, out_shape=jax.ShapeDtypeStruct((pairs, LAGS),...  15.4 us
    pallas_call x2, Pallas kernels, whiten(): pl.pallas_call(functools.partial(whiten_kernel, part), out_shape=(jax.Sha...  15.1 us
    all_to_all x2, starting transfers between devices, send(): lax.all_to_all(payload, 'wide', split_axis=0, concat_axis=0, tiled=True)  13.5 us
    pallas_call x2, Pallas kernels, pack(): pl.pallas_call(functools.partial(pack_kernel, low, count, noted), out_sha...  12.5 us
  transfers between devices with their start and end apart: 20, of which 10 were waited for; matrix products, arithmetic and copies ran while one was open for 8% of the time, Pallas kernels for 10%

profile of v5, /device:TPU:1, one launch (start us, length us, event | category | flops | bytes accessed | tf_op | source)
XLA Modules:
  0.0 205.9 jit_solution(2987238846608096845)
XLA Ops:
  0.0 4.5 %slice.122 = bf16[72,2,64,128]{3,1,2,0:T(2,128)(2,1)S(1)} slice(bf16[72,4,64,128]{3,1,2,0:T(4,128)(2,1)} %bitcast.52), slice={[0:72], [0:2], [0:64], [0:128]} | slice | bytes 4718592 | tf_op jit(solution)/shard_map/slice | solution.py:486
  4.5 3.3 %collective-permute-start.1 = (bf16[72,128,128]{2,1,0:T(8,128)(2,1)S(1)}, bf16[72,128,128]{2,1,0:T(8,128)(2,1)}, u32[]{:S(2)}, u32[]{:S(2)}) collective-permute-start(bf16[72,128,128]{2,1,0:T(8,128)(2,1)S(1)} %bitcast.49), channel_id=1, source_target_pairs={{0,8},{8,0},{16,24},{24,16},{32,40},{40,32},{48,56},{56,48},{64,72... | collective-permute-start | bytes 7077896 | tf_op jit(solution)/shard_map/ppermute | solution.py:492
  8.0 3.9 %collective-permute-done = s32[72]{0:T(128)S(1)} collective-permute-done((s32[72]{0:T(128)S(1)}, s32[72]{0:T(128)S(1)}, u32[]{:S(2)}, u32[]{:S(2)}) %collective-permute-start) | collective-permute-done | bytes 320 | tf_op jit(solution)/shard_map/ppermute | solution.py:479
  12.1 7.0 %pack.6 = (bf16[32,272,128]{2,1,0:T(8,128)(2,1)}, s32[1]{0:T(128)}) custom-call(s32[2,72]{1,0:T(2,128)S(1)} %add_select_fusion.packed, s32[1]{0:T(128)} %bitcast.7.core_ref.after, bf16[72,128,128]{2,1,0:T(8,128)(2,1)S(1)} %bitcast.50, bf16[72,128,128]{2,1,0:T(8,128)(2,1)} %collective-permute-done.1.mate, s32[1]{0:T(128)} %bitcast.7.core_ref.after), custom_call_target="tpu_custom_call" | custom-call | bytes 4194304 | tf_op jit(solution)/shard_map/pack/pallas_call | solution.py:141
  19.1 8.0 %all-to-all-start.2 = ((bf16[32,272,128]{2,1,0:T(8,128)(2,1)}), bf16[32,272,128]{2,1,0:T(8,128)(2,1)}, u32[]{:S(2)}, u32[]{:S(2)}) async-start(bf16[32,272,128]{2,1,0:T(8,128)(2,1)} %get-tuple-element.36), calls=%async_computation.2 | async-start | bytes 4456448 | tf_op jit(solution)/shard_map/all_to_all | solution.py:489
  27.8 7.4 %broadcast_select_fusion = bf16[72,2,64,128]{3,1,2,0:T(2,128)(2,1)} fusion(pred[]{:T(512)} %bitcast.14, bf16[72,4,64,128]{3,1,2,0:T(4,128)(2,1)} %bitcast.53), kind=kLoop, calls=%fused_computation.5 | loop fusion | flops 1179648 | bytes 4718593 | tf_op jit(solution)/shard_map/jit(_where)/select_n | solution.py:495
  36.6 4.5 %collective-permute-start.3 = (s32[8]{0:T(128)S(1)}, s32[8]{0:T(128)S(1)}, u32[]{:S(2)}, u32[]{:S(2)}) collective-permute-start(s32[8]{0:T(128)S(1)} %squeeze.32), channel_id=1, source_target_pairs={{0,7},{1,0},{2,1},{3,2},{4,3},{5,4},{6,5},{7,6},{8,15},{9,8},{10,9... | collective-permute-start | bytes 104 | tf_op jit(solution)/shard_map/ppermute | solution.py:501
  42.6 3.1 %collective-permute-start.6 = (s32[8]{0:T(128)S(1)}, s32[8]{0:T(128)S(1)}, u32[]{:S(2)}, u32[]{:S(2)}) collective-permute-start(s32[8]{0:T(128)S(1)} %squeeze.60), channel_id=1, source_target_pairs={{0,4},{1,5},{2,6},{3,7},{4,0},{5,1},{6,2},{7,3},{8,12},{9,13},{10,... | collective-permute-start | bytes 104 | tf_op jit(solution)/shard_map/ppermute | solution.py:501
  45.7 3.4 %collective-permute-start.8 = (s32[8]{0:T(128)S(1)}, s32[8]{0:T(128)S(1)}, u32[]{:S(2)}, u32[]{:S(2)}) collective-permute-start(s32[8]{0:T(128)S(1)} %squeeze.62), channel_id=1, source_target_pairs={{0,2},{1,3},{2,4},{3,5},{4,6},{5,7},{6,0},{7,1},{8,10},{9,11},{10,... | collective-permute-start | bytes 104 | tf_op jit(solution)/shard_map/ppermute | solution.py:501
  49.1 1.8 collective-permute-done.7
  50.9 1.2 collective-permute-done.8
  52.1 3.0 %collective-permute-done.9 = s32[8]{0:T(128)S(1)} collective-permute-done((s32[8]{0:T(128)S(1)}, s32[8]{0:T(128)S(1)}, u32[]{:S(2)}, u32[]{:S(2)}) %collective-permute-start.9) | collective-permute-done | bytes 64 | tf_op jit(solution)/shard_map/ppermute | solution.py:501
  55.7 5.5 %pack.7 = (bf16[32,256,128]{2,1,0:T(8,128)(2,1)}, s32[1]{0:T(128)}) custom-call(s32[2,72]{1,0:T(2,128)S(1)} %add_select_fusion.packed, s32[1]{0:T(128)} %bitcast.7.core_ref.after, bf16[72,128,128]{2,1,0:T(8,128)(2,1)} %bitcast.16.own, bf16[72,128,128]{2,1,0:T(8,128)(2,1)} %collective-permute-done.2.mate, s32[8,8]{1,0:T(8,128)} %stack.46.picks.after), custom_call_target="tpu_custom_call" | custom-call | bytes 4194304 | tf_op jit(solution)/shard_map/pack/pallas_call | solution.py:141
  61.2 18.2 %all-to-all-done.2.got = bf16[32,272,128]{2,1,0:T(8,128)(2,1)} async-done(((bf16[32,272,128]{2,1,0:T(8,128)(2,1)}), bf16[32,272,128]{2,1,0:T(8,128)(2,1)}, u32[]{:S(2)}, u32[]{:S(2)}) %all-to-all-start.2) | async-done | bytes 2228256 | tf_op jit(solution)/shard_map/all_to_all | solution.py:489
  82.0 5.5 %all-to-all-start.3 = ((bf16[32,256,128]{2,1,0:T(8,128)(2,1)}), bf16[32,256,128]{2,1,0:T(8,128)(2,1)S(1)}, u32[]{:S(2)}, u32[]{:S(2)}) async-start(bf16[32,256,128]{2,1,0:T(8,128)(2,1)} %get-tuple-element.43), calls=%async_computation.3 | async-start | bytes 4194304 | tf_op jit(solution)/shard_map/all_to_all | solution.py:489
  88.7 7.5 %whiten.2 = (bf16[24,2,64,128]{3,2,1,0:T(8,128)(2,1)}, bf16[8,8,2,64,128]{4,3,2,1,0:T(8,128)(2,1)}) custom-call(s32[24]{0:T(128)} %get-tuple-element.56.source, s32[24]{0:T(128)} %get-tuple-element.55.length, s32[8,8]{1,0:T(8,128)} %stack.46.picks.after, bf16[32,272,128]{2,1,0:T(8,128)(2,1)} %all-to-all-done.2.got, ...), custom_call_target="tpu_custom_call" | custom-call | flops 629145600 | bytes 4194304 | tf_op jit(solution)/shard_map/whiten/pallas_call | solution.py:252
  96.2 2.5 %slice_bitcast_fusion.1 = (bf16[8,2,64,128]{3,2,1,0:T(8,128)(2,1)S(1)}, bf16[8,2,64,128]{3,2,1,0:T(8,128)(2,1)S(1)}, bf16[8,2,64,128]{3,2,1,0:T(8,128)(2,1)}, bf...) fusion(bf16[8,8,2,64,128]{4,3,2,1,0:T(8,128)(2,1)} %get-tuple-e, ...), kind=kLoop, calls=%fused_computation.6 | loop fusion | bytes 3670016 | tf_op jit(solution)/shard_map/squeeze | solution.py:536
  98.7 4.5 %collective-permute-start.16 = (bf16[8,2,64,128]{3,2,1,0:T(8,128)(2,1)S(1)}, bf16[8,2,64,128]{3,2,1,0:T(8,128)(2,1)S(1)}, u32[]{:S(2)}, u32[]{:S(2)}) collective-permute-start(bf16[8,2,64,128]{3,2,1,0:T(8,128)(2,1)S(1)} %get-tuple-element.59), channel_id=1, source_target_pairs={{0,7},{1,0},{2,1},{3,2},{4,3},{5,4},{6,5},{7,6},{8,15},{9,8},{10,9... | collective-permute-start | bytes 786440 | tf_op jit(solution)/shard_map/ppermute | solution.py:536
  104.6 3.1 %collective-permute-start.13 = (bf16[8,2,64,128]{3,2,1,0:T(8,128)(2,1)}, bf16[8,2,64,128]{3,2,1,0:T(8,128)(2,1)S(1)}, u32[]{:S(2)}, u32[]{:S(2)}) collective-permute-start(bf16[8,2,64,128]{3,2,1,0:T(8,128)(2,1)} %get-tuple-element.62), channel_id=1, source_target_pairs={{0,4},{1,5},{2,6},{3,7},{4,0},{5,1},{6,2},{7,3},{8,12},{9,13},{10,... | collective-permute-start | bytes 786440 | tf_op jit(solution)/shard_map/ppermute | solution.py:536
  107.7 14.6 %collective-permute-done.16.refs_6_ = bf16[8,2,64,128]{3,2,1,0:T(8,128)(2,1)S(1)} collective-permute-done((bf16[8,2,64,128]{3,2,1,0:T(8,128)(2,1)S(1)}, bf16[8,2,64,128]{3,2,1,0:T(8,128)(2,1)S(1)}, u32[]{:S(2)}, u32[]{:S(2)}) %collective-permute-start.16) | collective-permute-done | bytes 262176 | tf_op jit(solution)/shard_map/ppermute | solution.py:536
  122.4 8.1 %collective-permute-start.10 = (bf16[8,2,64,128]{3,2,1,0:T(8,128)(2,1)}, bf16[8,2,64,128]{3,2,1,0:T(8,128)(2,1)}, u32[]{:S(2)}, u32[]{:S(2)}) collective-permute-start(bf16[8,2,64,128]{3,2,1,0:T(8,128)(2,1)} %get-tuple-element.65), channel_id=1, source_target_pairs={{0,1},{1,2},{2,3},{3,4},{4,5},{5,6},{6,7},{7,0},{8,9},{9,10},{10,1... | collective-permute-start | bytes 786440 | tf_op jit(solution)/shard_map/ppermute | solution.py:536
  130.5 1.1 gather_fusion
  131.6 9.5 %collective-permute-done.11.refs_1_ = bf16[8,2,64,128]{3,2,1,0:T(8,128)(2,1)} collective-permute-done((bf16[8,2,64,128]{3,2,1,0:T(8,128)(2,1)}, bf16[8,2,64,128]{3,2,1,0:T(8,128)(2,1)}, u32[]{:S(2)}, u32[]{:S(2)}) %collective-permute-start.11) | collective-permute-done | bytes 262176 | tf_op jit(solution)/shard_map/ppermute | solution.py:536
  141.2 4.4 %collective-permute-done.10.refs_0_ = bf16[8,2,64,128]{3,2,1,0:T(8,128)(2,1)} collective-permute-done((bf16[8,2,64,128]{3,2,1,0:T(8,128)(2,1)}, bf16[8,2,64,128]{3,2,1,0:T(8,128)(2,1)}, u32[]{:S(2)}, u32[]{:S(2)}) %collective-permute-start.10) | collective-permute-done | bytes 262176 | tf_op jit(solution)/shard_map/ppermute | solution.py:536
  145.6 1.3 copy-done.1
  146.9 7.6 %whiten.3 = (bf16[24,2,64,128]{3,2,1,0:T(8,128)(2,1)}, bf16[8,8,2,64,128]{4,3,2,1,0:T(8,128)(2,1)}) custom-call(s32[24]{0:T(128)} %get-tuple-element.56.source, s32[24]{0:T(128)} %get-tuple-element.55.length, s32[8,8]{1,0:T(8,128)} %gather_fusion, bf16[32,256,128]{2,1,0:T(8,128)(2,1)} %copy-done.1, bf16[32,144,128]{2,1,0:T(8,128)(2,1)} %get-tuple-element.44.more, ...), custom_call_target="tpu_custom_call" | custom-call | flops 629145600 | bytes 4194304 | tf_op jit(solution)/shard_map/whiten/pallas_call | solution.py:252
  154.5 3.8 %all-to-all-start.4 = ((bf16[8,8,2,64,128]{4,3,2,1,0:T(8,128)(2,1)}), bf16[8,8,2,64,128]{4,3,2,1,0:T(8,128)(2,1)S(1)}, u32[]{:S(2)}, u32[]{:S(2)}) async-start(bf16[8,8,2,64,128]{4,3,2,1,0:T(8,128)(2,1)} %get-tuple-element.46), calls=%async_computation.4 | async-start | bytes 4194304 | tf_op jit(solution)/shard_map/all_to_all | solution.py:540
  160.6 8.2 %cross_first.1.begun = f32[16384,128]{1,0:T(8,128)} custom-call(s32[8,8]{1,0:T(8,128)} %copy.50.near_pick, bf16[24,2,64,128]{3,2,1,0:T(8,128)(2,1)} %get-tuple-element.41.white, bf16[8,8,2,64,128]{4,3,2,1,0:T(8,128)(2,1)} %get-tuple-element.42.home, bf16[8,2,64,128]{3,2,1,0:T(8,128)(2,1)} %collective-permute-done.10.refs_0_, ...), custom_call_target="tpu_custom_call" | custom-call | flops 33554432 | bytes 25165824 | tf_op jit(solution)/shard_map/cross_first/pallas_call | solution.py:334
  168.8 17.9 %all-to-all-done.4.far_in = bf16[8,8,2,64,128]{4,3,2,1,0:T(8,128)(2,1)S(1)} async-done(((bf16[8,8,2,64,128]{4,3,2,1,0:T(8,128)(2,1)}), bf16[8,8,2,64,128]{4,3,2,1,0:T(8,128)(2,1)S(1)}, u32[]{:S(2)}, u32[]{:S(2)}) %all-to-all-start.4) | async-done | bytes 2097184 | tf_op jit(solution)/shard_map/all_to_all | solution.py:540
  186.7 1.4 copy-done
  188.0 15.4 %lagged.1 = f32[256,1024]{1,0:T(8,128)} custom-call(s32[8,8]{1,0:T(8,128)} %copy.50.near_pick, s32[8]{0:T(128)} %and_select_fusion.1.far_at, f32[16384,128]{1,0:T(8,128)} %cross_first.1.begun, bf16[24,2,64,128]{3,2,1,0:T(8,128)(2,1)} %get-tuple-element.45.white, bf16[8,8,2,64,128]{4,3,2,1,0:T(8,128)(2,1)} %copy-done, ...), custom_call_target="tpu_custom_call" | custom-call | flops 2147483648 | bytes 25165824 | tf_op jit(solution)/shard_map/lagged/pallas_call | solution.py:437
  203.4 2.5 %reshape.145 = f32[1,1,8,2,4,4,1024]{6,5,4,3,2,1,0:T(4,128)} reshape(f32[256,1024]{1,0:T(8,128)} %lagged.1) | data formatting | bytes 2097152 | tf_op jit(solution)/shard_map/reshape | solution.py:547
  (82 shorter events, 10.7 us)
Async XLA Ops:
  0.0 7.8 %copy-start.11 = (s32[1,72]{1,0:T(1,128)S(1)}, s32[1,72]{1,0:T(1,128)}, u32[]{:S(2)}) copy-start(s32[1,72]{1,0:T(1,128)} %param.15) | copy-start | bytes 868
  0.0 7.8 %copy-start.12 = (s32[1,72]{1,0:T(1,128)S(1)}, s32[1,72]{1,0:T(1,128)}, u32[]{:S(2)}) copy-start(s32[1,72]{1,0:T(1,128)} %param.14) | copy-start | bytes 868
  4.5 7.6 %collective-permute-start.1 = (bf16[72,128,128]{2,1,0:T(8,128)(2,1)S(1)}, bf16[72,128,128]{2,1,0:T(8,128)(2,1)}, u32[]{:S(2)}, u32[]{:S(2)}) collective-permute-start(bf16[72,128,128]{2,1,0:T(8,128)(2,1)S(1)} %bitcast.49), channel_id=1, source_target_pairs={{0,8},{8,0},{16,24},{24,16},{32,40},{40,32},{48,56},{56,48},{64,72... | collective-permute-start | bytes 7077896 | tf_op jit(solution)/shard_map/ppermute | solution.py:492
  7.8 4.0 %collective-permute-start = (s32[72]{0:T(128)S(1)}, s32[72]{0:T(128)S(1)}, u32[]{:S(2)}, u32[]{:S(2)}) collective-permute-start(s32[72]{0:T(128)S(1)} %bitcast.64), channel_id=1, source_target_pairs={{0,8},{8,0},{16,24},{24,16},{32,40},{40,32},{48,56},{56,48},{64,72... | collective-permute-start | bytes 872 | tf_op jit(solution)/shard_map/ppermute | solution.py:479
  19.1 60.3 %all-to-all-start.2 = ((bf16[32,272,128]{2,1,0:T(8,128)(2,1)}), bf16[32,272,128]{2,1,0:T(8,128)(2,1)}, u32[]{:S(2)}, u32[]{:S(2)}) async-start(bf16[32,272,128]{2,1,0:T(8,128)(2,1)} %get-tuple-element.36), calls=%async_computation.2 | async-start | bytes 4456448 | tf_op jit(solution)/shard_map/all_to_all | solution.py:489
  27.8 7.7 %copy-start.9 = (s32[1,1,8,2,4]{2,4,3,1,0:T(4,128)S(1)}, s32[1,1,8,2,4]{2,4,3,1,0:T(4,128)}, u32[]{:S(2)}) copy-start(s32[1,1,8,2,4]{2,4,3,1,0:T(4,128)} %param.17) | copy-start | bytes 772
  35.2 20.5 %collective-permute-start.2 = (bf16[72,128,128]{2,1,0:T(8,128)(2,1)}, bf16[72,128,128]{2,1,0:T(8,128)(2,1)}, u32[]{:S(2)}, u32[]{:S(2)}) collective-permute-start(bf16[72,128,128]{2,1,0:T(8,128)(2,1)} %bitcast.16.own), channel_id=1, source_target_pairs={{0,8},{8,0},{16,24},{24,16},{32,40},{40,32},{48,56},{56,48},{64,72... | collective-permute-start | bytes 7077896 | tf_op jit(solution)/shard_map/ppermute | solution.py:496
  36.6 9.1 %collective-permute-start.3 = (s32[8]{0:T(128)S(1)}, s32[8]{0:T(128)S(1)}, u32[]{:S(2)}, u32[]{:S(2)}) collective-permute-start(s32[8]{0:T(128)S(1)} %squeeze.32), channel_id=1, source_target_pairs={{0,7},{1,0},{2,1},{3,2},{4,3},{5,4},{6,5},{7,6},{8,15},{9,8},{10,9... | collective-permute-start | bytes 104 | tf_op jit(solution)/shard_map/ppermute | solution.py:501
  41.1 4.6 %collective-permute-start.4 = (s32[8]{0:T(128)S(1)}, s32[8]{0:T(128)S(1)}, u32[]{:S(2)}, u32[]{:S(2)}) collective-permute-start(s32[8]{0:T(128)S(1)} %squeeze.58), channel_id=1, source_target_pairs={{0,6},{1,7},{2,0},{3,1},{4,2},{5,3},{6,4},{7,5},{8,14},{9,15},{10,... | collective-permute-start | bytes 104 | tf_op jit(solution)/shard_map/ppermute | solution.py:501
  42.2 6.9 %collective-permute-start.5 = (s32[8]{0:T(128)S(1)}, s32[8]{0:T(128)S(1)}, u32[]{:S(2)}, u32[]{:S(2)}) collective-permute-start(s32[8]{0:T(128)S(1)} %squeeze.59), channel_id=1, source_target_pairs={{0,5},{1,6},{2,7},{3,0},{4,1},{5,2},{6,3},{7,4},{8,13},{9,14},{10,... | collective-permute-start | bytes 104 | tf_op jit(solution)/shard_map/ppermute | solution.py:501
  42.6 6.5 %collective-permute-start.6 = (s32[8]{0:T(128)S(1)}, s32[8]{0:T(128)S(1)}, u32[]{:S(2)}, u32[]{:S(2)}) collective-permute-start(s32[8]{0:T(128)S(1)} %squeeze.60), channel_id=1, source_target_pairs={{0,4},{1,5},{2,6},{3,7},{4,0},{5,1},{6,2},{7,3},{8,12},{9,13},{10,... | collective-permute-start | bytes 104 | tf_op jit(solution)/shard_map/ppermute | solution.py:501
  45.7 5.2 %collective-permute-start.7 = (s32[8]{0:T(128)S(1)}, s32[8]{0:T(128)S(1)}, u32[]{:S(2)}, u32[]{:S(2)}) collective-permute-start(s32[8]{0:T(128)S(1)} %squeeze.61), channel_id=1, source_target_pairs={{0,3},{1,4},{2,5},{3,6},{4,7},{5,0},{6,1},{7,2},{8,11},{9,12},{10,... | collective-permute-start | bytes 104 | tf_op jit(solution)/shard_map/ppermute | solution.py:501
  45.7 6.4 %collective-permute-start.8 = (s32[8]{0:T(128)S(1)}, s32[8]{0:T(128)S(1)}, u32[]{:S(2)}, u32[]{:S(2)}) collective-permute-start(s32[8]{0:T(128)S(1)} %squeeze.62), channel_id=1, source_target_pairs={{0,2},{1,3},{2,4},{3,5},{4,6},{5,7},{6,0},{7,1},{8,10},{9,11},{10,... | collective-permute-start | bytes 104 | tf_op jit(solution)/shard_map/ppermute | solution.py:501
  49.1 6.0 %collective-permute-start.9 = (s32[8]{0:T(128)S(1)}, s32[8]{0:T(128)S(1)}, u32[]{:S(2)}, u32[]{:S(2)}) collective-permute-start(s32[8]{0:T(128)S(1)} %squeeze.63), channel_id=1, source_target_pairs={{0,1},{1,2},{2,3},{3,4},{4,5},{5,6},{6,7},{7,0},{8,9},{9,10},{10,1... | collective-permute-start | bytes 104 | tf_op jit(solution)/shard_map/ppermute | solution.py:501
  82.0 63.6 %all-to-all-start.3 = ((bf16[32,256,128]{2,1,0:T(8,128)(2,1)}), bf16[32,256,128]{2,1,0:T(8,128)(2,1)S(1)}, u32[]{:S(2)}, u32[]{:S(2)}) async-start(bf16[32,256,128]{2,1,0:T(8,128)(2,1)} %get-tuple-element.43), calls=%async_computation.3 | async-start | bytes 4194304 | tf_op jit(solution)/shard_map/all_to_all | solution.py:489
  96.2 34.3 %copy-start.7 = (s32[8,8]{1,0:T(8,128)S(1)}, s32[8,8]{1,0:T(8,128)}, u32[]{:S(2)}) copy-start(s32[8,8]{1,0:T(8,128)} %stack.46.picks.after) | copy-start | bytes 772
  98.7 23.7 %collective-permute-start.16 = (bf16[8,2,64,128]{3,2,1,0:T(8,128)(2,1)S(1)}, bf16[8,2,64,128]{3,2,1,0:T(8,128)(2,1)S(1)}, u32[]{:S(2)}, u32[]{:S(2)}) collective-permute-start(bf16[8,2,64,128]{3,2,1,0:T(8,128)(2,1)S(1)} %get-tuple-element.59), channel_id=1, source_target_pairs={{0,7},{1,0},{2,1},{3,2},{4,3},{5,4},{6,5},{7,6},{8,15},{9,8},{10,9... | collective-permute-start | bytes 786440 | tf_op jit(solution)/shard_map/ppermute | solution.py:536
  103.1 19.2 %collective-permute-start.15 = (bf16[8,2,64,128]{3,2,1,0:T(8,128)(2,1)S(1)}, bf16[8,2,64,128]{3,2,1,0:T(8,128)(2,1)S(1)}, u32[]{:S(2)}, u32[]{:S(2)}) collective-permute-start(bf16[8,2,64,128]{3,2,1,0:T(8,128)(2,1)S(1)} %get-tuple-element.60), channel_id=1, source_target_pairs={{0,6},{1,7},{2,0},{3,1},{4,2},{5,3},{6,4},{7,5},{8,14},{9,15},{10,... | collective-permute-start | bytes 786440 | tf_op jit(solution)/shard_map/ppermute | solution.py:536
  104.2 27.4 %collective-permute-start.14 = (bf16[8,2,64,128]{3,2,1,0:T(8,128)(2,1)}, bf16[8,2,64,128]{3,2,1,0:T(8,128)(2,1)S(1)}, u32[]{:S(2)}, u32[]{:S(2)}) collective-permute-start(bf16[8,2,64,128]{3,2,1,0:T(8,128)(2,1)} %get-tuple-element.61), channel_id=1, source_target_pairs={{0,5},{1,6},{2,7},{3,0},{4,1},{5,2},{6,3},{7,4},{8,13},{9,14},{10,... | collective-permute-start | bytes 786440 | tf_op jit(solution)/shard_map/ppermute | solution.py:536
  104.6 27.0 %collective-permute-start.13 = (bf16[8,2,64,128]{3,2,1,0:T(8,128)(2,1)}, bf16[8,2,64,128]{3,2,1,0:T(8,128)(2,1)S(1)}, u32[]{:S(2)}, u32[]{:S(2)}) collective-permute-start(bf16[8,2,64,128]{3,2,1,0:T(8,128)(2,1)} %get-tuple-element.62), channel_id=1, source_target_pairs={{0,4},{1,5},{2,6},{3,7},{4,0},{5,1},{6,2},{7,3},{8,12},{9,13},{10,... | collective-permute-start | bytes 786440 | tf_op jit(solution)/shard_map/ppermute | solution.py:536
  107.7 23.9 %collective-permute-start.12 = (bf16[8,2,64,128]{3,2,1,0:T(8,128)(2,1)}, bf16[8,2,64,128]{3,2,1,0:T(8,128)(2,1)S(1)}, u32[]{:S(2)}, u32[]{:S(2)}) collective-permute-start(bf16[8,2,64,128]{3,2,1,0:T(8,128)(2,1)} %get-tuple-element.63), channel_id=1, source_target_pairs={{0,3},{1,4},{2,5},{3,6},{4,7},{5,0},{6,1},{7,2},{8,11},{9,12},{10,... | collective-permute-start | bytes 786440 | tf_op jit(solution)/shard_map/ppermute | solution.py:536
  122.4 23.2 %copy-start.2 = (bf16[8,2,64,128]{3,2,1,0:T(8,128)(2,1)}, bf16[8,2,64,128]{3,2,1,0:T(8,128)(2,1)S(1)}, u32[]{:S(2)}) copy-start(bf16[8,2,64,128]{3,2,1,0:T(8,128)(2,1)S(1)} %collective-permute-done.16.refs_6_) | copy-start | bytes 786436
  122.4 18.8 %collective-permute-start.11 = (bf16[8,2,64,128]{3,2,1,0:T(8,128)(2,1)}, bf16[8,2,64,128]{3,2,1,0:T(8,128)(2,1)}, u32[]{:S(2)}, u32[]{:S(2)}) collective-permute-start(bf16[8,2,64,128]{3,2,1,0:T(8,128)(2,1)} %get-tuple-element.64), channel_id=1, source_target_pairs={{0,2},{1,3},{2,4},{3,5},{4,6},{5,7},{6,0},{7,1},{8,10},{9,11},{10,... | collective-permute-start | bytes 786440 | tf_op jit(solution)/shard_map/ppermute | solution.py:536
  122.4 23.2 %copy-start.3 = (bf16[8,2,64,128]{3,2,1,0:T(8,128)(2,1)}, bf16[8,2,64,128]{3,2,1,0:T(8,128)(2,1)S(1)}, u32[]{:S(2)}) copy-start(bf16[8,2,64,128]{3,2,1,0:T(8,128)(2,1)S(1)} %collective-permute-done.15.refs_5_) | copy-start | bytes 786436
  122.4 23.2 %collective-permute-start.10 = (bf16[8,2,64,128]{3,2,1,0:T(8,128)(2,1)}, bf16[8,2,64,128]{3,2,1,0:T(8,128)(2,1)}, u32[]{:S(2)}, u32[]{:S(2)}) collective-permute-start(bf16[8,2,64,128]{3,2,1,0:T(8,128)(2,1)} %get-tuple-element.65), channel_id=1, source_target_pairs={{0,1},{1,2},{2,3},{3,4},{4,5},{5,6},{6,7},{7,0},{8,9},{9,10},{10,1... | collective-permute-start | bytes 786440 | tf_op jit(solution)/shard_map/ppermute | solution.py:536
  131.6 14.0 %copy-start.4 = (bf16[8,2,64,128]{3,2,1,0:T(8,128)(2,1)}, bf16[8,2,64,128]{3,2,1,0:T(8,128)(2,1)S(1)}, u32[]{:S(2)}) copy-start(bf16[8,2,64,128]{3,2,1,0:T(8,128)(2,1)S(1)} %collective-permute-done.14.refs_4_) | copy-start | bytes 786436
  131.6 14.0 %copy-start.5 = (bf16[8,2,64,128]{3,2,1,0:T(8,128)(2,1)}, bf16[8,2,64,128]{3,2,1,0:T(8,128)(2,1)S(1)}, u32[]{:S(2)}) copy-start(bf16[8,2,64,128]{3,2,1,0:T(8,128)(2,1)S(1)} %collective-permute-done.13.refs_3_) | copy-start | bytes 786436
  131.6 14.0 %copy-start.6 = (bf16[8,2,64,128]{3,2,1,0:T(8,128)(2,1)}, bf16[8,2,64,128]{3,2,1,0:T(8,128)(2,1)S(1)}, u32[]{:S(2)}) copy-start(bf16[8,2,64,128]{3,2,1,0:T(8,128)(2,1)S(1)} %collective-permute-done.12.refs_2_) | copy-start | bytes 786436
  154.5 3.9 %copy-start.10 = (s32[1,1,8,2,4]{2,4,3,1,0:T(4,128)S(1)}, s32[1,1,8,2,4]{2,4,3,1,0:T(4,128)}, u32[]{:S(2)}) copy-start(s32[1,1,8,2,4]{2,4,3,1,0:T(4,128)} %param.16) | copy-start | bytes 772
  154.5 4.5 %copy-start.8 = (s32[1,1,8,2,4,4]{2,5,4,3,1,0:T(4,128)S(1)}, s32[1,1,8,2,4,4]{2,5,4,3,1,0:T(4,128)}, u32[]{:S(2)}) copy-start(s32[1,1,8,2,4,4]{2,5,4,3,1,0:T(4,128)} %param.18) | copy-start | bytes 3076
  154.5 32.1 %all-to-all-start.4 = ((bf16[8,8,2,64,128]{4,3,2,1,0:T(8,128)(2,1)}), bf16[8,8,2,64,128]{4,3,2,1,0:T(8,128)(2,1)S(1)}, u32[]{:S(2)}, u32[]{:S(2)}) async-start(bf16[8,8,2,64,128]{4,3,2,1,0:T(8,128)(2,1)} %get-tuple-element.46), calls=%async_computation.4 | async-start | bytes 4194304 | tf_op jit(solution)/shard_map/all_to_all | solution.py:540
  186.7 1.4 copy-start
  (1 other events, 1.3 us)
